TPU v7x, 1024 devices: a whole 8x8x8 slice. The times are simulated.
1024 devices in a mesh: pipe: 8 (over z), seq: 32 (over y_hi, x), dp: 4 (over y_lo, core).
Axes of the slice: x: 8, y: 8 (y_hi: 4, y_lo: 2; y = y_hi * 2 + y_lo), z: 8, core: 2. Of those that a mesh axis runs over, the one named last changes fastest.
Arguments:
- inputs_saved: bfloat16 [8, 4, 2, 2048, 7168], P('pipe', 'dp', None, None, 'seq'), may hold values from -6 to 6
- grad_latent: bfloat16 [8, 4, 2, 2048, 384], P('pipe', 'dp', None, 'seq'), may hold values from -6 to 6
- weights: bfloat16 [8, 7168, 384], P('pipe', 'seq'), may hold values from -0.0625 to 0.0625
Outputs:
- input_grads: bfloat16 [8, 4, 2048, 7168], P('pipe', 'dp', None, 'seq')
- weight_grads: float32 [8, 7168, 384], P('pipe', 'seq', 'dp')
All inputs are finite; a program needn't handle non-finite values.
Results may differ from a plain program's by a relative error of at most 0.0039.
Values may be sent and summed in bfloat16 or wider, within the bound.
No kernel may reach another device: no remote copies, remote signals or barrier semaphores. Data moves between devices by JAX's collectives and lax.ppermute only.
A program may use at most 32 MiB of HBM per device.

v0:
```python
import jax
import jax.numpy as jnp
from jax import lax
from jax.sharding import PartitionSpec as P


def swapped(block, axis, stride):
    count = lax.axis_size(axis)
    route = []
    for low in range(count):
        high = low | 1 << stride
        if high != low and high < count:
            route += [(low, high), (high, low)]
    return lax.ppermute(block, axis, route)


def partner_part(values):
    bit_count = lax.axis_size("pipe").bit_length() - 1
    moved_part = values
    for bit_index in range(bit_count):
        moved_part = swapped(moved_part.astype(jnp.bfloat16), "pipe", bit_index).astype(
            moved_part.dtype
        )
    return moved_part


def local(inputs_saved, grad_latent, weights):
    saved_fwd = inputs_saved[0, 0, 0]
    saved_rev = inputs_saved[0, 0, 1]
    weight_rows = weights[0]
    token_total = saved_fwd.shape[0]
    contract_tokens = (((0,), (0,)), ((), ()))
    contract_latent = (((1,), (1,)), ((), ()))
    piece_fwd = lax.all_gather(grad_latent[0, 0, 0], "seq", axis=0, tiled=True)
    piece_rev = lax.all_gather(grad_latent[0, 0, 1], "seq", axis=0, tiled=True)
    grad_fwd = lax.dot_general(
        saved_fwd, piece_fwd, contract_tokens, preferred_element_type=jnp.float32
    )
    grad_rev = lax.dot_general(
        saved_rev, piece_rev, contract_tokens, preferred_element_type=jnp.float32
    )
    input_rows = lax.dot_general(
        piece_fwd, weight_rows, contract_latent, preferred_element_type=jnp.float32
    )
    input_grad = input_rows
    grad_fwd, grad_rev, input_grad = (grad_fwd, grad_rev, input_grad)
    share_fwd, share_rev = (
        lax.psum_scatter(grad_fwd, "dp", scatter_dimension=1, tiled=True),
        lax.psum_scatter(grad_rev, "dp", scatter_dimension=1, tiled=True),
    )
    reduced = share_fwd + partner_part(share_rev)
    weight_grad = (reduced * (1.0 / token_total))[None]
    return (input_grad.astype(jnp.bfloat16)[None, None], weight_grad)


def solution(mesh):
    in_specs = (
        P("pipe", "dp", None, None, "seq"),
        P("pipe", "dp", None, "seq", None),
        P("pipe", "seq", None),
    )
    out_specs = (P("pipe", "dp", None, "seq"), P("pipe", "seq", "dp"))
    return jax.shard_map(local, mesh=mesh, in_specs=in_specs, out_specs=out_specs, check_vma=False)
```

profile of v0, /device:TPU:1, one launch (start us, length us, event | category | flops | bytes accessed | tf_op | source)
XLA Modules:
  0.0 275.3 jit_solution(8325149643673231798)
XLA Ops:
  7.2 0.0 copy-start
  7.2 0.0 all-gather.7.cloned.1.call-start
  7.2 1.5 fusion.11
  8.7 0.0 all-gather.7.cloned.1.call-update
  8.7 0.0 all-gather.5.cloned.1.call-start
  8.8 0.7 all-gather.5.cloned.1.call-update
  9.5 0.0 reduce-scatter.5.cloned.1.call-start
  9.5 102.5 %all-gather.7.cloned.1.call-done = bf16[1,1,1,2048,384]{4,3,2,1,0:T(8,128)(2,1)} async-done(((bf16[1,1,1,64,384]{4,3,2,1,0:T(8,128)(2,1)}), bf16[1,1,1,2048,384]{4,3,2,1,0:T(8,128)(2,1)}) %all-gather.7.cloned.1.call-update) | async-done | bytes 1572880 | tf_op jit(solution)/shard_map/all_gather | solution.py:35
  112.0 3.2 %fusion.1 = f32[224,384]{0,1:T(8,128)} fusion(bf16[1,1,1,2048,384]{4,3,2,1,0:T(8,128)(2,1)} %all-gather.7.cloned.1.call-done, bf16[1,1,2,2048,224]{3,4,2,1,0:T(8,128)(2,1)} %param.3), kind=kOutput, calls=%fused_computation.2 | convolution fusion | flops 352321536 | bytes 2834432 | tf_op jit(solution)/shard_map/dot_general | solution.py:39
  115.2 0.0 reduce-scatter.5.cloned.1.call-update
  115.2 0.0 reduce-scatter.3.cloned.1.call-start
  115.2 89.5 %all-gather.5.cloned.1.call-done = bf16[1,1,1,2048,384]{4,3,2,1,0:T(8,128)(2,1)} async-done(((bf16[1,1,1,64,384]{4,3,2,1,0:T(8,128)(2,1)}), bf16[1,1,1,2048,384]{4,3,2,1,0:T(8,128)(2,1)}) %all-gather.5.cloned.1.call-update) | async-done | bytes 1572880 | tf_op jit(solution)/shard_map/all_gather | solution.py:34
  204.8 0.0 copy-start.1
  204.8 3.3 %fusion.3 = f32[224,384]{0,1:T(8,128)} fusion(bf16[1,1,1,2048,384]{4,3,2,1,0:T(8,128)(2,1)} %all-gather.5.cloned.1.call-done, bf16[1,1,2,2048,224]{3,4,2,1,0:T(8,128)(2,1)} %param.3), kind=kOutput, calls=%fused_computation.4 | convolution fusion | flops 352321536 | bytes 2834432 | tf_op jit(solution)/shard_map/dot_general | solution.py:36
  208.0 0.0 reduce-scatter.3.cloned.1.call-update
  208.1 28.8 %reduce-scatter.5.cloned.1.call-done = f32[224,96]{0,1:T(8,128)} async-done(((f32[224,384]{0,1:T(8,128)}), f32[224,96]{0,1:T(8,128)}) %reduce-scatter.5.cloned.1.call-update) | async-done | bytes 86032 | tf_op jit(solution)/shard_map/reduce_scatter | solution.py:49
  236.9 0.9 convert_element_type.14
  237.8 3.0 %collective-permute-start = (bf16[224,96]{0,1:T(8,128)(2,1)S(1)}, bf16[224,96]{0,1:T(8,128)(2,1)S(1)}, u32[]{:S(2)}, u32[]{:S(2)}) collective-permute-start(bf16[224,96]{0,1:T(8,128)(2,1)S(1)} %convert_element_type.14), channel_id=1, source_target_pairs={{0,128},{128,0},{256,384},{384,256},{512,640},{640,512},{768,896},... | collective-permute-start | bytes 129032 | tf_op jit(solution)/shard_map/ppermute | solution.py:14
  240.8 1.8 collective-permute-done
  242.6 4.7 %collective-permute-start.1 = (bf16[224,96]{0,1:T(8,128)(2,1)S(1)}, bf16[224,96]{0,1:T(8,128)(2,1)S(1)}, u32[]{:S(2)}, u32[]{:S(2)}) collective-permute-start(bf16[224,96]{0,1:T(8,128)(2,1)S(1)} %collective-permute-done), channel_id=1, source_target_pairs={{0,256},{256,0},{128,384},{384,128},{512,768},{768,512},{640,896},... | collective-permute-start | bytes 129032 | tf_op jit(solution)/shard_map/ppermute | solution.py:14
  247.3 1.5 collective-permute-done.1
  248.8 8.1 %collective-permute-start.2 = (bf16[224,96]{0,1:T(8,128)(2,1)S(1)}, bf16[224,96]{0,1:T(8,128)(2,1)S(1)}, u32[]{:S(2)}, u32[]{:S(2)}) collective-permute-start(bf16[224,96]{0,1:T(8,128)(2,1)S(1)} %collective-permute-done.1), channel_id=1, source_target_pairs={{0,512},{512,0},{128,640},{640,128},{256,768},{768,256},{384,896},... | collective-permute-start | bytes 129032 | tf_op jit(solution)/shard_map/ppermute | solution.py:14
  256.9 0.0 copy-done
  256.9 0.0 copy-done.1
  256.9 1.7 fusion
  258.6 8.7 %reduce-scatter.3.cloned.1.call-done = f32[224,96]{0,1:T(8,128)} async-done(((f32[224,384]{0,1:T(8,128)}), f32[224,96]{0,1:T(8,128)}) %reduce-scatter.3.cloned.1.call-update) | async-done | bytes 86032 | tf_op jit(solution)/shard_map/reduce_scatter | solution.py:48
  267.2 0.0 collective-permute-done.2
  267.2 1.5 multiply_bitcast_fusion
Async XLA Ops:
  7.2 249.7 %copy-start = (bf16[1,224,384]{2,1,0:T(8,128)(2,1)S(1)}, bf16[1,224,384]{2,1,0:T(8,128)(2,1)}, u32[]{:S(2)}) copy-start(bf16[1,224,384]{2,1,0:T(8,128)(2,1)} %param.5) | copy-start | bytes 516100
  7.2 104.8 %all-gather.7.cloned.1.call-start = ((), (), s32[]{:S(2)}) async-start(), calls=%async_computation.5 | async-start | bytes 1622016 | tf_op jit(solution)/shard_map/all_gather | solution.py:35
  8.7 196.0 %all-gather.5.cloned.1.call-start = ((), (), s32[]{:S(2)}) async-start(), calls=%async_computation.4 | async-start | bytes 1622016 | tf_op jit(solution)/shard_map/all_gather | solution.py:34
  9.5 227.4 %reduce-scatter.5.cloned.1.call-start = ((), (), s32[]{:S(2)}) async-start(), calls=%async_computation.3 | async-start | bytes 491520 | tf_op jit(solution)/shard_map/reduce_scatter | solution.py:49
  115.2 152.0 %reduce-scatter.3.cloned.1.call-start = ((), (), s32[]{:S(2)}) async-start(), calls=%async_computation.2 | async-start | bytes 491520 | tf_op jit(solution)/shard_map/reduce_scatter | solution.py:48
  204.8 52.1 %copy-start.1 = (bf16[1,1,1,2048,384]{4,3,2,1,0:T(8,128)(2,1)S(1)}, bf16[1,1,1,2048,384]{4,3,2,1,0:T(8,128)(2,1)}, u32[]{:S(2)}) copy-start(bf16[1,1,1,2048,384]{4,3,2,1,0:T(8,128)(2,1)} %all-gather.5.cloned.1.call-done) | copy-start | bytes 4718596
  237.8 4.8 %collective-permute-start = (bf16[224,96]{0,1:T(8,128)(2,1)S(1)}, bf16[224,96]{0,1:T(8,128)(2,1)S(1)}, u32[]{:S(2)}, u32[]{:S(2)}) collective-permute-start(bf16[224,96]{0,1:T(8,128)(2,1)S(1)} %convert_element_type.14), channel_id=1, source_target_pairs={{0,128},{128,0},{256,384},{384,256},{512,640},{640,512},{768,896},... | collective-permute-start | bytes 129032 | tf_op jit(solution)/shard_map/ppermute | solution.py:14
  242.6 6.2 %collective-permute-start.1 = (bf16[224,96]{0,1:T(8,128)(2,1)S(1)}, bf16[224,96]{0,1:T(8,128)(2,1)S(1)}, u32[]{:S(2)}, u32[]{:S(2)}) collective-permute-start(bf16[224,96]{0,1:T(8,128)(2,1)S(1)} %collective-permute-done), channel_id=1, source_target_pairs={{0,256},{256,0},{128,384},{384,128},{512,768},{768,512},{640,896},... | collective-permute-start | bytes 129032 | tf_op jit(solution)/shard_map/ppermute | solution.py:14
  248.8 18.4 %collective-permute-start.2 = (bf16[224,96]{0,1:T(8,128)(2,1)S(1)}, bf16[224,96]{0,1:T(8,128)(2,1)S(1)}, u32[]{:S(2)}, u32[]{:S(2)}) collective-permute-start(bf16[224,96]{0,1:T(8,128)(2,1)S(1)} %collective-permute-done.1), channel_id=1, source_target_pairs={{0,512},{512,0},{128,640},{640,128},{256,768},{768,256},{384,896},... | collective-permute-start | bytes 129032 | tf_op jit(solution)/shard_map/ppermute | solution.py:14
Sparse Core Ops, SparseCore 0:
  12.9 99.0 all-gather.6
  116.3 88.3 all-gather.4
  208.7 28.0 reduce-scatter.4
  240.5 26.6 reduce-scatter.2
where the time goes:
time: 276 us; the launch traced here: 275 us
  waiting for transfers between devices  233 us (84%)
  starting transfers between devices  15.9 us (6%)
  between operations  13.8 us (5%)
  matrix products  8.1 us (3%)
    all_gather x1, waiting for transfers between devices, local(): piece_rev = lax.all_gather(grad_latent[0, 0, 1], 'seq', axis=0, tiled=True)  102 us
    all_gather x1, waiting for transfers between devices, local(): piece_fwd = lax.all_gather(grad_latent[0, 0, 0], 'seq', axis=0, tiled=True)  89.5 us
    reduce_scatter x1, waiting for transfers between devices, local(): lax.psum_scatter(grad_rev, 'dp', scatter_dimension=1, tiled=True)  28.8 us
    ppermute x3, starting transfers between devices, swapped(): return lax.ppermute(block, axis, route)  15.8 us
    reduce_scatter x1, waiting for transfers between devices, local(): lax.psum_scatter(grad_fwd, 'dp', scatter_dimension=1, tiled=True)  8.65 us
  transfers between devices with their start and end apart: 7, of which 6 were waited for; matrix products, arithmetic and copies ran while one was open for 3% of the time, Pallas kernels for 0%

commit v1 on v0

v1 whole, which is shorter than its diff:
```python
import jax
import jax.numpy as jnp
from jax import lax
from jax.sharding import PartitionSpec as P

X_CHIPS = 8


def local(inputs_saved, grad_latent, weights):
    seq = lax.axis_size("seq")
    pipe = lax.axis_size("pipe")
    dp = lax.axis_size("dp")
    nx = X_CHIPS
    ny = seq // nx
    rows = [[y * nx + x for x in range(nx)] for y in range(ny)]
    columns = [[y * nx + x for y in range(ny)] for x in range(nx)]

    def along_x(step):
        return [(y * nx + x, y * nx + (x + step) % nx) for y in range(ny) for x in range(nx)]

    right, left = along_x(1), along_x(-1)
    tokens = inputs_saved.shape[3]
    width = inputs_saved.shape[4]
    channels = grad_latent.shape[-1]
    piece = grad_latent.shape[3]

    both = lax.all_gather(grad_latent[0, 0][:, None], "seq", axis=1, tiled=True, axis_index_groups=columns)
    rev = lax.all_gather(both[1][:, None], "seq", axis=1, tiled=True, axis_index_groups=rows)
    rev = rev.reshape(tokens, channels)

    own = both[0]
    half = ny // 2
    from_left, from_right = [own], [own]
    for _ in range(nx // 2 - 1):
        from_left.append(lax.ppermute(from_left[-1], "seq", right))
        from_right.append(lax.ppermute(from_right[-1], "seq", left))
    far = jnp.concatenate(
        [
            lax.ppermute(from_left[-1][:half], "seq", right),
            lax.ppermute(from_right[-1][half:], "seq", left),
        ]
    )
    x_here = lax.rem(lax.axis_index("seq"), nx)
    relative = from_right + [far] + from_left[:0:-1]
    fwd = jnp.zeros((ny, nx, piece, channels), own.dtype)
    for k, block in enumerate(relative):
        fwd = lax.dynamic_update_slice(fwd, block[:, None], (0, lax.rem(x_here + k, nx), 0, 0))
    fwd = fwd.reshape(tokens, channels)

    over_tokens = (((0,), (0,)), ((), ()))

    def dp_sum(latent, saved):
        partial = lax.dot_general(latent, saved, over_tokens, preferred_element_type=jnp.float32)
        shares = partial.astype(jnp.bfloat16).reshape(dp, channels // dp, width)
        shares = lax.all_to_all(shares, "dp", 0, 0, tiled=True)
        return jnp.sum(shares.astype(jnp.float32), axis=0)

    sum_rev = dp_sum(rev, inputs_saved[0, 0, 1])
    mirrored = lax.ppermute(sum_rev.astype(jnp.bfloat16), "pipe", [(i, pipe - 1 - i) for i in range(pipe)])
    sum_fwd = dp_sum(fwd, inputs_saved[0, 0, 0])
    input_grad = lax.dot_general(
        fwd, weights[0], (((1,), (1,)), ((), ())), preferred_element_type=jnp.float32
    ).astype(jnp.bfloat16)
    weight_grad = (sum_fwd + mirrored.astype(jnp.float32)) * (1.0 / tokens)
    return input_grad[None, None], weight_grad.T[None]


def solution(mesh):
    in_specs = (
        P("pipe", "dp", None, None, "seq"),
        P("pipe", "dp", None, "seq", None),
        P("pipe", "seq", None),
    )
    out_specs = (P("pipe", "dp", None, "seq"), P("pipe", "seq", "dp"))
    return jax.shard_map(local, mesh=mesh, in_specs=in_specs, out_specs=out_specs, check_vma=False)
```

time: 276 us -> 122 us (0.44)
  waiting for transfers between devices: 233 us -> 32 us
  starting transfers between devices: 15.9 us -> 49.1 us
  blocking collectives: 0 us -> 16.7 us
    all_gather x2 -> x1, waiting for transfers between devices: 192 us -> 16.2 us  [local(): lax.all_gather(both[1][:, None], 'seq', axis=1, tiled=True, axis_index_gr...]
    reduce_scatter x2 -> x0, waiting for transfers between devices: 37.5 us -> none  [the longest x1 28.8 us: local(): lax.psum_scatter(grad_rev, 'dp', scatter_dimension=1, tiled=True)]
    ppermute x3 -> x9, starting transfers between devices: 15.8 us -> 37 us  [the longest x3 14.3 us: local(): from_right.append(lax.ppermute(from_right[-1], 'seq', left))]
    all_gather x0 -> x1, blocking collectives: none -> 16.7 us  [local(): lax.all_gather(grad_latent[0, 0][:, None], 'seq', axis=1, tiled=True, axi...]
    all_to_all x0 -> x2, starting transfers between devices: none -> 12.1 us  [dp_sum(): shares = lax.all_to_all(shares, 'dp', 0, 0, tiled=True)]
    ppermute x3 -> x9, waiting for transfers between devices: 3.29 us -> 13.9 us  [the longest x3 5.68 us: local(): from_left.append(lax.ppermute(from_left[-1], 'seq', right))]
  transfers between devices with their start and end apart: 7 -> 12, of which waited for: 6 -> 8; matrix products, arithmetic and copies ran while one was open for 3% -> 4% of each run, Pallas kernels for 0% -> 0%
where the time goes in v1:
time: 122 us
  starting transfers between devices  49.1 us (40%)
  waiting for transfers between devices  32 us (26%)
  blocking collectives  16.7 us (14%)
  between operations  14.3 us (12%)
  matrix products  5.8 us (5%)
  local copies, waits for them, and re-layouts  2.89 us (2%)
    all_gather x1, blocking collectives, local(): lax.all_gather(grad_latent[0, 0][:, None], 'seq', axis=1, tiled=True, axi...  16.7 us
    all_gather x1, waiting for transfers between devices, local(): lax.all_gather(both[1][:, None], 'seq', axis=1, tiled=True, axis_index_gr...  16.2 us
    ppermute x3, starting transfers between devices, local(): from_right.append(lax.ppermute(from_right[-1], 'seq', left))  14.3 us
    all_to_all x2, starting transfers between devices, dp_sum(): shares = lax.all_to_all(shares, 'dp', 0, 0, tiled=True)  12.1 us
    ppermute x1, starting transfers between devices, local(): lax.ppermute(sum_rev.astype(jnp.bfloat16), 'pipe', [(i, pipe - 1 - i) for...  10.4 us
    ppermute x3, starting transfers between devices, local(): from_left.append(lax.ppermute(from_left[-1], 'seq', right))  5.75 us
    ppermute x3, waiting for transfers between devices, local(): from_left.append(lax.ppermute(from_left[-1], 'seq', right))  5.68 us
    ppermute x1, starting transfers between devices, local(): lax.ppermute(from_right[-1][half:], 'seq', left)  4.57 us
  transfers between devices with their start and end apart: 12, of which 8 were waited for; matrix products, arithmetic and copies ran while one was open for 4% of the time, Pallas kernels for 0%

profile of v1, /device:TPU:1, one launch (start us, length us, event | category | flops | bytes accessed | tf_op | source)
XLA Modules:
  0.0 121.6 jit_solution(7247553161297873826)
XLA Ops:
  7.2 0.0 copy-start
  7.2 0.0 all-gather.4.cloned.1.call-start
  7.2 16.7 %all-gather = bf16[1,1,2,256,384]{4,3,2,1,0:T(8,128)(2,1)S(1)} all-gather(bf16[1,1,2,64,384]{4,3,2,1,0:T(8,128)(2,1)} %param.4), channel_id=2, replica_groups={{0,32,64,96},{4,36,68,100},{8,40,72,104},{12,44,76,108},{16,48,80,112},..., dimensions={3}, use_global_device_ids=true | all-gather | bytes 491520 | tf_op jit(solution)/shard_map/all_gather | solution.py:27
  23.9 0.7 fusion.7
  24.6 0.0 all-gather.4.cloned.1.call-update
  24.7 4.3 %collective-permute-start = (bf16[4,64,384]{2,1,0:T(8,128)(2,1)S(1)}, bf16[4,64,384]{2,1,0:T(8,128)(2,1)S(1)}, u32[]{:S(2)}, u32[]{:S(2)}) collective-permute-start(bf16[4,64,384]{2,1,0:T(8,128)(2,1)S(1)} %bitcast.56), channel_id=1, source_target_pairs={{0,28},{4,0},{8,4},{12,8},{16,12},{20,16},{24,20},{28,24},{32,60},... | collective-permute-start | bytes 589832 | tf_op jit(solution)/shard_map/ppermute | solution.py:36
  29.0 1.9 %collective-permute-start.3 = (bf16[4,64,384]{2,1,0:T(8,128)(2,1)S(1)}, bf16[4,64,384]{2,1,0:T(8,128)(2,1)S(1)}, u32[]{:S(2)}, u32[]{:S(2)}) collective-permute-start(bf16[4,64,384]{2,1,0:T(8,128)(2,1)S(1)} %bitcast.57), channel_id=1, source_target_pairs={{0,4},{4,8},{8,12},{12,16},{16,20},{20,24},{24,28},{28,0},{32,36},... | collective-permute-start | bytes 589832 | tf_op jit(solution)/shard_map/ppermute | solution.py:35
  31.0 0.2 broadcast_in_dim.30
  31.3 0.3 collective-permute-done
  31.6 5.0 %collective-permute-start.1 = (bf16[4,64,384]{2,1,0:T(8,128)(2,1)S(1)}, bf16[4,64,384]{2,1,0:T(8,128)(2,1)S(1)}, u32[]{:S(2)}, u32[]{:S(2)}) collective-permute-start(bf16[4,64,384]{2,1,0:T(8,128)(2,1)S(1)} %collective-permute-done), channel_id=1, source_target_pairs={{0,28},{4,0},{8,4},{12,8},{16,12},{20,16},{24,20},{28,24},{32,60},... | collective-permute-start | bytes 589832 | tf_op jit(solution)/shard_map/ppermute | solution.py:36
  36.6 0.0 collective-permute-done.3
  36.6 1.9 %collective-permute-start.4 = (bf16[4,64,384]{2,1,0:T(8,128)(2,1)S(1)}, bf16[4,64,384]{2,1,0:T(8,128)(2,1)S(1)}, u32[]{:S(2)}, u32[]{:S(2)}) collective-permute-start(bf16[4,64,384]{2,1,0:T(8,128)(2,1)S(1)} %collective-permute-done.3), channel_id=1, source_target_pairs={{0,4},{4,8},{8,12},{12,16},{16,20},{20,24},{24,28},{28,0},{32,36},... | collective-permute-start | bytes 589832 | tf_op jit(solution)/shard_map/ppermute | solution.py:35
  38.6 0.6 collective-permute-done.1
  39.2 5.0 %collective-permute-start.2 = (bf16[4,64,384]{2,1,0:T(8,128)(2,1)S(1)}, bf16[4,64,384]{2,1,0:T(8,128)(2,1)S(1)}, u32[]{:S(2)}, u32[]{:S(2)}) collective-permute-start(bf16[4,64,384]{2,1,0:T(8,128)(2,1)S(1)} %collective-permute-done.1), channel_id=1, source_target_pairs={{0,28},{4,0},{8,4},{12,8},{16,12},{20,16},{24,20},{28,24},{32,60},... | collective-permute-start | bytes 589832 | tf_op jit(solution)/shard_map/ppermute | solution.py:36
  44.2 0.0 collective-permute-done.4
  44.2 1.9 %collective-permute-start.5 = (bf16[4,64,384]{2,1,0:T(8,128)(2,1)S(1)}, bf16[4,64,384]{2,1,0:T(8,128)(2,1)S(1)}, u32[]{:S(2)}, u32[]{:S(2)}) collective-permute-start(bf16[4,64,384]{2,1,0:T(8,128)(2,1)S(1)} %collective-permute-done.4), channel_id=1, source_target_pairs={{0,4},{4,8},{8,12},{12,16},{16,20},{20,24},{24,28},{28,0},{32,36},... | collective-permute-start | bytes 589832 | tf_op jit(solution)/shard_map/ppermute | solution.py:35
  46.2 5.7 %collective-permute-done.5 = bf16[4,64,384]{2,1,0:T(8,128)(2,1)S(1)} collective-permute-done((bf16[4,64,384]{2,1,0:T(8,128)(2,1)S(1)}, bf16[4,64,384]{2,1,0:T(8,128)(2,1)S(1)}, u32[]{:S(2)}, u32[]{:S(2)}) %collective-permute-start.5) | collective-permute-done | bytes 196640 | tf_op jit(solution)/shard_map/ppermute | solution.py:35
  51.8 1.9 %collective-permute-start.6 = (bf16[2,64,384]{2,1,0:T(8,128)(2,1)S(1)}, bf16[2,64,384]{2,1,0:T(8,128)(2,1)S(1)}, u32[]{:S(2)}, u32[]{:S(2)}) collective-permute-start(bf16[2,64,384]{2,1,0:T(8,128)(2,1)S(1)} %slice.27), channel_id=1, source_target_pairs={{0,4},{4,8},{8,12},{12,16},{16,20},{20,24},{24,28},{28,0},{32,36},... | collective-permute-start | bytes 294920 | tf_op jit(solution)/shard_map/ppermute | solution.py:39
  53.8 0.0 collective-permute-done.2
  53.8 4.6 %collective-permute-start.7 = (bf16[2,64,384]{2,1,0:T(8,128)(2,1)S(1)}, bf16[2,64,384]{2,1,0:T(8,128)(2,1)S(1)}, u32[]{:S(2)}, u32[]{:S(2)}) collective-permute-start(bf16[2,64,384]{2,1,0:T(8,128)(2,1)S(1)} %slice.28), channel_id=1, source_target_pairs={{0,28},{4,0},{8,4},{12,8},{16,12},{20,16},{24,20},{28,24},{32,60},... | collective-permute-start | bytes 294920 | tf_op jit(solution)/shard_map/ppermute | solution.py:40
  58.4 1.7 %collective-permute-done.6 = bf16[2,64,384]{2,1,0:T(8,128)(2,1)S(1)} collective-permute-done((bf16[2,64,384]{2,1,0:T(8,128)(2,1)S(1)}, bf16[2,64,384]{2,1,0:T(8,128)(2,1)S(1)}, u32[]{:S(2)}, u32[]{:S(2)}) %collective-permute-start.6) | collective-permute-done | bytes 98336 | tf_op jit(solution)/shard_map/ppermute | solution.py:39
  60.1 2.6 %collective-permute-done.7 = bf16[2,64,384]{2,1,0:T(8,128)(2,1)S(1)} collective-permute-done((bf16[2,64,384]{2,1,0:T(8,128)(2,1)S(1)}, bf16[2,64,384]{2,1,0:T(8,128)(2,1)S(1)}, u32[]{:S(2)}, u32[]{:S(2)}) %collective-permute-start.7) | collective-permute-done | bytes 98336 | tf_op jit(solution)/shard_map/ppermute | solution.py:40
  62.9 16.2 %all-gather.4.cloned.1.call-done = bf16[1,4,512,384]{3,2,1,0:T(8,128)(2,1)} async-done(((bf16[1,4,64,384]{3,2,1,0:T(8,128)(2,1)}), bf16[1,4,512,384]{3,2,1,0:T(8,128)(2,1)}) %all-gather.4.cloned.1.call-update) | async-done | bytes 1572880 | tf_op jit(solution)/shard_map/all_gather | solution.py:28
  79.2 2.3 %convolution_convert_fusion.1 = bf16[384,224]{0,1:T(8,128)(2,1)S(1)} fusion(bf16[2048,384]{1,0:T(8,128)(2,1)} %bitcast.59, bf16[1,1,2,2048,224]{3,4,2,1,0:T(8,128)(2,1)} %param.3), kind=kOutput, calls=%fused_computation.2 | convolution fusion | flops 352407552 | bytes 2662400 | tf_op jit(solution)/shard_map/dot_general | solution.py:53
  81.5 0.8 copy.12
  82.3 7.9 %all-to-all-start.1 = ((bf16[4,96,224]{2,1,0:T(8,128)(2,1)}), bf16[4,96,224]{2,1,0:T(8,128)(2,1)S(1)}, u32[]{:S(2)}, u32[]{:S(2)}) async-start(bf16[4,96,224]{2,1,0:T(8,128)(2,1)} %bitcast.23), calls=%async_computation.1 | async-start | bytes 393216 | tf_op jit(solution)/shard_map/all_to_all | solution.py:55
  90.2 1.8 %convolution_convert_fusion.2 = bf16[384,224]{0,1:T(8,128)(2,1)S(1)} fusion(bf16[2048,384]{1,0:T(8,128)(2,1)S(1)} %bitcast.53, bf16[1,1,2,2048,224]{3,4,2,1,0:T(8,128)(2,1)} %param.3), kind=kOutput, calls=%fused_computation.3 | convolution fusion | flops 352407552 | bytes 2662400 | tf_op jit(solution)/shard_map/dot_general | solution.py:53
  92.0 0.8 copy.11
  92.9 1.8 %all-to-all-done.1 = bf16[4,96,224]{2,1,0:T(8,128)(2,1)S(1)} async-done(((bf16[4,96,224]{2,1,0:T(8,128)(2,1)}), bf16[4,96,224]{2,1,0:T(8,128)(2,1)S(1)}, u32[]{:S(2)}, u32[]{:S(2)}) %all-to-all-start.1) | async-done | bytes 172064 | tf_op jit(solution)/shard_map/all_to_all | solution.py:55
  94.7 4.2 %all-to-all-start = ((bf16[4,96,224]{2,1,0:T(8,128)(2,1)}), bf16[4,96,224]{2,1,0:T(8,128)(2,1)S(1)}, u32[]{:S(2)}, u32[]{:S(2)}) async-start(bf16[4,96,224]{2,1,0:T(8,128)(2,1)} %bitcast.19), calls=%async_computation | async-start | bytes 393216 | tf_op jit(solution)/shard_map/all_to_all | solution.py:55
  98.9 0.0 copy-done
  98.9 1.7 %fusion = bf16[1,1,2048,224]{2,3,1,0:T(8,128)(2,1)} fusion(bf16[2048,384]{1,0:T(8,128)(2,1)S(1)} %bitcast.54, bf16[1,224,384]{2,1,0:T(8,128)(2,1)S(1)} %copy-done), kind=kOutput, calls=%fused_computation.1 | convolution fusion | flops 352780288 | bytes 2662400 | tf_op jit(solution)/shard_map/dot_general | solution.py:61
  100.6 10.4 %collective-permute-start.8 = (bf16[96,224]{1,0:T(8,128)(2,1)S(1)}, bf16[96,224]{1,0:T(8,128)(2,1)S(1)}, u32[]{:S(2)}, u32[]{:S(2)}) collective-permute-start(bf16[96,224]{1,0:T(8,128)(2,1)S(1)} %reduce_sum.22), channel_id=1, source_target_pairs={{0,896},{128,768},{256,640},{384,512},{512,384},{640,256},{768,128... | collective-permute-start | bytes 129032 | tf_op jit(solution)/shard_map/ppermute | solution.py:59
  111.0 0.0 all-to-all-done
  111.0 3.1 %collective-permute-done.8 = bf16[96,224]{1,0:T(8,128)(2,1)S(1)} collective-permute-done((bf16[96,224]{1,0:T(8,128)(2,1)S(1)}, bf16[96,224]{1,0:T(8,128)(2,1)S(1)}, u32[]{:S(2)}, u32[]{:S(2)}) %collective-permute-start.8) | collective-permute-done | bytes 43040 | tf_op jit(solution)/shard_map/ppermute | solution.py:59
  114.1 0.7 multiply_bitcast_fusion
  (12 shorter events, 0.4 us)
Async XLA Ops:
  7.2 91.7 %copy-start = (bf16[1,224,384]{2,1,0:T(8,128)(2,1)S(1)}, bf16[1,224,384]{2,1,0:T(8,128)(2,1)}, u32[]{:S(2)}) copy-start(bf16[1,224,384]{2,1,0:T(8,128)(2,1)} %param.5) | copy-start | bytes 516100
  7.2 72.0 %all-gather.4.cloned.1.call-start = ((), (), s32[]{:S(2)}) async-start(), calls=%async_computation.2 | async-start | bytes 1769472 | tf_op jit(solution)/shard_map/all_gather | solution.py:28
  24.7 6.9 %collective-permute-start = (bf16[4,64,384]{2,1,0:T(8,128)(2,1)S(1)}, bf16[4,64,384]{2,1,0:T(8,128)(2,1)S(1)}, u32[]{:S(2)}, u32[]{:S(2)}) collective-permute-start(bf16[4,64,384]{2,1,0:T(8,128)(2,1)S(1)} %bitcast.56), channel_id=1, source_target_pairs={{0,28},{4,0},{8,4},{12,8},{16,12},{20,16},{24,20},{28,24},{32,60},... | collective-permute-start | bytes 589832 | tf_op jit(solution)/shard_map/ppermute | solution.py:36
  29.0 7.6 %collective-permute-start.3 = (bf16[4,64,384]{2,1,0:T(8,128)(2,1)S(1)}, bf16[4,64,384]{2,1,0:T(8,128)(2,1)S(1)}, u32[]{:S(2)}, u32[]{:S(2)}) collective-permute-start(bf16[4,64,384]{2,1,0:T(8,128)(2,1)S(1)} %bitcast.57), channel_id=1, source_target_pairs={{0,4},{4,8},{8,12},{12,16},{16,20},{20,24},{24,28},{28,0},{32,36},... | collective-permute-start | bytes 589832 | tf_op jit(solution)/shard_map/ppermute | solution.py:35
  31.6 7.6 %collective-permute-start.1 = (bf16[4,64,384]{2,1,0:T(8,128)(2,1)S(1)}, bf16[4,64,384]{2,1,0:T(8,128)(2,1)S(1)}, u32[]{:S(2)}, u32[]{:S(2)}) collective-permute-start(bf16[4,64,384]{2,1,0:T(8,128)(2,1)S(1)} %collective-permute-done), channel_id=1, source_target_pairs={{0,28},{4,0},{8,4},{12,8},{16,12},{20,16},{24,20},{28,24},{32,60},... | collective-permute-start | bytes 589832 | tf_op jit(solution)/shard_map/ppermute | solution.py:36
  36.6 7.6 %collective-permute-start.4 = (bf16[4,64,384]{2,1,0:T(8,128)(2,1)S(1)}, bf16[4,64,384]{2,1,0:T(8,128)(2,1)S(1)}, u32[]{:S(2)}, u32[]{:S(2)}) collective-permute-start(bf16[4,64,384]{2,1,0:T(8,128)(2,1)S(1)} %collective-permute-done.3), channel_id=1, source_target_pairs={{0,4},{4,8},{8,12},{12,16},{16,20},{20,24},{24,28},{28,0},{32,36},... | collective-permute-start | bytes 589832 | tf_op jit(solution)/shard_map/ppermute | solution.py:35
  39.2 14.6 %collective-permute-start.2 = (bf16[4,64,384]{2,1,0:T(8,128)(2,1)S(1)}, bf16[4,64,384]{2,1,0:T(8,128)(2,1)S(1)}, u32[]{:S(2)}, u32[]{:S(2)}) collective-permute-start(bf16[4,64,384]{2,1,0:T(8,128)(2,1)S(1)} %collective-permute-done.1), channel_id=1, source_target_pairs={{0,28},{4,0},{8,4},{12,8},{16,12},{20,16},{24,20},{28,24},{32,60},... | collective-permute-start | bytes 589832 | tf_op jit(solution)/shard_map/ppermute | solution.py:36
  44.2 7.6 %collective-permute-start.5 = (bf16[4,64,384]{2,1,0:T(8,128)(2,1)S(1)}, bf16[4,64,384]{2,1,0:T(8,128)(2,1)S(1)}, u32[]{:S(2)}, u32[]{:S(2)}) collective-permute-start(bf16[4,64,384]{2,1,0:T(8,128)(2,1)S(1)} %collective-permute-done.4), channel_id=1, source_target_pairs={{0,4},{4,8},{8,12},{12,16},{16,20},{20,24},{24,28},{28,0},{32,36},... | collective-permute-start | bytes 589832 | tf_op jit(solution)/shard_map/ppermute | solution.py:35
  51.8 8.3 %collective-permute-start.6 = (bf16[2,64,384]{2,1,0:T(8,128)(2,1)S(1)}, bf16[2,64,384]{2,1,0:T(8,128)(2,1)S(1)}, u32[]{:S(2)}, u32[]{:S(2)}) collective-permute-start(bf16[2,64,384]{2,1,0:T(8,128)(2,1)S(1)} %slice.27), channel_id=1, source_target_pairs={{0,4},{4,8},{8,12},{12,16},{16,20},{20,24},{24,28},{28,0},{32,36},... | collective-permute-start | bytes 294920 | tf_op jit(solution)/shard_map/ppermute | solution.py:39
  53.8 8.9 %collective-permute-start.7 = (bf16[2,64,384]{2,1,0:T(8,128)(2,1)S(1)}, bf16[2,64,384]{2,1,0:T(8,128)(2,1)S(1)}, u32[]{:S(2)}, u32[]{:S(2)}) collective-permute-start(bf16[2,64,384]{2,1,0:T(8,128)(2,1)S(1)} %slice.28), channel_id=1, source_target_pairs={{0,28},{4,0},{8,4},{12,8},{16,12},{20,16},{24,20},{28,24},{32,60},... | collective-permute-start | bytes 294920 | tf_op jit(solution)/shard_map/ppermute | solution.py:40
  82.3 12.4 %all-to-all-start.1 = ((bf16[4,96,224]{2,1,0:T(8,128)(2,1)}), bf16[4,96,224]{2,1,0:T(8,128)(2,1)S(1)}, u32[]{:S(2)}, u32[]{:S(2)}) async-start(bf16[4,96,224]{2,1,0:T(8,128)(2,1)} %bitcast.23), calls=%async_computation.1 | async-start | bytes 393216 | tf_op jit(solution)/shard_map/all_to_all | solution.py:55
  94.7 16.3 %all-to-all-start = ((bf16[4,96,224]{2,1,0:T(8,128)(2,1)}), bf16[4,96,224]{2,1,0:T(8,128)(2,1)S(1)}, u32[]{:S(2)}, u32[]{:S(2)}) async-start(bf16[4,96,224]{2,1,0:T(8,128)(2,1)} %bitcast.19), calls=%async_computation | async-start | bytes 393216 | tf_op jit(solution)/shard_map/all_to_all | solution.py:55
  100.6 13.5 %collective-permute-start.8 = (bf16[96,224]{1,0:T(8,128)(2,1)S(1)}, bf16[96,224]{1,0:T(8,128)(2,1)S(1)}, u32[]{:S(2)}, u32[]{:S(2)}) collective-permute-start(bf16[96,224]{1,0:T(8,128)(2,1)S(1)} %reduce_sum.22), channel_id=1, source_target_pairs={{0,896},{128,768},{256,640},{384,512},{512,384},{640,256},{768,128... | collective-permute-start | bytes 129032 | tf_op jit(solution)/shard_map/ppermute | solution.py:59
Sparse Core Ops, SparseCore 0:
  24.8 54.3 all-gather.3

commit v2 on v1

v2 whole, which is shorter than its diff:
```python
import jax
import jax.numpy as jnp
from jax import lax
from jax.experimental import pallas as pl
from jax.experimental.pallas import tpu as pltpu
from jax.sharding import PartitionSpec as P

X_CHIPS = 8
VMEM_BYTES = 40 * 2**20


def partials_kernel(x_ref, *refs):
    blocks, (saved_ref, shares_ref, latent_ref, rev_ref) = refs[:-4], refs[-4:]
    nx = latent_ref.shape[1]
    far = nx // 2
    held = (latent_ref, rev_ref)
    for k in range(nx):
        place = lax.rem(x_ref[0] + k, nx)
        for direction in range(2):
            if k == far:
                block = blocks[k + direction]
                for y in range(latent_ref.shape[0]):
                    held[direction][y, place] = block[y]
            else:
                block = blocks[k if k < far else k + 1]
                for y in range(latent_ref.shape[0]):
                    held[direction][y, place] = block[direction, y]
    dp, _, share, _ = shares_ref.shape
    for direction in range(2):
        latent = held[direction][...].reshape(-1, dp * share)
        partial = jnp.dot(saved_ref[direction], latent, preferred_element_type=jnp.float32)
        turned = partial.T.astype(shares_ref.dtype)
        for part in range(dp):
            shares_ref[part, direction] = turned[part * share : (part + 1) * share]


def local(inputs_saved, grad_latent, weights):
    seq = lax.axis_size("seq")
    pipe = lax.axis_size("pipe")
    dp = lax.axis_size("dp")
    nx = X_CHIPS
    ny = seq // nx
    columns = [[y * nx + x for y in range(ny)] for x in range(nx)]

    def along_x(step):
        return [(y * nx + x, y * nx + (x + step) % nx) for y in range(ny) for x in range(nx)]

    right, left = along_x(1), along_x(-1)
    tokens = inputs_saved.shape[3]
    width = inputs_saved.shape[4]
    channels = grad_latent.shape[-1]
    piece = grad_latent.shape[3]

    both = lax.all_gather(grad_latent[0, 0][:, None], "seq", axis=1, tiled=True, axis_index_groups=columns)
    own = both
    from_left, from_right = [own], [own]
    for _ in range(nx // 2 - 1):
        from_left.append(lax.ppermute(from_left[-1], "seq", right))
        from_right.append(lax.ppermute(from_right[-1], "seq", left))
    far_fwd = lax.ppermute(from_left[-1][0], "seq", right)
    far_rev = lax.ppermute(from_right[-1][1], "seq", left)
    blocks = from_right + [far_fwd, far_rev] + from_left[:0:-1]
    x_here = lax.rem(lax.axis_index("seq"), nx).reshape(1)
    vmem = pl.BlockSpec(memory_space=pltpu.VMEM)
    shares, latent_fwd = pl.pallas_call(
        partials_kernel,
        out_shape=(
            jax.ShapeDtypeStruct((dp, 2, channels // dp, width), jnp.bfloat16),
            jax.ShapeDtypeStruct((ny, nx, piece, channels), own.dtype),
        ),
        in_specs=[pl.BlockSpec(memory_space=pltpu.SMEM)] + [vmem] * (len(blocks) + 1),
        out_specs=(vmem, vmem),
        scratch_shapes=[pltpu.VMEM((ny, nx, piece, channels), own.dtype)],
        compiler_params=pltpu.CompilerParams(vmem_limit_bytes=VMEM_BYTES),
        cost_estimate=pl.CostEstimate(
            flops=4 * tokens * channels * width,
            bytes_accessed=4 * tokens * (width + channels),
            transcendentals=0,
        ),
    )(x_here, *blocks, jnp.swapaxes(inputs_saved[0, 0], 1, 2))

    shares = lax.all_to_all(shares, "dp", 0, 0, tiled=True).astype(jnp.float32)
    sum_rev = jnp.sum(shares[:, 1], axis=0)
    mirrored = lax.ppermute(
        sum_rev.astype(jnp.bfloat16), "pipe", [(i, pipe - 1 - i) for i in range(pipe)]
    )
    sum_fwd = jnp.sum(shares[:, 0], axis=0)
    input_grad = lax.dot_general(
        latent_fwd.reshape(tokens, channels),
        weights[0],
        (((1,), (1,)), ((), ())),
        preferred_element_type=jnp.float32,
    ).astype(jnp.bfloat16)
    weight_grad = (sum_fwd + mirrored.astype(jnp.float32)) * (1.0 / tokens)
    return input_grad[None, None], weight_grad.T[None]


def solution(mesh):
    in_specs = (
        P("pipe", "dp", None, None, "seq"),
        P("pipe", "dp", None, "seq", None),
        P("pipe", "seq", None),
    )
    out_specs = (P("pipe", "dp", None, "seq"), P("pipe", "seq", "dp"))
    return jax.shard_map(local, mesh=mesh, in_specs=in_specs, out_specs=out_specs, check_vma=False)
```

time: 122 us -> 102 us (0.84)
  the two profiles are of different devices: /device:TPU:1 before, /device:TPU:6 now
where the time goes in v2:
time: 102 us; the launch traced here: 101 us
  starting transfers between devices  47.7 us (47%)
  blocking collectives  29.8 us (29%)
  waiting for transfers between devices  17 us (17%)
  local copies, waits for them, and re-layouts  2.23 us (2%)
  matrix products  1.64 us (2%)
  Pallas kernels  1.46 us (1%)
    all_gather x1, blocking collectives, local(): lax.all_gather(grad_latent[0, 0][:, None], 'seq', axis=1, tiled=True, axi...  19.3 us
    ppermute x1, starting transfers between devices, local(): lax.ppermute(sum_rev.astype(jnp.bfloat16), 'pipe', [(i, pipe - 1 - i) for...  16.1 us
    ppermute x3, starting transfers between devices, local(): from_left.append(lax.ppermute(from_left[-1], 'seq', right))  15.8 us
    ppermute x3, waiting for transfers between devices, local(): from_left.append(lax.ppermute(from_left[-1], 'seq', right))  11.4 us
    all_to_all x1, blocking collectives, local(): shares = lax.all_to_all(shares, 'dp', 0, 0, tiled=True).astype(jnp.float32)  10.5 us
    ppermute x3, starting transfers between devices, local(): from_right.append(lax.ppermute(from_right[-1], 'seq', left))  8.35 us
    ppermute x1, waiting for transfers between devices, local(): far_rev = lax.ppermute(from_right[-1][1], 'seq', left)  4.76 us
    ppermute x1, starting transfers between devices, local(): far_rev = lax.ppermute(from_right[-1][1], 'seq', left)  4.19 us
  transfers between devices with their start and end apart: 9, of which 6 were waited for; matrix products, arithmetic and copies ran while one was open for 2% of the time, Pallas kernels for 0%

profile of v2, /device:TPU:6, one launch (start us, length us, event | category | flops | bytes accessed | tf_op | source)
XLA Modules:
  0.0 101.3 jit_solution(12703925555776580432)
XLA Ops:
  0.6 0.0 copy-start
  0.6 19.3 %all-gather = bf16[1,1,2,256,384]{4,3,2,1,0:T(8,128)(2,1)S(1)} all-gather(bf16[1,1,2,64,384]{4,3,2,1,0:T(8,128)(2,1)} %param.4), channel_id=2, replica_groups={{0,32,64,96},{4,36,68,100},{8,40,72,104},{12,44,76,108},{16,48,80,112},..., dimensions={3}, use_global_device_ids=true | all-gather | bytes 491520 | tf_op jit(solution)/shard_map/all_gather | solution.py:54
  19.9 4.6 %collective-permute-start.3 = (bf16[2,4,64,384]{3,2,1,0:T(8,128)(2,1)S(1)}, bf16[2,4,64,384]{3,2,1,0:T(8,128)(2,1)S(1)}, u32[]{:S(2)}, u32[]{:S(2)}) collective-permute-start(bf16[2,4,64,384]{3,2,1,0:T(8,128)(2,1)S(1)} %bitcast.21), channel_id=1, source_target_pairs={{0,4},{4,8},{8,12},{12,16},{16,20},{20,24},{24,28},{28,0},{32,36},... | collective-permute-start | bytes 1179656 | tf_op jit(solution)/shard_map/ppermute | solution.py:58
  24.5 1.9 %collective-permute-start = (bf16[2,4,64,384]{3,2,1,0:T(8,128)(2,1)S(1)}, bf16[2,4,64,384]{3,2,1,0:T(8,128)(2,1)S(1)}, u32[]{:S(2)}, u32[]{:S(2)}) collective-permute-start(bf16[2,4,64,384]{3,2,1,0:T(8,128)(2,1)S(1)} %bitcast.22), channel_id=1, source_target_pairs={{0,28},{4,0},{8,4},{12,8},{16,12},{20,16},{24,20},{28,24},{32,60},... | collective-permute-start | bytes 1179656 | tf_op jit(solution)/shard_map/ppermute | solution.py:59
  26.4 3.3 %collective-permute-done.3.refs_8_ = bf16[2,4,64,384]{3,2,1,0:T(8,128)(2,1)S(1)} collective-permute-done((bf16[2,4,64,384]{3,2,1,0:T(8,128)(2,1)S(1)}, bf16[2,4,64,384]{3,2,1,0:T(8,128)(2,1)S(1)}, u32[]{:S(2)}, u32[]{:S(2)}) %collective-permute-start.3) | collective-permute-done | bytes 393248 | tf_op jit(solution)/shard_map/ppermute | solution.py:58
  29.8 5.6 %collective-permute-start.4 = (bf16[2,4,64,384]{3,2,1,0:T(8,128)(2,1)S(1)}, bf16[2,4,64,384]{3,2,1,0:T(8,128)(2,1)S(1)}, u32[]{:S(2)}, u32[]{:S(2)}) collective-permute-start(bf16[2,4,64,384]{3,2,1,0:T(8,128)(2,1)S(1)} %collective-permute-done.3.refs_8_), channel_id=1, source_target_pairs={{0,4},{4,8},{8,12},{12,16},{16,20},{20,24},{24,28},{28,0},{32,36},... | collective-permute-start | bytes 1179656 | tf_op jit(solution)/shard_map/ppermute | solution.py:58
  35.4 0.0 collective-permute-done.refs_1_
  35.4 1.9 %collective-permute-start.1 = (bf16[2,4,64,384]{3,2,1,0:T(8,128)(2,1)S(1)}, bf16[2,4,64,384]{3,2,1,0:T(8,128)(2,1)S(1)}, u32[]{:S(2)}, u32[]{:S(2)}) collective-permute-start(bf16[2,4,64,384]{3,2,1,0:T(8,128)(2,1)S(1)} %collective-permute-done.refs_1_), channel_id=1, source_target_pairs={{0,28},{4,0},{8,4},{12,8},{16,12},{20,16},{24,20},{28,24},{32,60},... | collective-permute-start | bytes 1179656 | tf_op jit(solution)/shard_map/ppermute | solution.py:59
  37.3 3.8 %collective-permute-done.4.refs_7_ = bf16[2,4,64,384]{3,2,1,0:T(8,128)(2,1)S(1)} collective-permute-done((bf16[2,4,64,384]{3,2,1,0:T(8,128)(2,1)S(1)}, bf16[2,4,64,384]{3,2,1,0:T(8,128)(2,1)S(1)}, u32[]{:S(2)}, u32[]{:S(2)}) %collective-permute-start.4) | collective-permute-done | bytes 393248 | tf_op jit(solution)/shard_map/ppermute | solution.py:58
  41.1 5.6 %collective-permute-start.5 = (bf16[2,4,64,384]{3,2,1,0:T(8,128)(2,1)S(1)}, bf16[2,4,64,384]{3,2,1,0:T(8,128)(2,1)S(1)}, u32[]{:S(2)}, u32[]{:S(2)}) collective-permute-start(bf16[2,4,64,384]{3,2,1,0:T(8,128)(2,1)S(1)} %collective-permute-done.4.refs_7_), channel_id=1, source_target_pairs={{0,4},{4,8},{8,12},{12,16},{16,20},{20,24},{24,28},{28,0},{32,36},... | collective-permute-start | bytes 1179656 | tf_op jit(solution)/shard_map/ppermute | solution.py:58
  46.7 0.3 collective-permute-done.1.refs_2_
  47.0 4.5 %collective-permute-start.2 = (bf16[2,4,64,384]{3,2,1,0:T(8,128)(2,1)S(1)}, bf16[2,4,64,384]{3,2,1,0:T(8,128)(2,1)S(1)}, u32[]{:S(2)}, u32[]{:S(2)}) collective-permute-start(bf16[2,4,64,384]{3,2,1,0:T(8,128)(2,1)S(1)} %collective-permute-done.1.refs_2_), channel_id=1, source_target_pairs={{0,28},{4,0},{8,4},{12,8},{16,12},{20,16},{24,20},{28,24},{32,60},... | collective-permute-start | bytes 1179656 | tf_op jit(solution)/shard_map/ppermute | solution.py:59
  51.5 4.3 %collective-permute-done.5.refs_6_ = bf16[2,4,64,384]{3,2,1,0:T(8,128)(2,1)S(1)} collective-permute-done((bf16[2,4,64,384]{3,2,1,0:T(8,128)(2,1)S(1)}, bf16[2,4,64,384]{3,2,1,0:T(8,128)(2,1)S(1)}, u32[]{:S(2)}, u32[]{:S(2)}) %collective-permute-start.5) | collective-permute-done | bytes 393248 | tf_op jit(solution)/shard_map/ppermute | solution.py:58
  55.8 3.2 %collective-permute-start.6 = (bf16[4,64,384]{2,1,0:T(8,128)(2,1)S(1)}, bf16[4,64,384]{2,1,0:T(8,128)(2,1)S(1)}, u32[]{:S(2)}, u32[]{:S(2)}) collective-permute-start(bf16[4,64,384]{2,1,0:T(8,128)(2,1)S(1)} %slice_bitcast_fusion.1), channel_id=1, source_target_pairs={{0,4},{4,8},{8,12},{12,16},{16,20},{20,24},{24,28},{28,0},{32,36},... | collective-permute-start | bytes 589832 | tf_op jit(solution)/shard_map/ppermute | solution.py:60
  59.1 0.0 collective-permute-done.2.refs_3_
  59.1 0.7 slice_bitcast_fusion
  59.8 4.2 %collective-permute-start.7 = (bf16[4,64,384]{2,1,0:T(8,128)(2,1)}, bf16[4,64,384]{2,1,0:T(8,128)(2,1)S(1)}, u32[]{:S(2)}, u32[]{:S(2)}) collective-permute-start(bf16[4,64,384]{2,1,0:T(8,128)(2,1)} %slice_bitcast_fusion), channel_id=1, source_target_pairs={{0,28},{4,0},{8,4},{12,8},{16,12},{20,16},{24,20},{28,24},{32,60},... | collective-permute-start | bytes 589832 | tf_op jit(solution)/shard_map/ppermute | solution.py:61
  64.0 0.0 collective-permute-done.6.refs_4_
  64.0 4.8 %collective-permute-done.7.refs_5_ = bf16[4,64,384]{2,1,0:T(8,128)(2,1)S(1)} collective-permute-done((bf16[4,64,384]{2,1,0:T(8,128)(2,1)}, bf16[4,64,384]{2,1,0:T(8,128)(2,1)S(1)}, u32[]{:S(2)}, u32[]{:S(2)}) %collective-permute-start.7) | collective-permute-done | bytes 196640 | tf_op jit(solution)/shard_map/ppermute | solution.py:61
  68.7 0.0 copy-start.1
  68.7 1.5 %copy-done.1 = bf16[1,1,2,2048,224]{3,4,2,1,0:T(8,128)(2,1)S(1)} copy-done((bf16[1,1,2,2048,224]{3,4,2,1,0:T(8,128)(2,1)S(1)}, bf16[1,1,2,2048,224]{3,4,2,1,0:T(8,128)(2,1)}, u32[]{:S(2)}) %copy-start.1) | copy-done | bytes 1835032
  70.2 1.5 %shard_map.50 = (bf16[4,2,96,224]{3,2,1,0:T(8,128)(2,1)S(1)}, bf16[4,8,64,384]{3,2,1,0:T(8,128)(2,1)S(1)}) custom-call(s32[1]{0:T(128)} %bitcast.x_ref, bf16[2,4,64,384]{3,2,1,0:T(8,128)(2,1)S(1)} %bitcast.23, bf16[2,4,64,384]{3,2,1,0:T(8,128)(2,1)S(1)} %collective-permute-done.refs_1_, bf16[2,4,64,384]{3,2,1,0:T(8,128)(2,1)S(1)} %collective-permute-done.1.refs_2_, ...), custom_call_target="tpu_custom_call" | custom-call | flops 704643072 | bytes 4980736 | tf_op jit(solution)/shard_map/pallas_call | solution.py:65
  71.7 10.5 %all_to_all.5 = bf16[4,2,96,224]{3,2,1,0:T(8,128)(2,1)S(1)} all-to-all(bf16[4,2,96,224]{3,2,1,0:T(8,128)(2,1)S(1)} %get-tuple-element.5), channel_id=1, replica_groups=mesh['pipe'=8,'seq'=32,'dp'=4] {'dp'}, dimensions={0} | all-to-all | bytes 688128 | tf_op jit(solution)/shard_map/all_to_all | solution.py:82
  82.2 0.1 convert_element_type.13
  82.3 0.1 slice_reduce_fusion
  82.4 16.1 %collective-permute-start.8 = (bf16[96,224]{1,0:T(8,128)(2,1)S(1)}, bf16[96,224]{1,0:T(8,128)(2,1)S(1)}, u32[]{:S(2)}, u32[]{:S(2)}) collective-permute-start(bf16[96,224]{1,0:T(8,128)(2,1)S(1)} %get-tuple-element.6), channel_id=1, source_target_pairs={{0,896},{128,768},{256,640},{384,512},{512,384},{640,256},{768,128... | collective-permute-start | bytes 129032 | tf_op jit(solution)/shard_map/ppermute | solution.py:84
  98.5 0.0 copy-done
  98.5 1.6 %fusion = bf16[1,1,2048,224]{2,3,1,0:T(8,128)(2,1)} fusion(bf16[2048,384]{1,0:T(8,128)(2,1)S(1)} %bitcast.24, bf16[1,224,384]{2,1,0:T(8,128)(2,1)S(1)} %copy-done), kind=kOutput, calls=%fused_computation.1 | convolution fusion | flops 352780288 | bytes 2662400 | tf_op jit(solution)/shard_map/dot_general | solution.py:88
  100.2 0.5 collective-permute-done.8
  100.7 0.7 multiply_bitcast_fusion
  (1 shorter events, 0.0 us)
Async XLA Ops:
  0.6 97.9 %copy-start = (bf16[1,224,384]{2,1,0:T(8,128)(2,1)S(1)}, bf16[1,224,384]{2,1,0:T(8,128)(2,1)}, u32[]{:S(2)}) copy-start(bf16[1,224,384]{2,1,0:T(8,128)(2,1)} %param.5) | copy-start | bytes 516100
  19.9 9.9 %collective-permute-start.3 = (bf16[2,4,64,384]{3,2,1,0:T(8,128)(2,1)S(1)}, bf16[2,4,64,384]{3,2,1,0:T(8,128)(2,1)S(1)}, u32[]{:S(2)}, u32[]{:S(2)}) collective-permute-start(bf16[2,4,64,384]{3,2,1,0:T(8,128)(2,1)S(1)} %bitcast.21), channel_id=1, source_target_pairs={{0,4},{4,8},{8,12},{12,16},{16,20},{20,24},{24,28},{28,0},{32,36},... | collective-permute-start | bytes 1179656 | tf_op jit(solution)/shard_map/ppermute | solution.py:58
  24.5 10.9 %collective-permute-start = (bf16[2,4,64,384]{3,2,1,0:T(8,128)(2,1)S(1)}, bf16[2,4,64,384]{3,2,1,0:T(8,128)(2,1)S(1)}, u32[]{:S(2)}, u32[]{:S(2)}) collective-permute-start(bf16[2,4,64,384]{3,2,1,0:T(8,128)(2,1)S(1)} %bitcast.22), channel_id=1, source_target_pairs={{0,28},{4,0},{8,4},{12,8},{16,12},{20,16},{24,20},{28,24},{32,60},... | collective-permute-start | bytes 1179656 | tf_op jit(solution)/shard_map/ppermute | solution.py:59
  29.8 11.3 %collective-permute-start.4 = (bf16[2,4,64,384]{3,2,1,0:T(8,128)(2,1)S(1)}, bf16[2,4,64,384]{3,2,1,0:T(8,128)(2,1)S(1)}, u32[]{:S(2)}, u32[]{:S(2)}) collective-permute-start(bf16[2,4,64,384]{3,2,1,0:T(8,128)(2,1)S(1)} %collective-permute-done.3.refs_8_), channel_id=1, source_target_pairs={{0,4},{4,8},{8,12},{12,16},{16,20},{20,24},{24,28},{28,0},{32,36},... | collective-permute-start | bytes 1179656 | tf_op jit(solution)/shard_map/ppermute | solution.py:58
  35.4 11.6 %collective-permute-start.1 = (bf16[2,4,64,384]{3,2,1,0:T(8,128)(2,1)S(1)}, bf16[2,4,64,384]{3,2,1,0:T(8,128)(2,1)S(1)}, u32[]{:S(2)}, u32[]{:S(2)}) collective-permute-start(bf16[2,4,64,384]{3,2,1,0:T(8,128)(2,1)S(1)} %collective-permute-done.refs_1_), channel_id=1, source_target_pairs={{0,28},{4,0},{8,4},{12,8},{16,12},{20,16},{24,20},{28,24},{32,60},... | collective-permute-start | bytes 1179656 | tf_op jit(solution)/shard_map/ppermute | solution.py:59
  41.1 14.7 %collective-permute-start.5 = (bf16[2,4,64,384]{3,2,1,0:T(8,128)(2,1)S(1)}, bf16[2,4,64,384]{3,2,1,0:T(8,128)(2,1)S(1)}, u32[]{:S(2)}, u32[]{:S(2)}) collective-permute-start(bf16[2,4,64,384]{3,2,1,0:T(8,128)(2,1)S(1)} %collective-permute-done.4.refs_7_), channel_id=1, source_target_pairs={{0,4},{4,8},{8,12},{12,16},{16,20},{20,24},{24,28},{28,0},{32,36},... | collective-permute-start | bytes 1179656 | tf_op jit(solution)/shard_map/ppermute | solution.py:58
  47.0 12.1 %collective-permute-start.2 = (bf16[2,4,64,384]{3,2,1,0:T(8,128)(2,1)S(1)}, bf16[2,4,64,384]{3,2,1,0:T(8,128)(2,1)S(1)}, u32[]{:S(2)}, u32[]{:S(2)}) collective-permute-start(bf16[2,4,64,384]{3,2,1,0:T(8,128)(2,1)S(1)} %collective-permute-done.1.refs_2_), channel_id=1, source_target_pairs={{0,28},{4,0},{8,4},{12,8},{16,12},{20,16},{24,20},{28,24},{32,60},... | collective-permute-start | bytes 1179656 | tf_op jit(solution)/shard_map/ppermute | solution.py:59
  55.8 8.1 %collective-permute-start.6 = (bf16[4,64,384]{2,1,0:T(8,128)(2,1)S(1)}, bf16[4,64,384]{2,1,0:T(8,128)(2,1)S(1)}, u32[]{:S(2)}, u32[]{:S(2)}) collective-permute-start(bf16[4,64,384]{2,1,0:T(8,128)(2,1)S(1)} %slice_bitcast_fusion.1), channel_id=1, source_target_pairs={{0,4},{4,8},{8,12},{12,16},{16,20},{20,24},{24,28},{28,0},{32,36},... | collective-permute-start | bytes 589832 | tf_op jit(solution)/shard_map/ppermute | solution.py:60
  59.8 9.0 %collective-permute-start.7 = (bf16[4,64,384]{2,1,0:T(8,128)(2,1)}, bf16[4,64,384]{2,1,0:T(8,128)(2,1)S(1)}, u32[]{:S(2)}, u32[]{:S(2)}) collective-permute-start(bf16[4,64,384]{2,1,0:T(8,128)(2,1)} %slice_bitcast_fusion), channel_id=1, source_target_pairs={{0,28},{4,0},{8,4},{12,8},{16,12},{20,16},{24,20},{28,24},{32,60},... | collective-permute-start | bytes 589832 | tf_op jit(solution)/shard_map/ppermute | solution.py:61
  68.7 1.5 %copy-start.1 = (bf16[1,1,2,2048,224]{3,4,2,1,0:T(8,128)(2,1)S(1)}, bf16[1,1,2,2048,224]{3,4,2,1,0:T(8,128)(2,1)}, u32[]{:S(2)}) copy-start(bf16[1,1,2,2048,224]{3,4,2,1,0:T(8,128)(2,1)} %param.3) | copy-start | bytes 5505028
  82.4 18.3 %collective-permute-start.8 = (bf16[96,224]{1,0:T(8,128)(2,1)S(1)}, bf16[96,224]{1,0:T(8,128)(2,1)S(1)}, u32[]{:S(2)}, u32[]{:S(2)}) collective-permute-start(bf16[96,224]{1,0:T(8,128)(2,1)S(1)} %get-tuple-element.6), channel_id=1, source_target_pairs={{0,896},{128,768},{256,640},{384,512},{512,384},{640,256},{768,128... | collective-permute-start | bytes 129032 | tf_op jit(solution)/shard_map/ppermute | solution.py:84

commit v3 on v2

v3 whole, which is shorter than its diff:
```python
import jax
import jax.numpy as jnp
from jax import lax
from jax.experimental import pallas as pl
from jax.experimental.pallas import tpu as pltpu
from jax.sharding import PartitionSpec as P

X_CHIPS = 8
VMEM_BYTES = 40 * 2**20


def partials_kernel(place_ref, *refs):
    pieces, (fwd_ref, rev_ref, shares_ref, latent_ref, held_ref) = refs[:-5], refs[-5:]
    ny, nx = latent_ref.shape[:2]
    far, blocks = pieces[:2], pieces[2:]
    half = ny // 2
    dp, _, share, _ = shares_ref.shape
    for direction, (target, saved_ref) in enumerate(((latent_ref, fwd_ref), (held_ref, rev_ref))):
        for y in range(ny):
            target[y, place_ref[0]] = far[y // half][y % half, direction]
            for k, block in enumerate(blocks):
                target[y, place_ref[k + 1]] = block[y, direction]
        latent = target[...].reshape(-1, dp * share)
        partial = jnp.dot(saved_ref[...], latent, preferred_element_type=jnp.float32)
        turned = partial.T.astype(shares_ref.dtype)
        for part in range(dp):
            shares_ref[part, direction] = turned[part * share : (part + 1) * share]


def local(inputs_saved, grad_latent, weights):
    seq = lax.axis_size("seq")
    pipe = lax.axis_size("pipe")
    dp = lax.axis_size("dp")
    nx = X_CHIPS
    ny = seq // nx
    columns = [[y * nx + x for y in range(ny)] for x in range(nx)]

    def along_x(step):
        return [
            (
                (y * nx + x) * dp + d,
                (y * nx + (x + (step if d % 2 == 0 else -step)) % nx) * dp + d,
            )
            for y in range(ny)
            for x in range(nx)
            for d in range(dp)
        ]

    ahead, back = along_x(1), along_x(-1)
    tokens = inputs_saved.shape[3]
    width = inputs_saved.shape[4]
    channels = grad_latent.shape[-1]
    piece = grad_latent.shape[3]

    own = lax.all_gather(grad_latent[0, 0], "seq", axis=0, tiled=True, axis_index_groups=columns)
    own = own.reshape(ny, 2, piece, channels)
    half = ny // 2
    first, second = [own], [own]
    for _ in range(nx // 2 - 1):
        first.append(lax.ppermute(first[-1], ("seq", "dp"), ahead))
        second.append(lax.ppermute(second[-1], ("seq", "dp"), back))
    blocks = [
        lax.ppermute(first[-1][:half], ("seq", "dp"), ahead),
        lax.ppermute(second[-1][half:], ("seq", "dp"), back),
    ]
    x_here = lax.rem(lax.axis_index("seq"), nx)
    sign = 1 - 2 * lax.rem(lax.axis_index("dp"), 2)
    blocks += first + second[1:]
    steps = [nx // 2] + [-k for k in range(len(first))] + list(range(1, len(second)))
    places = jnp.stack([lax.rem(x_here + nx + sign * step, nx) for step in steps])
    saved_fwd, saved_rev = inputs_saved[0, 0, 0].T, inputs_saved[0, 0, 1].T
    vmem = pl.BlockSpec(memory_space=pltpu.VMEM)
    shares, latent_fwd = pl.pallas_call(
        partials_kernel,
        out_shape=(
            jax.ShapeDtypeStruct((dp, 2, channels // dp, width), jnp.bfloat16),
            jax.ShapeDtypeStruct((ny, nx, piece, channels), own.dtype),
        ),
        in_specs=[pl.BlockSpec(memory_space=pltpu.SMEM)] + [vmem] * (len(blocks) + 2),
        out_specs=(vmem, vmem),
        scratch_shapes=[pltpu.VMEM((ny, nx, piece, channels), own.dtype)],
        compiler_params=pltpu.CompilerParams(vmem_limit_bytes=VMEM_BYTES),
        cost_estimate=pl.CostEstimate(
            flops=4 * tokens * channels * width,
            bytes_accessed=4 * tokens * (width + channels),
            transcendentals=0,
        ),
    )(places, *blocks, saved_fwd, saved_rev)

    shares = lax.all_to_all(shares, "dp", 0, 0, tiled=True).astype(jnp.float32)
    sum_rev = jnp.sum(shares[:, 1], axis=0)
    mirrored = lax.ppermute(
        sum_rev.astype(jnp.bfloat16), "pipe", [(i, pipe - 1 - i) for i in range(pipe)]
    )
    sum_fwd = jnp.sum(shares[:, 0], axis=0)
    input_grad = lax.dot_general(
        latent_fwd.reshape(tokens, channels),
        weights[0],
        (((1,), (1,)), ((), ())),
        preferred_element_type=jnp.float32,
    ).astype(jnp.bfloat16)
    weight_grad = (sum_fwd + mirrored.astype(jnp.float32)) * (1.0 / tokens)
    return input_grad[None, None], weight_grad.T[None]


def solution(mesh):
    in_specs = (
        P("pipe", "dp", None, None, "seq"),
        P("pipe", "dp", None, "seq", None),
        P("pipe", "seq", None),
    )
    out_specs = (P("pipe", "dp", None, "seq"), P("pipe", "seq", "dp"))
    return jax.shard_map(local, mesh=mesh, in_specs=in_specs, out_specs=out_specs, check_vma=False)
```

time: 102 us -> 113 us (1.11)
  the two profiles are of different devices: /device:TPU:6 before, /device:TPU:1 now
where the time goes in v3:
time: 113 us; the launch traced here: 112 us
  blocking collectives  42.2 us (37%)
  starting transfers between devices  34.8 us (31%)
  waiting for transfers between devices  20.6 us (18%)
  local copies, waits for them, and re-layouts  8.54 us (8%)
  Pallas kernels  2.43 us (2%)
  matrix products  1.65 us (1%)
    all_to_all x1, blocking collectives, local(): shares = lax.all_to_all(shares, 'dp', 0, 0, tiled=True).astype(jnp.float32)  25.6 us
    all_gather x1, blocking collectives, local(): lax.all_gather(grad_latent[0, 0], 'seq', axis=0, tiled=True, axis_index_g...  16.7 us
    ppermute x1, starting transfers between devices, local(): lax.ppermute(sum_rev.astype(jnp.bfloat16), 'pipe', [(i, pipe - 1 - i) for...  12.3 us
    ppermute x3, starting transfers between devices, local(): first.append(lax.ppermute(first[-1], ('seq', 'dp'), ahead))  11.1 us
    ppermute x3, waiting for transfers between devices, local(): first.append(lax.ppermute(first[-1], ('seq', 'dp'), ahead))  8.26 us
    ppermute x3, waiting for transfers between devices, local(): second.append(lax.ppermute(second[-1], ('seq', 'dp'), back))  8.06 us
    ppermute x3, starting transfers between devices, local(): second.append(lax.ppermute(second[-1], ('seq', 'dp'), back))  6.61 us
    unnamed x18, local copies, waits for them, and re-layouts  5.48 us
  transfers between devices with their start and end apart: 9, of which 6 were waited for; matrix products, arithmetic and copies ran while one was open for 4% of the time, Pallas kernels for 0%

profile of v3, /device:TPU:1, one launch (start us, length us, event | category | flops | bytes accessed | tf_op | source)
XLA Modules:
  0.0 111.9 jit_solution(5780381062350605885)
XLA Ops:
  0.6 0.0 copy-start
  0.6 16.7 %all-gather = bf16[1,1,8,64,384]{4,3,1,0,2:T(8,128)(2,1)S(1)} all-gather(bf16[1,1,2,64,384]{4,3,1,0,2:T(8,128)(2,1)} %bitcast.33), channel_id=2, replica_groups={{0,32,64,96},{4,36,68,100},{8,40,72,104},{12,44,76,108},{16,48,80,112},..., dimensions={2}, use_global_device_ids=true | all-gather | bytes 491520 | tf_op jit(solution)/shard_map/all_gather | solution.py:55
  17.3 2.8 %collective-permute-start.4 = (bf16[4,2,64,384]{3,2,1,0:T(8,128)(2,1)S(1)}, bf16[4,2,64,384]{3,2,1,0:T(8,128)(2,1)S(1)}, u32[]{:S(2)}, u32[]{:S(2)}) collective-permute-start(bf16[4,2,64,384]{3,2,1,0:T(8,128)(2,1)S(1)} %bitcast.29), channel_id=1, source_target_pairs={{0,28},{1,5},{2,30},{3,7},{4,0},{5,9},{6,2},{7,11},{8,4},{9,13},{1... | collective-permute-start | bytes 1179656 | tf_op jit(solution)/shard_map/ppermute | solution.py:61
  20.1 3.7 %collective-permute-start = (bf16[4,2,64,384]{3,2,1,0:T(8,128)(2,1)S(1)}, bf16[4,2,64,384]{3,2,1,0:T(8,128)(2,1)S(1)}, u32[]{:S(2)}, u32[]{:S(2)}) collective-permute-start(bf16[4,2,64,384]{3,2,1,0:T(8,128)(2,1)S(1)} %bitcast.30), channel_id=1, source_target_pairs={{0,4},{1,29},{2,6},{3,31},{4,8},{5,1},{6,10},{7,3},{8,12},{9,5},{1... | collective-permute-start | bytes 1179656 | tf_op jit(solution)/shard_map/ppermute | solution.py:60
  23.8 3.2 %collective-permute-done.4.refs_6_ = bf16[4,2,64,384]{3,2,1,0:T(8,128)(2,1)S(1)} collective-permute-done((bf16[4,2,64,384]{3,2,1,0:T(8,128)(2,1)S(1)}, bf16[4,2,64,384]{3,2,1,0:T(8,128)(2,1)S(1)}, u32[]{:S(2)}, u32[]{:S(2)}) %collective-permute-start.4) | collective-permute-done | bytes 393248 | tf_op jit(solution)/shard_map/ppermute | solution.py:61
  27.0 0.0 copy-start.1
  27.0 1.9 %collective-permute-start.5 = (bf16[4,2,64,384]{3,2,1,0:T(8,128)(2,1)S(1)}, bf16[4,2,64,384]{3,2,1,0:T(8,128)(2,1)S(1)}, u32[]{:S(2)}, u32[]{:S(2)}) collective-permute-start(bf16[4,2,64,384]{3,2,1,0:T(8,128)(2,1)S(1)} %collective-permute-done.4.refs_6_), channel_id=1, source_target_pairs={{0,28},{1,5},{2,30},{3,7},{4,0},{5,9},{6,2},{7,11},{8,4},{9,13},{1... | collective-permute-start | bytes 1179656 | tf_op jit(solution)/shard_map/ppermute | solution.py:61
  29.0 0.0 collective-permute-done.refs_3_
  29.0 0.0 copy-start.3
  29.0 4.6 %collective-permute-start.1 = (bf16[4,2,64,384]{3,2,1,0:T(8,128)(2,1)S(1)}, bf16[4,2,64,384]{3,2,1,0:T(8,128)(2,1)S(1)}, u32[]{:S(2)}, u32[]{:S(2)}) collective-permute-start(bf16[4,2,64,384]{3,2,1,0:T(8,128)(2,1)S(1)} %collective-permute-done.refs_3_), channel_id=1, source_target_pairs={{0,4},{1,29},{2,6},{3,31},{4,8},{5,1},{6,10},{7,3},{8,12},{9,5},{1... | collective-permute-start | bytes 1179656 | tf_op jit(solution)/shard_map/ppermute | solution.py:60
  33.6 3.2 %collective-permute-done.5.refs_7_ = bf16[4,2,64,384]{3,2,1,0:T(8,128)(2,1)S(1)} collective-permute-done((bf16[4,2,64,384]{3,2,1,0:T(8,128)(2,1)S(1)}, bf16[4,2,64,384]{3,2,1,0:T(8,128)(2,1)S(1)}, u32[]{:S(2)}, u32[]{:S(2)}) %collective-permute-start.5) | collective-permute-done | bytes 393248 | tf_op jit(solution)/shard_map/ppermute | solution.py:61
  36.8 1.9 %collective-permute-start.6 = (bf16[4,2,64,384]{3,2,1,0:T(8,128)(2,1)S(1)}, bf16[4,2,64,384]{3,2,1,0:T(8,128)(2,1)S(1)}, u32[]{:S(2)}, u32[]{:S(2)}) collective-permute-start(bf16[4,2,64,384]{3,2,1,0:T(8,128)(2,1)S(1)} %collective-permute-done.5.refs_7_), channel_id=1, source_target_pairs={{0,28},{1,5},{2,30},{3,7},{4,0},{5,9},{6,2},{7,11},{8,4},{9,13},{1... | collective-permute-start | bytes 1179656 | tf_op jit(solution)/shard_map/ppermute | solution.py:61
  38.7 0.0 copy-start.5
  38.7 0.7 copy-done.5
  39.4 3.2 %collective-permute-done.1.refs_4_ = bf16[4,2,64,384]{3,2,1,0:T(8,128)(2,1)S(1)} collective-permute-done((bf16[4,2,64,384]{3,2,1,0:T(8,128)(2,1)S(1)}, bf16[4,2,64,384]{3,2,1,0:T(8,128)(2,1)S(1)}, u32[]{:S(2)}, u32[]{:S(2)}) %collective-permute-start.1) | collective-permute-done | bytes 393248 | tf_op jit(solution)/shard_map/ppermute | solution.py:60
  42.6 2.8 %collective-permute-start.2 = (bf16[4,2,64,384]{3,2,1,0:T(8,128)(2,1)S(1)}, bf16[4,2,64,384]{3,2,1,0:T(8,128)(2,1)S(1)}, u32[]{:S(2)}, u32[]{:S(2)}) collective-permute-start(bf16[4,2,64,384]{3,2,1,0:T(8,128)(2,1)S(1)} %collective-permute-done.1.refs_4_), channel_id=1, source_target_pairs={{0,4},{1,29},{2,6},{3,31},{4,8},{5,1},{6,10},{7,3},{8,12},{9,5},{1... | collective-permute-start | bytes 1179656 | tf_op jit(solution)/shard_map/ppermute | solution.py:60
  45.5 0.0 copy-start.7
  45.5 0.7 copy-done.7
  46.2 1.6 %collective-permute-done.6.refs_8_ = bf16[4,2,64,384]{3,2,1,0:T(8,128)(2,1)S(1)} collective-permute-done((bf16[4,2,64,384]{3,2,1,0:T(8,128)(2,1)S(1)}, bf16[4,2,64,384]{3,2,1,0:T(8,128)(2,1)S(1)}, u32[]{:S(2)}, u32[]{:S(2)}) %collective-permute-start.6) | collective-permute-done | bytes 393248 | tf_op jit(solution)/shard_map/ppermute | solution.py:61
  47.9 0.7 slice.25
  48.6 1.9 %collective-permute-start.7 = (bf16[2,2,64,384]{3,2,1,0:T(8,128)(2,1)}, bf16[2,2,64,384]{3,2,1,0:T(8,128)(2,1)S(1)}, u32[]{:S(2)}, u32[]{:S(2)}) collective-permute-start(bf16[2,2,64,384]{3,2,1,0:T(8,128)(2,1)} %slice.25), channel_id=1, source_target_pairs={{0,28},{1,5},{2,30},{3,7},{4,0},{5,9},{6,2},{7,11},{8,4},{9,13},{1... | collective-permute-start | bytes 589832 | tf_op jit(solution)/shard_map/ppermute | solution.py:64
  50.5 5.0 %collective-permute-done.2.refs_5_ = bf16[4,2,64,384]{3,2,1,0:T(8,128)(2,1)S(1)} collective-permute-done((bf16[4,2,64,384]{3,2,1,0:T(8,128)(2,1)S(1)}, bf16[4,2,64,384]{3,2,1,0:T(8,128)(2,1)S(1)}, u32[]{:S(2)}, u32[]{:S(2)}) %collective-permute-start.2) | collective-permute-done | bytes 393248 | tf_op jit(solution)/shard_map/ppermute | solution.py:60
  55.5 0.7 slice.24
  56.2 0.0 copy-done.1
  56.2 0.0 copy-done.3
  56.2 3.0 %collective-permute-start.3 = (bf16[2,2,64,384]{3,2,1,0:T(8,128)(2,1)}, bf16[2,2,64,384]{3,2,1,0:T(8,128)(2,1)}, u32[]{:S(2)}, u32[]{:S(2)}) collective-permute-start(bf16[2,2,64,384]{3,2,1,0:T(8,128)(2,1)} %slice.24), channel_id=1, source_target_pairs={{0,4},{1,29},{2,6},{3,31},{4,8},{5,1},{6,10},{7,3},{8,12},{9,5},{1... | collective-permute-start | bytes 589832 | tf_op jit(solution)/shard_map/ppermute | solution.py:63
  59.2 1.6 %slice_bitcast_fusion = (bf16[224,2048]{1,0:T(8,128)(2,1)S(1)}, bf16[224,2048]{1,0:T(8,128)(2,1)S(1)}) fusion(bf16[1,1,2,2048,224]{3,4,2,1,0:T(8,128)(2,1)} %param.3), kind=kLoop, calls=%fused_computation.2 | loop fusion | bytes 3670016 | tf_op jit(solution)/shard_map/transpose | solution.py:71
  60.8 0.1 stack.35.place_ref
  60.9 0.0 collective-permute-done.7.refs_1_
  60.9 4.3 %collective-permute-done.3.refs_0_ = bf16[2,2,64,384]{3,2,1,0:T(8,128)(2,1)} collective-permute-done((bf16[2,2,64,384]{3,2,1,0:T(8,128)(2,1)}, bf16[2,2,64,384]{3,2,1,0:T(8,128)(2,1)}, u32[]{:S(2)}, u32[]{:S(2)}) %collective-permute-start.3) | collective-permute-done | bytes 196640 | tf_op jit(solution)/shard_map/ppermute | solution.py:63
  65.3 0.0 copy-start.2
  65.3 1.0 copy-done.2
  66.3 0.0 copy-start.4
  66.3 1.0 copy-done.4
  67.3 0.0 copy-start.6
  67.3 1.0 copy-done.6
  68.2 0.0 copy-start.8
  68.2 1.0 copy-done.8
  69.2 2.4 %shard_map.50 = (bf16[4,2,96,224]{3,2,1,0:T(8,128)(2,1)S(1)}, bf16[4,8,64,384]{3,2,1,0:T(8,128)(2,1)S(1)}) custom-call(s32[8]{0:T(128)S(1)} %stack.35.place_ref, bf16[2,2,64,384]{3,2,1,0:T(8,128)(2,1)} %collective-permute-done.3.refs_0_, bf16[2,2,64,384]{3,2,1,0:T(8,128)(2,1)S(1)} %collective-permute-done.7.refs_1_, bf16[4,2,64,384]{3,2,1,0:T(8,128)(2,1)S(1)} %bitcast.31, ...), custom_call_target="tpu_custom_call" | custom-call | flops 704643072 | bytes 4980736 | tf_op jit(solution)/shard_map/pallas_call | solution.py:73
  71.7 25.6 %all_to_all.5 = bf16[4,2,96,224]{3,2,1,0:T(8,128)(2,1)S(1)} all-to-all(bf16[4,2,96,224]{3,2,1,0:T(8,128)(2,1)S(1)} %get-tuple-element.5), channel_id=1, replica_groups=mesh['pipe'=8,'seq'=32,'dp'=4] {'dp'}, dimensions={0} | all-to-all | bytes 688128 | tf_op jit(solution)/shard_map/all_to_all | solution.py:90
  97.2 0.1 convert_element_type.13
  97.3 0.1 slice_reduce_fusion
  97.4 12.3 %collective-permute-start.8 = (bf16[96,224]{1,0:T(8,128)(2,1)S(1)}, bf16[96,224]{1,0:T(8,128)(2,1)S(1)}, u32[]{:S(2)}, u32[]{:S(2)}) collective-permute-start(bf16[96,224]{1,0:T(8,128)(2,1)S(1)} %get-tuple-element.6), channel_id=1, source_target_pairs={{0,896},{128,768},{256,640},{384,512},{512,384},{640,256},{768,128... | collective-permute-start | bytes 129032 | tf_op jit(solution)/shard_map/ppermute | solution.py:92
  109.6 0.0 copy-done
  109.6 1.6 %fusion = bf16[1,1,2048,224]{2,3,1,0:T(8,128)(2,1)} fusion(bf16[2048,384]{1,0:T(8,128)(2,1)S(1)} %bitcast.32, bf16[1,224,384]{2,1,0:T(8,128)(2,1)S(1)} %copy-done), kind=kOutput, calls=%fused_computation.1 | convolution fusion | flops 352780288 | bytes 2662400 | tf_op jit(solution)/shard_map/dot_general | solution.py:96
  111.3 0.0 collective-permute-done.8
  111.3 0.7 multiply_bitcast_fusion
Async XLA Ops:
  0.6 109.0 %copy-start = (bf16[1,224,384]{2,1,0:T(8,128)(2,1)S(1)}, bf16[1,224,384]{2,1,0:T(8,128)(2,1)}, u32[]{:S(2)}) copy-start(bf16[1,224,384]{2,1,0:T(8,128)(2,1)} %param.5) | copy-start | bytes 516100
  17.3 9.7 %collective-permute-start.4 = (bf16[4,2,64,384]{3,2,1,0:T(8,128)(2,1)S(1)}, bf16[4,2,64,384]{3,2,1,0:T(8,128)(2,1)S(1)}, u32[]{:S(2)}, u32[]{:S(2)}) collective-permute-start(bf16[4,2,64,384]{3,2,1,0:T(8,128)(2,1)S(1)} %bitcast.29), channel_id=1, source_target_pairs={{0,28},{1,5},{2,30},{3,7},{4,0},{5,9},{6,2},{7,11},{8,4},{9,13},{1... | collective-permute-start | bytes 1179656 | tf_op jit(solution)/shard_map/ppermute | solution.py:61
  20.1 8.8 %collective-permute-start = (bf16[4,2,64,384]{3,2,1,0:T(8,128)(2,1)S(1)}, bf16[4,2,64,384]{3,2,1,0:T(8,128)(2,1)S(1)}, u32[]{:S(2)}, u32[]{:S(2)}) collective-permute-start(bf16[4,2,64,384]{3,2,1,0:T(8,128)(2,1)S(1)} %bitcast.30), channel_id=1, source_target_pairs={{0,4},{1,29},{2,6},{3,31},{4,8},{5,1},{6,10},{7,3},{8,12},{9,5},{1... | collective-permute-start | bytes 1179656 | tf_op jit(solution)/shard_map/ppermute | solution.py:60
  27.0 29.2 %copy-start.1 = (bf16[4,2,64,384]{3,2,1,0:T(8,128)(2,1)}, bf16[4,2,64,384]{3,2,1,0:T(8,128)(2,1)S(1)}, u32[]{:S(2)}) copy-start(bf16[4,2,64,384]{3,2,1,0:T(8,128)(2,1)S(1)} %collective-permute-done.4.refs_6_) | copy-start | bytes 1179652
  27.0 9.7 %collective-permute-start.5 = (bf16[4,2,64,384]{3,2,1,0:T(8,128)(2,1)S(1)}, bf16[4,2,64,384]{3,2,1,0:T(8,128)(2,1)S(1)}, u32[]{:S(2)}, u32[]{:S(2)}) collective-permute-start(bf16[4,2,64,384]{3,2,1,0:T(8,128)(2,1)S(1)} %collective-permute-done.4.refs_6_), channel_id=1, source_target_pairs={{0,28},{1,5},{2,30},{3,7},{4,0},{5,9},{6,2},{7,11},{8,4},{9,13},{1... | collective-permute-start | bytes 1179656 | tf_op jit(solution)/shard_map/ppermute | solution.py:61
  29.0 27.3 %copy-start.3 = (bf16[4,2,64,384]{3,2,1,0:T(8,128)(2,1)}, bf16[4,2,64,384]{3,2,1,0:T(8,128)(2,1)S(1)}, u32[]{:S(2)}) copy-start(bf16[4,2,64,384]{3,2,1,0:T(8,128)(2,1)S(1)} %collective-permute-done.refs_3_) | copy-start | bytes 1179652
  29.0 13.7 %collective-permute-start.1 = (bf16[4,2,64,384]{3,2,1,0:T(8,128)(2,1)S(1)}, bf16[4,2,64,384]{3,2,1,0:T(8,128)(2,1)S(1)}, u32[]{:S(2)}, u32[]{:S(2)}) collective-permute-start(bf16[4,2,64,384]{3,2,1,0:T(8,128)(2,1)S(1)} %collective-permute-done.refs_3_), channel_id=1, source_target_pairs={{0,4},{1,29},{2,6},{3,31},{4,8},{5,1},{6,10},{7,3},{8,12},{9,5},{1... | collective-permute-start | bytes 1179656 | tf_op jit(solution)/shard_map/ppermute | solution.py:60
  36.8 11.1 %collective-permute-start.6 = (bf16[4,2,64,384]{3,2,1,0:T(8,128)(2,1)S(1)}, bf16[4,2,64,384]{3,2,1,0:T(8,128)(2,1)S(1)}, u32[]{:S(2)}, u32[]{:S(2)}) collective-permute-start(bf16[4,2,64,384]{3,2,1,0:T(8,128)(2,1)S(1)} %collective-permute-done.5.refs_7_), channel_id=1, source_target_pairs={{0,28},{1,5},{2,30},{3,7},{4,0},{5,9},{6,2},{7,11},{8,4},{9,13},{1... | collective-permute-start | bytes 1179656 | tf_op jit(solution)/shard_map/ppermute | solution.py:61
  38.7 0.7 copy-start.5
  42.6 12.9 %collective-permute-start.2 = (bf16[4,2,64,384]{3,2,1,0:T(8,128)(2,1)S(1)}, bf16[4,2,64,384]{3,2,1,0:T(8,128)(2,1)S(1)}, u32[]{:S(2)}, u32[]{:S(2)}) collective-permute-start(bf16[4,2,64,384]{3,2,1,0:T(8,128)(2,1)S(1)} %collective-permute-done.1.refs_4_), channel_id=1, source_target_pairs={{0,4},{1,29},{2,6},{3,31},{4,8},{5,1},{6,10},{7,3},{8,12},{9,5},{1... | collective-permute-start | bytes 1179656 | tf_op jit(solution)/shard_map/ppermute | solution.py:60
  45.5 0.7 copy-start.7
  48.6 12.4 %collective-permute-start.7 = (bf16[2,2,64,384]{3,2,1,0:T(8,128)(2,1)}, bf16[2,2,64,384]{3,2,1,0:T(8,128)(2,1)S(1)}, u32[]{:S(2)}, u32[]{:S(2)}) collective-permute-start(bf16[2,2,64,384]{3,2,1,0:T(8,128)(2,1)} %slice.25), channel_id=1, source_target_pairs={{0,28},{1,5},{2,30},{3,7},{4,0},{5,9},{6,2},{7,11},{8,4},{9,13},{1... | collective-permute-start | bytes 589832 | tf_op jit(solution)/shard_map/ppermute | solution.py:64
  56.2 9.0 %collective-permute-start.3 = (bf16[2,2,64,384]{3,2,1,0:T(8,128)(2,1)}, bf16[2,2,64,384]{3,2,1,0:T(8,128)(2,1)}, u32[]{:S(2)}, u32[]{:S(2)}) collective-permute-start(bf16[2,2,64,384]{3,2,1,0:T(8,128)(2,1)} %slice.24), channel_id=1, source_target_pairs={{0,4},{1,29},{2,6},{3,31},{4,8},{5,1},{6,10},{7,3},{8,12},{9,5},{1... | collective-permute-start | bytes 589832 | tf_op jit(solution)/shard_map/ppermute | solution.py:63
  65.3 1.0 copy-start.2
  66.3 1.0 copy-start.4
  67.3 1.0 copy-start.6
  68.2 1.0 copy-start.8
  97.4 13.9 %collective-permute-start.8 = (bf16[96,224]{1,0:T(8,128)(2,1)S(1)}, bf16[96,224]{1,0:T(8,128)(2,1)S(1)}, u32[]{:S(2)}, u32[]{:S(2)}) collective-permute-start(bf16[96,224]{1,0:T(8,128)(2,1)S(1)} %get-tuple-element.6), channel_id=1, source_target_pairs={{0,896},{128,768},{256,640},{384,512},{512,384},{640,256},{768,128... | collective-permute-start | bytes 129032 | tf_op jit(solution)/shard_map/ppermute | solution.py:92

commit v4 on v2

--- a/solution.py
+++ b/solution.py
@@ -9,29 +9,48 @@
 VMEM_BYTES = 40 * 2**20
 
 
-def partials_kernel(x_ref, *refs):
-    blocks, (saved_ref, shares_ref, latent_ref, rev_ref) = refs[:-4], refs[-4:]
-    nx = latent_ref.shape[1]
+def early_kernel(x_ref, *refs):
+    blocks, (saved_ref, partial_ref, picked_ref, latent_ref, rev_ref) = refs[:-5], refs[-5:]
+    ny, nx, piece, channels = latent_ref.shape
     far = nx // 2
-    held = (latent_ref, rev_ref)
-    for k in range(nx):
-        place = lax.rem(x_ref[0] + k, nx)
-        for direction in range(2):
-            if k == far:
-                block = blocks[k + direction]
-                for y in range(latent_ref.shape[0]):
-                    held[direction][y, place] = block[y]
-            else:
-                block = blocks[k if k < far else k + 1]
-                for y in range(latent_ref.shape[0]):
-                    held[direction][y, place] = block[direction, y]
+    width = saved_ref.shape[1]
+    far_place = lax.rem(x_ref[0] + far, nx)
+    row = lax.broadcasted_iota(jnp.int32, (nx * piece, piece), 0)
+    column = lax.broadcasted_iota(jnp.int32, (nx * piece, piece), 1)
+    pick = jnp.where(row == column + far_place * piece, 1.0, 0.0).astype(saved_ref.dtype)
+    for direction, target in enumerate((latent_ref, rev_ref)):
+        for k, block in enumerate(blocks):
+            place = lax.rem(x_ref[0] + (k if k < far else k + 1), nx)
+            for y in range(ny):
+                target[y, place] = block[direction, y]
+        for y in range(ny):
+            target[y, far_place] = jnp.zeros((piece, channels), target.dtype)
+            part = saved_ref[direction, :, y * nx * piece : (y + 1) * nx * piece]
+            picked = jnp.dot(part, pick, preferred_element_type=jnp.float32)
+            picked_ref[direction, y] = picked.astype(picked_ref.dtype)
+        latent = target[...].reshape(-1, channels)
+        partial_ref[direction] = jnp.dot(
+            saved_ref[direction], latent, preferred_element_type=jnp.float32
+        )
+
+
+def late_kernel(x_ref, fwd_ref, rev_ref, partial_ref, picked_ref, latent_in, *refs):
+    shares_ref, latent_ref, sem = refs
+    ny, nx = latent_in.shape[:2]
     dp, _, share, _ = shares_ref.shape
-    for direction in range(2):
-        latent = held[direction][...].reshape(-1, dp * share)
-        partial = jnp.dot(saved_ref[direction], latent, preferred_element_type=jnp.float32)
-        turned = partial.T.astype(shares_ref.dtype)
+    far_place = lax.rem(x_ref[0] + nx // 2, nx)
+    fill = pltpu.make_async_copy(fwd_ref, latent_ref.at[:, far_place], sem)
+    fill.start()
+    for direction, far_ref in enumerate((fwd_ref, rev_ref)):
+        total = partial_ref[direction]
+        for y in range(ny):
+            total += jnp.dot(
+                picked_ref[direction, y], far_ref[y], preferred_element_type=jnp.float32
+            )
+        turned = total.T.astype(shares_ref.dtype)
         for part in range(dp):
             shares_ref[part, direction] = turned[part * share : (part + 1) * share]
+    fill.wait()
 
 
 def local(inputs_saved, grad_latent, weights):
@@ -59,25 +78,48 @@
         from_right.append(lax.ppermute(from_right[-1], "seq", left))
     far_fwd = lax.ppermute(from_left[-1][0], "seq", right)
     far_rev = lax.ppermute(from_right[-1][1], "seq", left)
-    blocks = from_right + [far_fwd, far_rev] + from_left[:0:-1]
+    blocks = from_right + from_left[:0:-1]
     x_here = lax.rem(lax.axis_index("seq"), nx).reshape(1)
+    saved = jnp.swapaxes(inputs_saved[0, 0], 1, 2)
     vmem = pl.BlockSpec(memory_space=pltpu.VMEM)
-    shares, latent_fwd = pl.pallas_call(
-        partials_kernel,
+    smem = pl.BlockSpec(memory_space=pltpu.SMEM)
+    anywhere = pl.BlockSpec(memory_space=pl.ANY)
+    latent_shape = jax.ShapeDtypeStruct((ny, nx, piece, channels), own.dtype)
+    settings = pltpu.CompilerParams(vmem_limit_bytes=VMEM_BYTES)
+    partial, picked, latent_fwd = pl.pallas_call(
+        early_kernel,
         out_shape=(
-            jax.ShapeDtypeStruct((dp, 2, channels // dp, width), jnp.bfloat16),
-            jax.ShapeDtypeStruct((ny, nx, piece, channels), own.dtype),
+            jax.ShapeDtypeStruct((2, width, channels), jnp.float32),
+            jax.ShapeDtypeStruct((2, ny, width, piece), saved.dtype),
+            latent_shape,
         ),
-        in_specs=[pl.BlockSpec(memory_space=pltpu.SMEM)] + [vmem] * (len(blocks) + 1),
-        out_specs=(vmem, vmem),
-        scratch_shapes=[pltpu.VMEM((ny, nx, piece, channels), own.dtype)],
-        compiler_params=pltpu.CompilerParams(vmem_limit_bytes=VMEM_BYTES),
+        in_specs=[smem] + [vmem] * (len(blocks) + 1),
+        out_specs=(vmem, vmem, vmem),
+        scratch_shapes=[pltpu.VMEM(latent_shape.shape, own.dtype)],
+        compiler_params=settings,
         cost_estimate=pl.CostEstimate(
             flops=4 * tokens * channels * width,
             bytes_accessed=4 * tokens * (width + channels),
             transcendentals=0,
         ),
-    )(x_here, *blocks, jnp.swapaxes(inputs_saved[0, 0], 1, 2))
+    )(x_here, *blocks, saved)
+    shares, latent_fwd = pl.pallas_call(
+        late_kernel,
+        out_shape=(
+            jax.ShapeDtypeStruct((dp, 2, channels // dp, width), jnp.bfloat16),
+            latent_shape,
+        ),
+        in_specs=[smem] + [vmem] * 4 + [anywhere],
+        out_specs=(vmem, anywhere),
+        scratch_shapes=[pltpu.SemaphoreType.DMA],
+        input_output_aliases={5: 1},
+        compiler_params=settings,
+        cost_estimate=pl.CostEstimate(
+            flops=4 * ny * piece * channels * width,
+            bytes_accessed=12 * channels * width,
+            transcendentals=0,
+        ),
+    )(x_here, far_fwd, far_rev, partial, picked, latent_fwd)
 
     shares = lax.all_to_all(shares, "dp", 0, 0, tiled=True).astype(jnp.float32)
     sum_rev = jnp.sum(shares[:, 1], axis=0)

time: 102 us -> 99.5 us (0.975)
  waiting for transfers between devices: 17 us -> 13.7 us
  Pallas kernels: 1.46 us -> 2.51 us
    ppermute x1, waiting for transfers between devices: 4.76 us -> 1.43 us  [local(): far_rev = lax.ppermute(from_right[-1][1], 'seq', left)]
    pallas_call x1 -> x2, Pallas kernels: 1.46 us -> 2.51 us  [the longest x1 1.83 us: local(): pl.pallas_call(early_kernel, out_shape=(jax.ShapeDtypeStruct((2, width, c...]
  transfers between devices with their start and end apart: 9 -> 9, of which waited for: 6 -> 6; matrix products, arithmetic and copies ran while one was open for 2% -> 2% of each run, Pallas kernels for 0% -> 2%
where the time goes in v4:
time: 99.5 us; the launch traced here: 99 us
  starting transfers between devices  47.7 us (48%)
  blocking collectives  29.8 us (30%)
  waiting for transfers between devices  13.7 us (14%)
  Pallas kernels  2.51 us (3%)
  local copies, waits for them, and re-layouts  2.22 us (2%)
  matrix products  1.64 us (2%)
    all_gather x1, blocking collectives, local(): lax.all_gather(grad_latent[0, 0][:, None], 'seq', axis=1, tiled=True, axi...  19.3 us
    ppermute x1, starting transfers between devices, local(): lax.ppermute(sum_rev.astype(jnp.bfloat16), 'pipe', [(i, pipe - 1 - i) for...  16.1 us
    ppermute x3, starting transfers between devices, local(): from_left.append(lax.ppermute(from_left[-1], 'seq', right))  15.8 us
    ppermute x3, waiting for transfers between devices, local(): from_left.append(lax.ppermute(from_left[-1], 'seq', right))  11.4 us
    all_to_all x1, blocking collectives, local(): shares = lax.all_to_all(shares, 'dp', 0, 0, tiled=True).astype(jnp.float32)  10.5 us
    ppermute x3, starting transfers between devices, local(): from_right.append(lax.ppermute(from_right[-1], 'seq', left))  8.35 us
    ppermute x1, starting transfers between devices, local(): far_rev = lax.ppermute(from_right[-1][1], 'seq', left)  4.19 us
    ppermute x1, starting transfers between devices, local(): far_fwd = lax.ppermute(from_left[-1][0], 'seq', right)  3.22 us
  transfers between devices with their start and end apart: 9, of which 6 were waited for; matrix products, arithmetic and copies ran while one was open for 2% of the time, Pallas kernels for 2%

profile of v4, /device:TPU:6, one launch (start us, length us, event | category | flops | bytes accessed | tf_op | source)
XLA Modules:
  0.0 99.0 jit_solution(1723365922100386473)
XLA Ops:
  0.6 0.0 copy-start
  0.6 19.3 %all-gather = bf16[1,1,2,256,384]{4,3,2,1,0:T(8,128)(2,1)S(1)} all-gather(bf16[1,1,2,64,384]{4,3,2,1,0:T(8,128)(2,1)} %param.4), channel_id=2, replica_groups={{0,32,64,96},{4,36,68,100},{8,40,72,104},{12,44,76,108},{16,48,80,112},..., dimensions={3}, use_global_device_ids=true | all-gather | bytes 491520 | tf_op jit(solution)/shard_map/all_gather | solution.py:73
  19.9 4.6 %collective-permute-start = (bf16[2,4,64,384]{3,2,1,0:T(8,128)(2,1)S(1)}, bf16[2,4,64,384]{3,2,1,0:T(8,128)(2,1)S(1)}, u32[]{:S(2)}, u32[]{:S(2)}) collective-permute-start(bf16[2,4,64,384]{3,2,1,0:T(8,128)(2,1)S(1)} %bitcast.22), channel_id=1, source_target_pairs={{0,4},{4,8},{8,12},{12,16},{16,20},{20,24},{24,28},{28,0},{32,36},... | collective-permute-start | bytes 1179656 | tf_op jit(solution)/shard_map/ppermute | solution.py:77
  24.5 1.9 %collective-permute-start.4 = (bf16[2,4,64,384]{3,2,1,0:T(8,128)(2,1)S(1)}, bf16[2,4,64,384]{3,2,1,0:T(8,128)(2,1)S(1)}, u32[]{:S(2)}, u32[]{:S(2)}) collective-permute-start(bf16[2,4,64,384]{3,2,1,0:T(8,128)(2,1)S(1)} %bitcast.23), channel_id=1, source_target_pairs={{0,28},{4,0},{8,4},{12,8},{16,12},{20,16},{24,20},{28,24},{32,60},... | collective-permute-start | bytes 1179656 | tf_op jit(solution)/shard_map/ppermute | solution.py:78
  26.4 3.3 %collective-permute-done.refs_6_ = bf16[2,4,64,384]{3,2,1,0:T(8,128)(2,1)S(1)} collective-permute-done((bf16[2,4,64,384]{3,2,1,0:T(8,128)(2,1)S(1)}, bf16[2,4,64,384]{3,2,1,0:T(8,128)(2,1)S(1)}, u32[]{:S(2)}, u32[]{:S(2)}) %collective-permute-start) | collective-permute-done | bytes 393248 | tf_op jit(solution)/shard_map/ppermute | solution.py:77
  29.8 5.6 %collective-permute-start.1 = (bf16[2,4,64,384]{3,2,1,0:T(8,128)(2,1)S(1)}, bf16[2,4,64,384]{3,2,1,0:T(8,128)(2,1)S(1)}, u32[]{:S(2)}, u32[]{:S(2)}) collective-permute-start(bf16[2,4,64,384]{3,2,1,0:T(8,128)(2,1)S(1)} %collective-permute-done.refs_6_), channel_id=1, source_target_pairs={{0,4},{4,8},{8,12},{12,16},{16,20},{20,24},{24,28},{28,0},{32,36},... | collective-permute-start | bytes 1179656 | tf_op jit(solution)/shard_map/ppermute | solution.py:77
  35.4 0.0 collective-permute-done.4.refs_1_
  35.4 1.9 %collective-permute-start.5 = (bf16[2,4,64,384]{3,2,1,0:T(8,128)(2,1)S(1)}, bf16[2,4,64,384]{3,2,1,0:T(8,128)(2,1)S(1)}, u32[]{:S(2)}, u32[]{:S(2)}) collective-permute-start(bf16[2,4,64,384]{3,2,1,0:T(8,128)(2,1)S(1)} %collective-permute-done.4.refs_1_), channel_id=1, source_target_pairs={{0,28},{4,0},{8,4},{12,8},{16,12},{20,16},{24,20},{28,24},{32,60},... | collective-permute-start | bytes 1179656 | tf_op jit(solution)/shard_map/ppermute | solution.py:78
  37.3 3.8 %collective-permute-done.1.refs_5_ = bf16[2,4,64,384]{3,2,1,0:T(8,128)(2,1)S(1)} collective-permute-done((bf16[2,4,64,384]{3,2,1,0:T(8,128)(2,1)S(1)}, bf16[2,4,64,384]{3,2,1,0:T(8,128)(2,1)S(1)}, u32[]{:S(2)}, u32[]{:S(2)}) %collective-permute-start.1) | collective-permute-done | bytes 393248 | tf_op jit(solution)/shard_map/ppermute | solution.py:77
  41.1 5.6 %collective-permute-start.2 = (bf16[2,4,64,384]{3,2,1,0:T(8,128)(2,1)S(1)}, bf16[2,4,64,384]{3,2,1,0:T(8,128)(2,1)S(1)}, u32[]{:S(2)}, u32[]{:S(2)}) collective-permute-start(bf16[2,4,64,384]{3,2,1,0:T(8,128)(2,1)S(1)} %collective-permute-done.1.refs_5_), channel_id=1, source_target_pairs={{0,4},{4,8},{8,12},{12,16},{16,20},{20,24},{24,28},{28,0},{32,36},... | collective-permute-start | bytes 1179656 | tf_op jit(solution)/shard_map/ppermute | solution.py:77
  46.7 0.3 collective-permute-done.5.refs_2_
  47.0 4.5 %collective-permute-start.6 = (bf16[2,4,64,384]{3,2,1,0:T(8,128)(2,1)S(1)}, bf16[2,4,64,384]{3,2,1,0:T(8,128)(2,1)S(1)}, u32[]{:S(2)}, u32[]{:S(2)}) collective-permute-start(bf16[2,4,64,384]{3,2,1,0:T(8,128)(2,1)S(1)} %collective-permute-done.5.refs_2_), channel_id=1, source_target_pairs={{0,28},{4,0},{8,4},{12,8},{16,12},{20,16},{24,20},{28,24},{32,60},... | collective-permute-start | bytes 1179656 | tf_op jit(solution)/shard_map/ppermute | solution.py:78
  51.5 4.3 %collective-permute-done.2.refs_4_ = bf16[2,4,64,384]{3,2,1,0:T(8,128)(2,1)S(1)} collective-permute-done((bf16[2,4,64,384]{3,2,1,0:T(8,128)(2,1)S(1)}, bf16[2,4,64,384]{3,2,1,0:T(8,128)(2,1)S(1)}, u32[]{:S(2)}, u32[]{:S(2)}) %collective-permute-start.2) | collective-permute-done | bytes 393248 | tf_op jit(solution)/shard_map/ppermute | solution.py:77
  55.8 3.2 %collective-permute-start.3 = (bf16[4,64,384]{2,1,0:T(8,128)(2,1)S(1)}, bf16[4,64,384]{2,1,0:T(8,128)(2,1)S(1)}, u32[]{:S(2)}, u32[]{:S(2)}) collective-permute-start(bf16[4,64,384]{2,1,0:T(8,128)(2,1)S(1)} %slice_bitcast_fusion.1), channel_id=1, source_target_pairs={{0,4},{4,8},{8,12},{12,16},{16,20},{20,24},{24,28},{28,0},{32,36},... | collective-permute-start | bytes 589832 | tf_op jit(solution)/shard_map/ppermute | solution.py:79
  59.1 0.0 collective-permute-done.6.refs_3_
  59.1 0.7 slice_bitcast_fusion
  59.8 4.2 %collective-permute-start.7 = (bf16[4,64,384]{2,1,0:T(8,128)(2,1)}, bf16[4,64,384]{2,1,0:T(8,128)(2,1)S(1)}, u32[]{:S(2)}, u32[]{:S(2)}) collective-permute-start(bf16[4,64,384]{2,1,0:T(8,128)(2,1)} %slice_bitcast_fusion), channel_id=1, source_target_pairs={{0,28},{4,0},{8,4},{12,8},{16,12},{20,16},{24,20},{28,24},{32,60},... | collective-permute-start | bytes 589832 | tf_op jit(solution)/shard_map/ppermute | solution.py:80
  64.0 0.0 copy-start.1
  64.0 1.5 %copy-done.1 = bf16[1,1,2,2048,224]{3,4,2,1,0:T(8,128)(2,1)S(1)} copy-done((bf16[1,1,2,2048,224]{3,4,2,1,0:T(8,128)(2,1)S(1)}, bf16[1,1,2,2048,224]{3,4,2,1,0:T(8,128)(2,1)}, u32[]{:S(2)}) %copy-start.1) | copy-done | bytes 1835032
  65.5 1.8 %shard_map.50 = (f32[2,224,384]{2,1,0:T(8,128)S(1)}, bf16[2,4,224,64]{3,2,1,0:T(8,128)(2,1)S(1)}, bf16[4,8,64,384]{3,2,1,0:T(8,128)(2,1)S(1)}) custom-call(s32[1]{0:T(128)} %bitcast.x_ref, bf16[2,4,64,384]{3,2,1,0:T(8,128)(2,1)S(1)} %bitcast.24, bf16[2,4,64,384]{3,2,1,0:T(8,128)(2,1)S(1)} %collective-permute-done.4.refs_1_, ...), custom_call_target="tpu_custom_call" | custom-call | flops 704643072 | bytes 4980736 | tf_op jit(solution)/shard_map/pallas_call | solution.py:89
  67.3 0.0 collective-permute-done.3.fwd_ref
  67.3 1.4 %collective-permute-done.7.rev_ref = bf16[4,64,384]{2,1,0:T(8,128)(2,1)S(1)} collective-permute-done((bf16[4,64,384]{2,1,0:T(8,128)(2,1)}, bf16[4,64,384]{2,1,0:T(8,128)(2,1)S(1)}, u32[]{:S(2)}, u32[]{:S(2)}) %collective-permute-start.7) | collective-permute-done | bytes 196640 | tf_op jit(solution)/shard_map/ppermute | solution.py:80
  68.7 0.7 shard_map.51
  69.4 10.5 %all_to_all.5 = bf16[4,2,96,224]{3,2,1,0:T(8,128)(2,1)S(1)} all-to-all(bf16[4,2,96,224]{3,2,1,0:T(8,128)(2,1)S(1)} %get-tuple-element.11), channel_id=1, replica_groups=mesh['pipe'=8,'seq'=32,'dp'=4] {'dp'}, dimensions={0} | all-to-all | bytes 688128 | tf_op jit(solution)/shard_map/all_to_all | solution.py:124
  80.0 0.1 convert_element_type.13
  80.0 0.1 slice_reduce_fusion
  80.1 16.1 %collective-permute-start.8 = (bf16[96,224]{1,0:T(8,128)(2,1)S(1)}, bf16[96,224]{1,0:T(8,128)(2,1)S(1)}, u32[]{:S(2)}, u32[]{:S(2)}) collective-permute-start(bf16[96,224]{1,0:T(8,128)(2,1)S(1)} %get-tuple-element.12), channel_id=1, source_target_pairs={{0,896},{128,768},{256,640},{384,512},{512,384},{640,256},{768,128... | collective-permute-start | bytes 129032 | tf_op jit(solution)/shard_map/ppermute | solution.py:126
  96.2 0.0 copy-done
  96.2 1.6 %fusion = bf16[1,1,2048,224]{2,3,1,0:T(8,128)(2,1)} fusion(bf16[2048,384]{1,0:T(8,128)(2,1)S(1)} %bitcast.20, bf16[1,224,384]{2,1,0:T(8,128)(2,1)S(1)} %copy-done), kind=kOutput, calls=%fused_computation.1 | convolution fusion | flops 352780288 | bytes 2662400 | tf_op jit(solution)/shard_map/dot_general | solution.py:130
  97.9 0.5 collective-permute-done.8
  98.4 0.7 multiply_bitcast_fusion
  (1 shorter events, 0.0 us)
Async XLA Ops:
  0.6 95.6 %copy-start = (bf16[1,224,384]{2,1,0:T(8,128)(2,1)S(1)}, bf16[1,224,384]{2,1,0:T(8,128)(2,1)}, u32[]{:S(2)}) copy-start(bf16[1,224,384]{2,1,0:T(8,128)(2,1)} %param.5) | copy-start | bytes 516100
  19.9 9.9 %collective-permute-start = (bf16[2,4,64,384]{3,2,1,0:T(8,128)(2,1)S(1)}, bf16[2,4,64,384]{3,2,1,0:T(8,128)(2,1)S(1)}, u32[]{:S(2)}, u32[]{:S(2)}) collective-permute-start(bf16[2,4,64,384]{3,2,1,0:T(8,128)(2,1)S(1)} %bitcast.22), channel_id=1, source_target_pairs={{0,4},{4,8},{8,12},{12,16},{16,20},{20,24},{24,28},{28,0},{32,36},... | collective-permute-start | bytes 1179656 | tf_op jit(solution)/shard_map/ppermute | solution.py:77
  24.5 10.9 %collective-permute-start.4 = (bf16[2,4,64,384]{3,2,1,0:T(8,128)(2,1)S(1)}, bf16[2,4,64,384]{3,2,1,0:T(8,128)(2,1)S(1)}, u32[]{:S(2)}, u32[]{:S(2)}) collective-permute-start(bf16[2,4,64,384]{3,2,1,0:T(8,128)(2,1)S(1)} %bitcast.23), channel_id=1, source_target_pairs={{0,28},{4,0},{8,4},{12,8},{16,12},{20,16},{24,20},{28,24},{32,60},... | collective-permute-start | bytes 1179656 | tf_op jit(solution)/shard_map/ppermute | solution.py:78
  29.8 11.3 %collective-permute-start.1 = (bf16[2,4,64,384]{3,2,1,0:T(8,128)(2,1)S(1)}, bf16[2,4,64,384]{3,2,1,0:T(8,128)(2,1)S(1)}, u32[]{:S(2)}, u32[]{:S(2)}) collective-permute-start(bf16[2,4,64,384]{3,2,1,0:T(8,128)(2,1)S(1)} %collective-permute-done.refs_6_), channel_id=1, source_target_pairs={{0,4},{4,8},{8,12},{12,16},{16,20},{20,24},{24,28},{28,0},{32,36},... | collective-permute-start | bytes 1179656 | tf_op jit(solution)/shard_map/ppermute | solution.py:77
  35.4 11.6 %collective-permute-start.5 = (bf16[2,4,64,384]{3,2,1,0:T(8,128)(2,1)S(1)}, bf16[2,4,64,384]{3,2,1,0:T(8,128)(2,1)S(1)}, u32[]{:S(2)}, u32[]{:S(2)}) collective-permute-start(bf16[2,4,64,384]{3,2,1,0:T(8,128)(2,1)S(1)} %collective-permute-done.4.refs_1_), channel_id=1, source_target_pairs={{0,28},{4,0},{8,4},{12,8},{16,12},{20,16},{24,20},{28,24},{32,60},... | collective-permute-start | bytes 1179656 | tf_op jit(solution)/shard_map/ppermute | solution.py:78
  41.1 14.7 %collective-permute-start.2 = (bf16[2,4,64,384]{3,2,1,0:T(8,128)(2,1)S(1)}, bf16[2,4,64,384]{3,2,1,0:T(8,128)(2,1)S(1)}, u32[]{:S(2)}, u32[]{:S(2)}) collective-permute-start(bf16[2,4,64,384]{3,2,1,0:T(8,128)(2,1)S(1)} %collective-permute-done.1.refs_5_), channel_id=1, source_target_pairs={{0,4},{4,8},{8,12},{12,16},{16,20},{20,24},{24,28},{28,0},{32,36},... | collective-permute-start | bytes 1179656 | tf_op jit(solution)/shard_map/ppermute | solution.py:77
  47.0 12.1 %collective-permute-start.6 = (bf16[2,4,64,384]{3,2,1,0:T(8,128)(2,1)S(1)}, bf16[2,4,64,384]{3,2,1,0:T(8,128)(2,1)S(1)}, u32[]{:S(2)}, u32[]{:S(2)}) collective-permute-start(bf16[2,4,64,384]{3,2,1,0:T(8,128)(2,1)S(1)} %collective-permute-done.5.refs_2_), channel_id=1, source_target_pairs={{0,28},{4,0},{8,4},{12,8},{16,12},{20,16},{24,20},{28,24},{32,60},... | collective-permute-start | bytes 1179656 | tf_op jit(solution)/shard_map/ppermute | solution.py:78
  55.8 11.5 %collective-permute-start.3 = (bf16[4,64,384]{2,1,0:T(8,128)(2,1)S(1)}, bf16[4,64,384]{2,1,0:T(8,128)(2,1)S(1)}, u32[]{:S(2)}, u32[]{:S(2)}) collective-permute-start(bf16[4,64,384]{2,1,0:T(8,128)(2,1)S(1)} %slice_bitcast_fusion.1), channel_id=1, source_target_pairs={{0,4},{4,8},{8,12},{12,16},{16,20},{20,24},{24,28},{28,0},{32,36},... | collective-permute-start | bytes 589832 | tf_op jit(solution)/shard_map/ppermute | solution.py:79
  59.8 9.0 %collective-permute-start.7 = (bf16[4,64,384]{2,1,0:T(8,128)(2,1)}, bf16[4,64,384]{2,1,0:T(8,128)(2,1)S(1)}, u32[]{:S(2)}, u32[]{:S(2)}) collective-permute-start(bf16[4,64,384]{2,1,0:T(8,128)(2,1)} %slice_bitcast_fusion), channel_id=1, source_target_pairs={{0,28},{4,0},{8,4},{12,8},{16,12},{20,16},{24,20},{28,24},{32,60},... | collective-permute-start | bytes 589832 | tf_op jit(solution)/shard_map/ppermute | solution.py:80
  64.0 1.5 %copy-start.1 = (bf16[1,1,2,2048,224]{3,4,2,1,0:T(8,128)(2,1)S(1)}, bf16[1,1,2,2048,224]{3,4,2,1,0:T(8,128)(2,1)}, u32[]{:S(2)}) copy-start(bf16[1,1,2,2048,224]{3,4,2,1,0:T(8,128)(2,1)} %param.3) | copy-start | bytes 5505028
  80.1 18.3 %collective-permute-start.8 = (bf16[96,224]{1,0:T(8,128)(2,1)S(1)}, bf16[96,224]{1,0:T(8,128)(2,1)S(1)}, u32[]{:S(2)}, u32[]{:S(2)}) collective-permute-start(bf16[96,224]{1,0:T(8,128)(2,1)S(1)} %get-tuple-element.12), channel_id=1, source_target_pairs={{0,896},{128,768},{256,640},{384,512},{512,384},{640,256},{768,128... | collective-permute-start | bytes 129032 | tf_op jit(solution)/shard_map/ppermute | solution.py:126

commit v5 on v4

v5 whole, which is shorter than its diff:
```python
import jax
import jax.numpy as jnp
from jax import lax
from jax.experimental import pallas as pl
from jax.experimental.pallas import tpu as pltpu
from jax.sharding import PartitionSpec as P

X_CHIPS = 8
VMEM_BYTES = 40 * 2**20


ROWS_BY_ROWS = (((1,), (1,)), ((), ()))


def early_kernel(here_ref, *refs):
    blocks, refs = refs[:-7], refs[-7:]
    saved_ref, weight_ref, partial_ref, picked_ref, grad_ref, latent_ref, rev_ref = refs
    ny, nx, piece, channels = latent_ref.shape
    far = nx // 2
    far_place = lax.rem(here_ref[0] + far, nx)
    row = lax.broadcasted_iota(jnp.int32, (nx * piece, piece), 0)
    column = lax.broadcasted_iota(jnp.int32, (nx * piece, piece), 1)
    pick = jnp.where(row == column + far_place * piece, 1.0, 0.0).astype(saved_ref.dtype)
    for direction, target in enumerate((latent_ref, rev_ref)):
        for k, block in enumerate(blocks):
            place = lax.rem(here_ref[0] + (k if k < far else k + 1), nx)
            for y in range(ny):
                target[y, place] = block[direction, y]
        for y in range(ny):
            target[y, far_place] = jnp.zeros((piece, channels), target.dtype)
            part = saved_ref[direction, :, y * nx * piece : (y + 1) * nx * piece]
            picked = jnp.dot(part, pick, preferred_element_type=jnp.float32)
            picked_ref[direction, y] = picked.astype(picked_ref.dtype)
        latent = target[...].reshape(-1, channels)
        partial_ref[direction] = jnp.dot(
            saved_ref[direction], latent, preferred_element_type=jnp.float32
        )
        if direction == 0:
            grad = lax.dot_general(
                weight_ref[...], latent, ROWS_BY_ROWS, preferred_element_type=jnp.float32
            )
            grad_ref[...] = grad.astype(grad_ref.dtype)


def late_kernel(here_ref, fwd_ref, rev_ref, *refs):
    weight_ref, partial_ref, picked_ref, early_ref, shares_ref, grad_ref = refs
    _, dp, share, _ = shares_ref.shape
    ny, piece, channels = fwd_ref.shape
    run = early_ref.shape[1] // ny
    nx = run // piece
    far_place = lax.rem(here_ref[0] + nx // 2, nx)
    for direction, far_ref in enumerate((fwd_ref, rev_ref)):
        total = partial_ref[direction]
        for y in range(ny):
            total += jnp.dot(
                picked_ref[direction, y], far_ref[y], preferred_element_type=jnp.float32
            )
        turned = total.T.astype(shares_ref.dtype)
        slot = lax.rem(here_ref[1] + direction, 2)
        for part in range(dp):
            shares_ref[slot, part] = turned[part * share : (part + 1) * share]
    row = lax.broadcasted_iota(jnp.int32, (piece, run), 0)
    column = lax.broadcasted_iota(jnp.int32, (piece, run), 1)
    put = jnp.where(column == row + far_place * piece, 1.0, 0.0).astype(grad_ref.dtype)
    for y in range(ny):
        grad = lax.dot_general(
            weight_ref[...], fwd_ref[y], ROWS_BY_ROWS, preferred_element_type=jnp.float32
        )
        spread = jnp.dot(grad.astype(grad_ref.dtype), put, preferred_element_type=jnp.float32)
        lanes = slice(y * run, (y + 1) * run)
        grad_ref[:, lanes] = early_ref[:, lanes] + spread.astype(grad_ref.dtype)


def local(inputs_saved, grad_latent, weights):
    seq = lax.axis_size("seq")
    pipe = lax.axis_size("pipe")
    dp = lax.axis_size("dp")
    nx = X_CHIPS
    ny = seq // nx
    columns = [[y * nx + x for y in range(ny)] for x in range(nx)]

    def along_x(step):
        return [(y * nx + x, y * nx + (x + step) % nx) for y in range(ny) for x in range(nx)]

    right, left = along_x(1), along_x(-1)
    tokens = inputs_saved.shape[3]
    width = inputs_saved.shape[4]
    channels = grad_latent.shape[-1]
    piece = grad_latent.shape[3]

    both = lax.all_gather(grad_latent[0, 0][:, None], "seq", axis=1, tiled=True, axis_index_groups=columns)
    own = both
    from_left, from_right = [own], [own]
    for _ in range(nx // 2 - 1):
        from_left.append(lax.ppermute(from_left[-1], "seq", right))
        from_right.append(lax.ppermute(from_right[-1], "seq", left))
    far_fwd = lax.ppermute(from_left[-1][0], "seq", right)
    far_rev = lax.ppermute(from_right[-1][1], "seq", left)
    blocks = from_right + from_left[:0:-1]
    here = jnp.stack(
        [lax.rem(lax.axis_index("seq"), nx), lax.div(lax.axis_index("pipe"), pipe // 2)]
    )
    saved = jnp.swapaxes(inputs_saved[0, 0], 1, 2)
    vmem = pl.BlockSpec(memory_space=pltpu.VMEM)
    smem = pl.BlockSpec(memory_space=pltpu.SMEM)
    held = pltpu.VMEM((ny, nx, piece, channels), own.dtype)
    grad_shape = jax.ShapeDtypeStruct((width, tokens), own.dtype)
    settings = pltpu.CompilerParams(vmem_limit_bytes=VMEM_BYTES)
    partial, picked, grad = pl.pallas_call(
        early_kernel,
        out_shape=(
            jax.ShapeDtypeStruct((2, width, channels), jnp.float32),
            jax.ShapeDtypeStruct((2, ny, width, piece), saved.dtype),
            grad_shape,
        ),
        in_specs=[smem] + [vmem] * (len(blocks) + 2),
        out_specs=(vmem, vmem, vmem),
        scratch_shapes=[held, held],
        compiler_params=settings,
        cost_estimate=pl.CostEstimate(
            flops=6 * tokens * channels * width,
            bytes_accessed=4 * tokens * (width + channels),
            transcendentals=0,
        ),
    )(here, *blocks, saved, weights[0])
    shares, grad = pl.pallas_call(
        late_kernel,
        out_shape=(
            jax.ShapeDtypeStruct((2, dp, channels // dp, width), jnp.bfloat16),
            grad_shape,
        ),
        in_specs=[smem] + [vmem] * 6,
        out_specs=(vmem, vmem),
        compiler_params=settings,
        cost_estimate=pl.CostEstimate(
            flops=6 * ny * piece * channels * width,
            bytes_accessed=12 * channels * width,
            transcendentals=0,
        ),
    )(here, far_fwd, far_rev, weights[0], partial, picked, grad)

    ends = [[p * dp + d for p in (i, pipe - 1 - i) for d in range(dp)] for i in range(pipe // 2)]
    shares = lax.all_to_all(
        shares.reshape(2 * dp, channels // dp, width),
        ("pipe", "dp"),
        0,
        0,
        tiled=True,
        axis_index_groups=ends,
    )
    weight_grad = jnp.sum(shares.astype(jnp.float32), axis=0) * (1.0 / tokens)
    return grad.T[None, None], weight_grad.T[None]


def solution(mesh):
    in_specs = (
        P("pipe", "dp", None, None, "seq"),
        P("pipe", "dp", None, "seq", None),
        P("pipe", "seq", None),
    )
    out_specs = (P("pipe", "dp", None, "seq"), P("pipe", "seq", "dp"))
    return jax.shard_map(local, mesh=mesh, in_specs=in_specs, out_specs=out_specs, check_vma=False)
```

time: 99.5 us -> 101 us (1.015)
  the two profiles are of different devices: /device:TPU:6 before, /device:TPU:1 now
where the time goes in v5:
time: 101 us; the launch traced here: 100 us
  blocking collectives  53 us (52%)
  starting transfers between devices  25.9 us (26%)
  waiting for transfers between devices  11.9 us (12%)
  Pallas kernels  5.68 us (6%)
  local copies, waits for them, and re-layouts  2.46 us (2%)
    all_to_all x1, blocking collectives, local(): lax.all_to_all(shares.reshape(2 * dp, channels // dp, width), ('pipe', 'd...  36.4 us
    all_gather x1, blocking collectives, local(): lax.all_gather(grad_latent[0, 0][:, None], 'seq', axis=1, tiled=True, axi...  16.6 us
    ppermute x3, starting transfers between devices, local(): from_right.append(lax.ppermute(from_right[-1], 'seq', left))  12.9 us
    ppermute x3, waiting for transfers between devices, local(): from_left.append(lax.ppermute(from_left[-1], 'seq', right))  11.9 us
    ppermute x3, starting transfers between devices, local(): from_left.append(lax.ppermute(from_left[-1], 'seq', right))  6.56 us
    ppermute x1, starting transfers between devices, local(): far_rev = lax.ppermute(from_right[-1][1], 'seq', left)  4.57 us
    pallas_call x1, Pallas kernels, local(): pl.pallas_call(early_kernel, out_shape=(jax.ShapeDtypeStruct((2, width, c...  2.93 us
    pallas_call x1, Pallas kernels, local(): pl.pallas_call(late_kernel, out_shape=(jax.ShapeDtypeStruct((2, dp, chann...  2.74 us
  transfers between devices with their start and end apart: 8, of which 3 were waited for; matrix products, arithmetic and copies ran while one was open for 0% of the time, Pallas kernels for 3%

profile of v5, /device:TPU:1, one launch (start us, length us, event | category | flops | bytes accessed | tf_op | source)
XLA Modules:
  0.0 100.5 jit_solution(387960476697087679)
XLA Ops:
  0.6 16.6 %all-gather = bf16[1,1,2,256,384]{4,3,2,1,0:T(8,128)(2,1)S(1)} all-gather(bf16[1,1,2,64,384]{4,3,2,1,0:T(8,128)(2,1)} %param.4), channel_id=2, replica_groups={{0,32,64,96},{4,36,68,100},{8,40,72,104},{12,44,76,108},{16,48,80,112},..., dimensions={3}, use_global_device_ids=true | all-gather | bytes 491520 | tf_op jit(solution)/shard_map/all_gather | solution.py:91
  17.2 2.7 %collective-permute-start = (bf16[2,4,64,384]{3,2,1,0:T(8,128)(2,1)S(1)}, bf16[2,4,64,384]{3,2,1,0:T(8,128)(2,1)S(1)}, u32[]{:S(2)}, u32[]{:S(2)}) collective-permute-start(bf16[2,4,64,384]{3,2,1,0:T(8,128)(2,1)S(1)} %bitcast.20), channel_id=1, source_target_pairs={{0,4},{4,8},{8,12},{12,16},{16,20},{20,24},{24,28},{28,0},{32,36},... | collective-permute-start | bytes 1179656 | tf_op jit(solution)/shard_map/ppermute | solution.py:95
  19.9 3.7 %collective-permute-start.4 = (bf16[2,4,64,384]{3,2,1,0:T(8,128)(2,1)S(1)}, bf16[2,4,64,384]{3,2,1,0:T(8,128)(2,1)S(1)}, u32[]{:S(2)}, u32[]{:S(2)}) collective-permute-start(bf16[2,4,64,384]{3,2,1,0:T(8,128)(2,1)S(1)} %bitcast.21), channel_id=1, source_target_pairs={{0,28},{4,0},{8,4},{12,8},{16,12},{20,16},{24,20},{28,24},{32,60},... | collective-permute-start | bytes 1179656 | tf_op jit(solution)/shard_map/ppermute | solution.py:96
  23.7 3.2 %collective-permute-done.refs_6_ = bf16[2,4,64,384]{3,2,1,0:T(8,128)(2,1)S(1)} collective-permute-done((bf16[2,4,64,384]{3,2,1,0:T(8,128)(2,1)S(1)}, bf16[2,4,64,384]{3,2,1,0:T(8,128)(2,1)S(1)}, u32[]{:S(2)}, u32[]{:S(2)}) %collective-permute-start) | collective-permute-done | bytes 393248 | tf_op jit(solution)/shard_map/ppermute | solution.py:95
  26.9 1.9 %collective-permute-start.1 = (bf16[2,4,64,384]{3,2,1,0:T(8,128)(2,1)S(1)}, bf16[2,4,64,384]{3,2,1,0:T(8,128)(2,1)S(1)}, u32[]{:S(2)}, u32[]{:S(2)}) collective-permute-start(bf16[2,4,64,384]{3,2,1,0:T(8,128)(2,1)S(1)} %collective-permute-done.refs_6_), channel_id=1, source_target_pairs={{0,4},{4,8},{8,12},{12,16},{16,20},{20,24},{24,28},{28,0},{32,36},... | collective-permute-start | bytes 1179656 | tf_op jit(solution)/shard_map/ppermute | solution.py:95
  28.8 0.0 collective-permute-done.4.refs_1_
  28.8 4.6 %collective-permute-start.5 = (bf16[2,4,64,384]{3,2,1,0:T(8,128)(2,1)S(1)}, bf16[2,4,64,384]{3,2,1,0:T(8,128)(2,1)S(1)}, u32[]{:S(2)}, u32[]{:S(2)}) collective-permute-start(bf16[2,4,64,384]{3,2,1,0:T(8,128)(2,1)S(1)} %collective-permute-done.4.refs_1_), channel_id=1, source_target_pairs={{0,28},{4,0},{8,4},{12,8},{16,12},{20,16},{24,20},{28,24},{32,60},... | collective-permute-start | bytes 1179656 | tf_op jit(solution)/shard_map/ppermute | solution.py:96
  33.4 4.8 %collective-permute-done.1.refs_5_ = bf16[2,4,64,384]{3,2,1,0:T(8,128)(2,1)S(1)} collective-permute-done((bf16[2,4,64,384]{3,2,1,0:T(8,128)(2,1)S(1)}, bf16[2,4,64,384]{3,2,1,0:T(8,128)(2,1)S(1)}, u32[]{:S(2)}, u32[]{:S(2)}) %collective-permute-start.1) | collective-permute-done | bytes 393248 | tf_op jit(solution)/shard_map/ppermute | solution.py:95
  38.2 1.9 %collective-permute-start.2 = (bf16[2,4,64,384]{3,2,1,0:T(8,128)(2,1)S(1)}, bf16[2,4,64,384]{3,2,1,0:T(8,128)(2,1)S(1)}, u32[]{:S(2)}, u32[]{:S(2)}) collective-permute-start(bf16[2,4,64,384]{3,2,1,0:T(8,128)(2,1)S(1)} %collective-permute-done.1.refs_5_), channel_id=1, source_target_pairs={{0,4},{4,8},{8,12},{12,16},{16,20},{20,24},{24,28},{28,0},{32,36},... | collective-permute-start | bytes 1179656 | tf_op jit(solution)/shard_map/ppermute | solution.py:95
  40.1 0.0 collective-permute-done.5.refs_2_
  40.1 4.6 %collective-permute-start.6 = (bf16[2,4,64,384]{3,2,1,0:T(8,128)(2,1)S(1)}, bf16[2,4,64,384]{3,2,1,0:T(8,128)(2,1)S(1)}, u32[]{:S(2)}, u32[]{:S(2)}) collective-permute-start(bf16[2,4,64,384]{3,2,1,0:T(8,128)(2,1)S(1)} %collective-permute-done.5.refs_2_), channel_id=1, source_target_pairs={{0,28},{4,0},{8,4},{12,8},{16,12},{20,16},{24,20},{28,24},{32,60},... | collective-permute-start | bytes 1179656 | tf_op jit(solution)/shard_map/ppermute | solution.py:96
  44.7 3.9 %collective-permute-done.2.refs_4_ = bf16[2,4,64,384]{3,2,1,0:T(8,128)(2,1)S(1)} collective-permute-done((bf16[2,4,64,384]{3,2,1,0:T(8,128)(2,1)S(1)}, bf16[2,4,64,384]{3,2,1,0:T(8,128)(2,1)S(1)}, u32[]{:S(2)}, u32[]{:S(2)}) %collective-permute-start.2) | collective-permute-done | bytes 393248 | tf_op jit(solution)/shard_map/ppermute | solution.py:95
  48.6 1.9 %collective-permute-start.3 = (bf16[4,64,384]{2,1,0:T(8,128)(2,1)S(1)}, bf16[4,64,384]{2,1,0:T(8,128)(2,1)S(1)}, u32[]{:S(2)}, u32[]{:S(2)}) collective-permute-start(bf16[4,64,384]{2,1,0:T(8,128)(2,1)S(1)} %slice_bitcast_fusion.1), channel_id=1, source_target_pairs={{0,4},{4,8},{8,12},{12,16},{16,20},{20,24},{24,28},{28,0},{32,36},... | collective-permute-start | bytes 589832 | tf_op jit(solution)/shard_map/ppermute | solution.py:97
  50.5 0.0 collective-permute-done.6.refs_3_
  50.6 4.6 %collective-permute-start.7 = (bf16[4,64,384]{2,1,0:T(8,128)(2,1)S(1)}, bf16[4,64,384]{2,1,0:T(8,128)(2,1)S(1)}, u32[]{:S(2)}, u32[]{:S(2)}) collective-permute-start(bf16[4,64,384]{2,1,0:T(8,128)(2,1)S(1)} %slice_bitcast_fusion), channel_id=1, source_target_pairs={{0,28},{4,0},{8,4},{12,8},{16,12},{20,16},{24,20},{28,24},{32,60},... | collective-permute-start | bytes 589832 | tf_op jit(solution)/shard_map/ppermute | solution.py:98
  55.1 0.1 pad_add_fusion.here_ref
  55.2 0.0 copy-start
  55.2 1.5 %copy-done = bf16[1,1,2,2048,224]{3,4,2,1,0:T(8,128)(2,1)S(1)} copy-done((bf16[1,1,2,2048,224]{3,4,2,1,0:T(8,128)(2,1)S(1)}, bf16[1,1,2,2048,224]{3,4,2,1,0:T(8,128)(2,1)}, u32[]{:S(2)}) %copy-start) | copy-done | bytes 1835032
  56.7 0.0 copy-start.1
  56.7 0.9 copy-done.1
  57.6 2.9 %shard_map.50 = (f32[2,224,384]{2,1,0:T(8,128)S(1)}, bf16[2,4,224,64]{3,2,1,0:T(8,128)(2,1)S(1)}, bf16[224,2048]{1,0:T(8,128)(2,1)S(1)}) custom-call(s32[2]{0:T(128)S(1)} %pad_add_fusion.here_ref, bf16[2,4,64,384]{3,2,1,0:T(8,128)(2,1)S(1)} %bitcast.22, bf16[2,4,64,384]{3,2,1,0:T(8,128)(2,1)S(1)} %collective-permute-done.4.refs_1_, ...), custom_call_target="tpu_custom_call" | custom-call | flops 1056964608 | bytes 4980736 | tf_op jit(solution)/shard_map/pallas_call | solution.py:109
  60.6 0.0 collective-permute-done.3.fwd_ref
  60.6 0.0 collective-permute-done.7.rev_ref
  60.6 2.7 %shard_map.51 = (bf16[2,4,96,224]{3,2,1,0:T(8,128)(2,1)S(1)}, bf16[224,2048]{1,0:T(8,128)(2,1)}) custom-call(s32[2]{0:T(128)S(1)} %pad_add_fusion.here_ref, bf16[4,64,384]{2,1,0:T(8,128)(2,1)S(1)} %collective-permute-done.3.fwd_ref, bf16[4,64,384]{2,1,0:T(8,128)(2,1)S(1)} %collective-permute-done.7.rev_ref, bf16[224,384]{1,0:T(8,128)(2,1)S(1)} %bitcast.24, ...), custom_call_target="tpu_custom_call" | custom-call | flops 132120576 | bytes 1032192 | tf_op jit(solution)/shard_map/pallas_call | solution.py:126
  63.3 36.4 %all_to_all.5 = bf16[8,96,224]{2,1,0:T(8,128)(2,1)S(1)} all-to-all(bf16[8,96,224]{2,1,0:T(8,128)(2,1)S(1)} %bitcast.25), channel_id=1, replica_groups={{0,1,2,3,896,897,898,899},{128,129,130,131,768,769,770,771},{256,257,25..., dimensions={0} | all-to-all | bytes 688128 | tf_op jit(solution)/shard_map/all_to_all | solution.py:143
  99.8 0.1 convert_reduce_fusion
  99.8 0.6 multiply_bitcast_fusion
  (2 shorter events, 0.0 us)
Async XLA Ops:
  17.2 9.7 %collective-permute-start = (bf16[2,4,64,384]{3,2,1,0:T(8,128)(2,1)S(1)}, bf16[2,4,64,384]{3,2,1,0:T(8,128)(2,1)S(1)}, u32[]{:S(2)}, u32[]{:S(2)}) collective-permute-start(bf16[2,4,64,384]{3,2,1,0:T(8,128)(2,1)S(1)} %bitcast.20), channel_id=1, source_target_pairs={{0,4},{4,8},{8,12},{12,16},{16,20},{20,24},{24,28},{28,0},{32,36},... | collective-permute-start | bytes 1179656 | tf_op jit(solution)/shard_map/ppermute | solution.py:95
  19.9 8.9 %collective-permute-start.4 = (bf16[2,4,64,384]{3,2,1,0:T(8,128)(2,1)S(1)}, bf16[2,4,64,384]{3,2,1,0:T(8,128)(2,1)S(1)}, u32[]{:S(2)}, u32[]{:S(2)}) collective-permute-start(bf16[2,4,64,384]{3,2,1,0:T(8,128)(2,1)S(1)} %bitcast.21), channel_id=1, source_target_pairs={{0,28},{4,0},{8,4},{12,8},{16,12},{20,16},{24,20},{28,24},{32,60},... | collective-permute-start | bytes 1179656 | tf_op jit(solution)/shard_map/ppermute | solution.py:96
  26.9 11.3 %collective-permute-start.1 = (bf16[2,4,64,384]{3,2,1,0:T(8,128)(2,1)S(1)}, bf16[2,4,64,384]{3,2,1,0:T(8,128)(2,1)S(1)}, u32[]{:S(2)}, u32[]{:S(2)}) collective-permute-start(bf16[2,4,64,384]{3,2,1,0:T(8,128)(2,1)S(1)} %collective-permute-done.refs_6_), channel_id=1, source_target_pairs={{0,4},{4,8},{8,12},{12,16},{16,20},{20,24},{24,28},{28,0},{32,36},... | collective-permute-start | bytes 1179656 | tf_op jit(solution)/shard_map/ppermute | solution.py:95
  28.8 11.3 %collective-permute-start.5 = (bf16[2,4,64,384]{3,2,1,0:T(8,128)(2,1)S(1)}, bf16[2,4,64,384]{3,2,1,0:T(8,128)(2,1)S(1)}, u32[]{:S(2)}, u32[]{:S(2)}) collective-permute-start(bf16[2,4,64,384]{3,2,1,0:T(8,128)(2,1)S(1)} %collective-permute-done.4.refs_1_), channel_id=1, source_target_pairs={{0,28},{4,0},{8,4},{12,8},{16,12},{20,16},{24,20},{28,24},{32,60},... | collective-permute-start | bytes 1179656 | tf_op jit(solution)/shard_map/ppermute | solution.py:96
  38.2 10.4 %collective-permute-start.2 = (bf16[2,4,64,384]{3,2,1,0:T(8,128)(2,1)S(1)}, bf16[2,4,64,384]{3,2,1,0:T(8,128)(2,1)S(1)}, u32[]{:S(2)}, u32[]{:S(2)}) collective-permute-start(bf16[2,4,64,384]{3,2,1,0:T(8,128)(2,1)S(1)} %collective-permute-done.1.refs_5_), channel_id=1, source_target_pairs={{0,4},{4,8},{8,12},{12,16},{16,20},{20,24},{24,28},{28,0},{32,36},... | collective-permute-start | bytes 1179656 | tf_op jit(solution)/shard_map/ppermute | solution.py:95
  40.1 10.4 %collective-permute-start.6 = (bf16[2,4,64,384]{3,2,1,0:T(8,128)(2,1)S(1)}, bf16[2,4,64,384]{3,2,1,0:T(8,128)(2,1)S(1)}, u32[]{:S(2)}, u32[]{:S(2)}) collective-permute-start(bf16[2,4,64,384]{3,2,1,0:T(8,128)(2,1)S(1)} %collective-permute-done.5.refs_2_), channel_id=1, source_target_pairs={{0,28},{4,0},{8,4},{12,8},{16,12},{20,16},{24,20},{28,24},{32,60},... | collective-permute-start | bytes 1179656 | tf_op jit(solution)/shard_map/ppermute | solution.py:96
  48.6 12.0 %collective-permute-start.3 = (bf16[4,64,384]{2,1,0:T(8,128)(2,1)S(1)}, bf16[4,64,384]{2,1,0:T(8,128)(2,1)S(1)}, u32[]{:S(2)}, u32[]{:S(2)}) collective-permute-start(bf16[4,64,384]{2,1,0:T(8,128)(2,1)S(1)} %slice_bitcast_fusion.1), channel_id=1, source_target_pairs={{0,4},{4,8},{8,12},{12,16},{16,20},{20,24},{24,28},{28,0},{32,36},... | collective-permute-start | bytes 589832 | tf_op jit(solution)/shard_map/ppermute | solution.py:97
  50.6 10.0 %collective-permute-start.7 = (bf16[4,64,384]{2,1,0:T(8,128)(2,1)S(1)}, bf16[4,64,384]{2,1,0:T(8,128)(2,1)S(1)}, u32[]{:S(2)}, u32[]{:S(2)}) collective-permute-start(bf16[4,64,384]{2,1,0:T(8,128)(2,1)S(1)} %slice_bitcast_fusion), channel_id=1, source_target_pairs={{0,28},{4,0},{8,4},{12,8},{16,12},{20,16},{24,20},{28,24},{32,60},... | collective-permute-start | bytes 589832 | tf_op jit(solution)/shard_map/ppermute | solution.py:98
  55.2 1.5 %copy-start = (bf16[1,1,2,2048,224]{3,4,2,1,0:T(8,128)(2,1)S(1)}, bf16[1,1,2,2048,224]{3,4,2,1,0:T(8,128)(2,1)}, u32[]{:S(2)}) copy-start(bf16[1,1,2,2048,224]{3,4,2,1,0:T(8,128)(2,1)} %param.3) | copy-start | bytes 5505028
  56.7 0.9 copy-start.1

commit v6 on v1

v6 whole, which is shorter than its diff:
```python
import jax
import jax.numpy as jnp
from jax import lax
from jax.experimental import pallas as pl
from jax.experimental.pallas import tpu as pltpu
from jax.sharding import PartitionSpec as P

X_CHIPS = 8
VMEM_BYTES = 40 * 2**20


def near_steps(nx):
    far = nx // 2
    return list(range(far - 1)) + [nx - k for k in range(1, far - 1)]


def late_steps(nx):
    return nx // 2 - 1, nx // 2 + 1, nx // 2


def early_kernel(here_ref, *refs):
    blocks, (saved_ref, partial_ref, picked_ref, latent_ref) = refs[:-4], refs[-4:]
    ny, nx, piece, channels = latent_ref.shape
    run = nx * piece
    row = lax.broadcasted_iota(jnp.int32, (run, piece), 0)
    column = lax.broadcasted_iota(jnp.int32, (run, piece), 1)
    nothing = jnp.zeros((piece, channels), latent_ref.dtype)
    for direction in range(2):
        for step, block in zip(near_steps(nx), blocks):
            place = lax.rem(here_ref[0] + step, nx)
            for y in range(ny):
                latent_ref[y, place] = block[direction, y]
        for j, step in enumerate(late_steps(nx)):
            place = lax.rem(here_ref[0] + step, nx)
            pick = jnp.where(row == column + place * piece, 1.0, 0.0).astype(saved_ref.dtype)
            for y in range(ny):
                latent_ref[y, place] = nothing
                part = saved_ref[direction, :, y * run : (y + 1) * run]
                picked = jnp.dot(part, pick, preferred_element_type=jnp.float32)
                picked_ref[direction, j, y] = picked.astype(picked_ref.dtype)
        partial_ref[direction] = jnp.dot(
            saved_ref[direction],
            latent_ref[...].reshape(-1, channels),
            preferred_element_type=jnp.float32,
        )


def put_shares(total, shares, slot):
    dp, share, _ = shares.shape[1:]
    turned = total.T.astype(shares.dtype)
    for part in range(dp):
        shares[slot, part] = turned[part * share : (part + 1) * share]


def middle_kernel(here_ref, *refs):
    blocks, refs = refs[:-8], refs[-8:]
    far_ref, weight_ref, partial_ref, picked_ref, fwd_ref, rev_ref, grad_ref, latent_ref = refs
    ny, nx, _, channels = latent_ref.shape
    late = blocks[-2:]
    for step, block in zip(near_steps(nx) + list(late_steps(nx)[:2]), blocks):
        place = lax.rem(here_ref[0] + step, nx)
        for y in range(ny):
            latent_ref[y, place] = block[0, y]
    place = lax.rem(here_ref[0] + late_steps(nx)[2], nx)
    for y in range(ny):
        latent_ref[y, place] = far_ref[y]
    grad = lax.dot_general(
        weight_ref[...],
        latent_ref[...].reshape(-1, channels),
        (((1,), (1,)), ((), ())),
        preferred_element_type=jnp.float32,
    )
    grad_ref[...] = grad.astype(grad_ref.dtype)
    for direction in range(2):
        total = partial_ref[direction]
        for y in range(ny):
            for j, block in enumerate(late):
                total += jnp.dot(
                    picked_ref[direction, j, y],
                    block[direction, y],
                    preferred_element_type=jnp.float32,
                )
            if direction == 0:
                total += jnp.dot(
                    picked_ref[0, 2, y], far_ref[y], preferred_element_type=jnp.float32
                )
        if direction == 0:
            put_shares(total, fwd_ref, 0)
        else:
            rev_ref[...] = total


def late_kernel(here_ref, far_ref, rev_ref, picked_ref, fwd_ref, shares_ref):
    total = rev_ref[...]
    for y in range(far_ref.shape[0]):
        total += jnp.dot(picked_ref[1, 2, y], far_ref[y], preferred_element_type=jnp.float32)
    put_shares(total, shares_ref, 1 - here_ref[1])
    shares_ref[here_ref[1]] = fwd_ref[0]


def local(inputs_saved, grad_latent, weights):
    seq = lax.axis_size("seq")
    pipe = lax.axis_size("pipe")
    dp = lax.axis_size("dp")
    nx = X_CHIPS
    ny = seq // nx
    columns = [[y * nx + x for y in range(ny)] for x in range(nx)]

    def along_x(step):
        return [(y * nx + x, y * nx + (x + step) % nx) for y in range(ny) for x in range(nx)]

    right, left = along_x(1), along_x(-1)
    tokens = inputs_saved.shape[3]
    width = inputs_saved.shape[4]
    channels = grad_latent.shape[-1]
    piece = grad_latent.shape[3]

    both = lax.all_gather(grad_latent[0, 0][:, None], "seq", axis=1, tiled=True, axis_index_groups=columns)
    own = both
    from_left, from_right = [own], [own]
    for _ in range(nx // 2 - 1):
        from_left.append(lax.ppermute(from_left[-1], "seq", right))
        from_right.append(lax.ppermute(from_right[-1], "seq", left))
    far = nx // 2
    near = from_right[: far - 1] + from_left[1 : far - 1]
    here = jnp.stack(
        [lax.rem(lax.axis_index("seq"), nx), lax.div(lax.axis_index("pipe"), pipe // 2)]
    )
    saved = jnp.swapaxes(inputs_saved[0, 0], 1, 2)
    vmem = pl.BlockSpec(memory_space=pltpu.VMEM)
    smem = pl.BlockSpec(memory_space=pltpu.SMEM)
    held = pltpu.VMEM((ny, nx, piece, channels), own.dtype)
    settings = pltpu.CompilerParams(vmem_limit_bytes=VMEM_BYTES)

    def kernel_call(body, out_shape, scratch, flops, *operands):
        return pl.pallas_call(
            body,
            out_shape=out_shape,
            in_specs=[smem] + [vmem] * len(operands),
            out_specs=(vmem,) * len(out_shape),
            scratch_shapes=scratch,
            compiler_params=settings,
            cost_estimate=pl.CostEstimate(
                flops=flops, bytes_accessed=4 * tokens * channels, transcendentals=0
            ),
        )(here, *operands)

    product = 2 * tokens * channels * width
    partial, picked = kernel_call(
        early_kernel,
        (
            jax.ShapeDtypeStruct((2, width, channels), jnp.float32),
            jax.ShapeDtypeStruct((2, 3, ny, width, piece), saved.dtype),
        ),
        [held],
        2 * product,
        *near,
        saved,
    )
    last_left, partial = lax.optimization_barrier((from_left[-1], partial))
    far_fwd = lax.ppermute(last_left[0], "seq", right)
    far_rev = lax.ppermute(from_right[-1][1], "seq", left)
    share_shape = (dp, channels // dp, width)
    shares_fwd, total_rev, grad = kernel_call(
        middle_kernel,
        (
            jax.ShapeDtypeStruct((1,) + share_shape, jnp.bfloat16),
            jax.ShapeDtypeStruct((width, channels), jnp.float32),
            jax.ShapeDtypeStruct((width, tokens), own.dtype),
        ),
        [held],
        2 * product,
        *near,
        from_right[-1],
        last_left,
        far_fwd,
        weights[0],
        partial,
        picked,
    )
    (shares,) = kernel_call(
        late_kernel,
        (jax.ShapeDtypeStruct((2,) + share_shape, jnp.bfloat16),),
        [],
        product // 8,
        far_rev,
        total_rev,
        picked,
        shares_fwd,
    )

    ends = [[p * dp + d for p in (i, pipe - 1 - i) for d in range(dp)] for i in range(pipe // 2)]
    shares = lax.all_to_all(
        shares.reshape(2 * dp, channels // dp, width),
        ("pipe", "dp"),
        0,
        0,
        tiled=True,
        axis_index_groups=ends,
    )
    weight_grad = jnp.sum(shares.astype(jnp.float32), axis=0) * (1.0 / tokens)
    return grad.T[None, None], weight_grad.T[None]


def solution(mesh):
    in_specs = (
        P("pipe", "dp", None, None, "seq"),
        P("pipe", "dp", None, "seq", None),
        P("pipe", "seq", None),
    )
    out_specs = (P("pipe", "dp", None, "seq"), P("pipe", "seq", "dp"))
    return jax.shard_map(local, mesh=mesh, in_specs=in_specs, out_specs=out_specs, check_vma=False)
```

time: 122 us -> 98.9 us (0.81)
  blocking collectives: 16.7 us -> 52.1 us
  starting transfers between devices: 49.1 us -> 25.9 us
  waiting for transfers between devices: 32 us -> 9.09 us
  between operations: 14.3 us -> 0.77 us
  Pallas kernels: 0 us -> 7.3 us
  matrix products: 5.8 us -> 0 us
  local copies, waits for them, and re-layouts: 2.89 us -> 1.55 us
    all_to_all x0 -> x1, blocking collectives: none -> 35.6 us  [local(): lax.all_to_all(shares.reshape(2 * dp, channels // dp, width), ('pipe', 'd...]
    all_gather x1 -> x0, waiting for transfers between devices: 16.2 us -> none  [local(): lax.all_gather(both[1][:, None], 'seq', axis=1, tiled=True, axis_index_gr...]
    all_to_all x2 -> x0, starting transfers between devices: 12.1 us -> none  [dp_sum(): shares = lax.all_to_all(shares, 'dp', 0, 0, tiled=True)]
    ppermute x3 -> x2, starting transfers between devices: 16.9 us -> 6.49 us  [the longest x1 4.57 us: local(): far_rev = lax.ppermute(from_right[-1][1], 'seq', left)]
    pallas_call x0 -> x3, Pallas kernels: none -> 7.3 us  [kernel_call(): pl.pallas_call(body, out_shape=out_shape, in_specs=[smem] + [vmem] * len(...]
    ppermute x3 -> x2, waiting for transfers between devices: 7.36 us -> 1.08 us  [the longest x1 1.08 us: local(): far_fwd = lax.ppermute(last_left[0], 'seq', right)]
    dot_general x3 -> x0, matrix products: 5.8 us -> none  [the longest x2 4.15 us: dp_sum(): lax.dot_general(latent, saved, over_tokens, preferred_element_type=jnp.fl...]
    ppermute x3, waiting for transfers between devices: 5.68 us -> 8 us  [local(): from_left.append(lax.ppermute(from_left[-1], 'seq', right))]
  transfers between devices with their start and end apart: 12 -> 8, of which waited for: 8 -> 3; matrix products, arithmetic and copies ran while one was open for 4% -> 0% of each run, Pallas kernels for 0% -> 6%
where the time goes in v6:
time: 98.9 us; the launch traced here: 97.6 us
  blocking collectives  52.1 us (53%)
  starting transfers between devices  25.9 us (26%)
  waiting for transfers between devices  9.09 us (9%)
  Pallas kernels  7.3 us (7%)
  local copies, waits for them, and re-layouts  1.55 us (2%)
    all_to_all x1, blocking collectives, local(): lax.all_to_all(shares.reshape(2 * dp, channels // dp, width), ('pipe', 'd...  35.6 us
    all_gather x1, blocking collectives, local(): lax.all_gather(grad_latent[0, 0][:, None], 'seq', axis=1, tiled=True, axi...  16.6 us
    ppermute x3, starting transfers between devices, local(): from_right.append(lax.ppermute(from_right[-1], 'seq', left))  12.9 us
    ppermute x3, waiting for transfers between devices, local(): from_left.append(lax.ppermute(from_left[-1], 'seq', right))  8 us
    pallas_call x3, Pallas kernels, kernel_call(): pl.pallas_call(body, out_shape=out_shape, in_specs=[smem] + [vmem] * len(...  7.3 us
    ppermute x3, starting transfers between devices, local(): from_left.append(lax.ppermute(from_left[-1], 'seq', right))  6.56 us
    ppermute x1, starting transfers between devices, local(): far_rev = lax.ppermute(from_right[-1][1], 'seq', left)  4.57 us
  transfers between devices with their start and end apart: 8, of which 3 were waited for; matrix products, arithmetic and copies ran while one was open for 0% of the time, Pallas kernels for 6%

profile of v6, /device:TPU:1, one launch (start us, length us, event | category | flops | bytes accessed | tf_op | source)
XLA Modules:
  0.0 97.6 jit_solution(13706633987159823481)
XLA Ops:
  0.6 16.6 %all-gather = bf16[1,1,2,256,384]{4,3,2,1,0:T(8,128)(2,1)S(1)} all-gather(bf16[1,1,2,64,384]{4,3,2,1,0:T(8,128)(2,1)} %param.4), channel_id=2, replica_groups={{0,32,64,96},{4,36,68,100},{8,40,72,104},{12,44,76,108},{16,48,80,112},..., dimensions={3}, use_global_device_ids=true | all-gather | bytes 491520 | tf_op jit(solution)/shard_map/all_gather | solution.py:118
  17.2 2.7 %collective-permute-start.2 = (bf16[2,4,64,384]{3,2,1,0:T(8,128)(2,1)S(1)}, bf16[2,4,64,384]{3,2,1,0:T(8,128)(2,1)S(1)}, u32[]{:S(2)}, u32[]{:S(2)}) collective-permute-start(bf16[2,4,64,384]{3,2,1,0:T(8,128)(2,1)S(1)} %bitcast.19), channel_id=1, source_target_pairs={{0,4},{4,8},{8,12},{12,16},{16,20},{20,24},{24,28},{28,0},{32,36},... | collective-permute-start | bytes 1179656 | tf_op jit(solution)/shard_map/ppermute | solution.py:122
  19.9 3.7 %collective-permute-start = (bf16[2,4,64,384]{3,2,1,0:T(8,128)(2,1)S(1)}, bf16[2,4,64,384]{3,2,1,0:T(8,128)(2,1)S(1)}, u32[]{:S(2)}, u32[]{:S(2)}) collective-permute-start(bf16[2,4,64,384]{3,2,1,0:T(8,128)(2,1)S(1)} %bitcast.20), channel_id=1, source_target_pairs={{0,28},{4,0},{8,4},{12,8},{16,12},{20,16},{24,20},{28,24},{32,60},... | collective-permute-start | bytes 1179656 | tf_op jit(solution)/shard_map/ppermute | solution.py:123
  23.7 3.2 %collective-permute-done.2.refs_3_ = bf16[2,4,64,384]{3,2,1,0:T(8,128)(2,1)S(1)} collective-permute-done((bf16[2,4,64,384]{3,2,1,0:T(8,128)(2,1)S(1)}, bf16[2,4,64,384]{3,2,1,0:T(8,128)(2,1)S(1)}, u32[]{:S(2)}, u32[]{:S(2)}) %collective-permute-start.2) | collective-permute-done | bytes 393248 | tf_op jit(solution)/shard_map/ppermute | solution.py:122
  26.9 1.9 %collective-permute-start.3 = (bf16[2,4,64,384]{3,2,1,0:T(8,128)(2,1)S(1)}, bf16[2,4,64,384]{3,2,1,0:T(8,128)(2,1)S(1)}, u32[]{:S(2)}, u32[]{:S(2)}) collective-permute-start(bf16[2,4,64,384]{3,2,1,0:T(8,128)(2,1)S(1)} %collective-permute-done.2.refs_3_), channel_id=1, source_target_pairs={{0,4},{4,8},{8,12},{12,16},{16,20},{20,24},{24,28},{28,0},{32,36},... | collective-permute-start | bytes 1179656 | tf_op jit(solution)/shard_map/ppermute | solution.py:122
  28.8 0.0 collective-permute-done.refs_1_
  28.8 4.6 %collective-permute-start.1 = (bf16[2,4,64,384]{3,2,1,0:T(8,128)(2,1)S(1)}, bf16[2,4,64,384]{3,2,1,0:T(8,128)(2,1)S(1)}, u32[]{:S(2)}, u32[]{:S(2)}) collective-permute-start(bf16[2,4,64,384]{3,2,1,0:T(8,128)(2,1)S(1)} %collective-permute-done.refs_1_), channel_id=1, source_target_pairs={{0,28},{4,0},{8,4},{12,8},{16,12},{20,16},{24,20},{28,24},{32,60},... | collective-permute-start | bytes 1179656 | tf_op jit(solution)/shard_map/ppermute | solution.py:123
  33.4 4.8 %collective-permute-done.3.refs_4_ = bf16[2,4,64,384]{3,2,1,0:T(8,128)(2,1)S(1)} collective-permute-done((bf16[2,4,64,384]{3,2,1,0:T(8,128)(2,1)S(1)}, bf16[2,4,64,384]{3,2,1,0:T(8,128)(2,1)S(1)}, u32[]{:S(2)}, u32[]{:S(2)}) %collective-permute-start.3) | collective-permute-done | bytes 393248 | tf_op jit(solution)/shard_map/ppermute | solution.py:122
  38.2 1.9 %collective-permute-start.5 = (bf16[2,4,64,384]{3,2,1,0:T(8,128)(2,1)S(1)}, bf16[2,4,64,384]{3,2,1,0:T(8,128)(2,1)S(1)}, u32[]{:S(2)}, u32[]{:S(2)}) collective-permute-start(bf16[2,4,64,384]{3,2,1,0:T(8,128)(2,1)S(1)} %collective-permute-done.3.refs_4_), channel_id=1, source_target_pairs={{0,4},{4,8},{8,12},{12,16},{16,20},{20,24},{24,28},{28,0},{32,36},... | collective-permute-start | bytes 1179656 | tf_op jit(solution)/shard_map/ppermute | solution.py:122
  40.1 0.0 collective-permute-done.1.refs_2_
  40.1 4.6 %collective-permute-start.4 = (bf16[2,4,64,384]{3,2,1,0:T(8,128)(2,1)S(1)}, bf16[2,4,64,384]{3,2,1,0:T(8,128)(2,1)S(1)}, u32[]{:S(2)}, u32[]{:S(2)}) collective-permute-start(bf16[2,4,64,384]{3,2,1,0:T(8,128)(2,1)S(1)} %collective-permute-done.1.refs_2_), channel_id=1, source_target_pairs={{0,28},{4,0},{8,4},{12,8},{16,12},{20,16},{24,20},{28,24},{32,60},... | collective-permute-start | bytes 1179656 | tf_op jit(solution)/shard_map/ppermute | solution.py:123
  44.7 0.1 pad_add_fusion.here_ref
  44.8 0.0 copy-start
  44.8 1.5 %copy-done = bf16[1,1,2,2048,224]{3,4,2,1,0:T(8,128)(2,1)S(1)} copy-done((bf16[1,1,2,2048,224]{3,4,2,1,0:T(8,128)(2,1)S(1)}, bf16[1,1,2,2048,224]{3,4,2,1,0:T(8,128)(2,1)}, u32[]{:S(2)}) %copy-start) | copy-done | bytes 1835032
  46.3 0.0 copy-start.1
  46.3 3.4 %shard_map.50 = (f32[2,224,384]{2,1,0:T(8,128)S(1)}, bf16[2,3,4,224,64]{4,3,2,1,0:T(8,128)(2,1)S(1)}) custom-call(s32[2]{0:T(128)S(1)} %pad_add_fusion.here_ref, bf16[2,4,64,384]{3,2,1,0:T(8,128)(2,1)S(1)} %bitcast.21, bf16[2,4,64,384]{3,2,1,0:T(8,128)(2,1)S(1)} %collective-permute-done.refs_1_, bf16[2,4,64,384]{3,2,1,0:T(8,128)(2,1)S(1)} %collective-permute-done.1.refs_2_, ...), custom_call_target="tpu_custom_call" | custom-call | flops 704643072 | bytes 3145728 | tf_op jit(solution)/shard_map/pallas_call | solution.py:136
  49.6 0.0 collective-permute-done.5.refs_6_
  49.7 1.9 %collective-permute-start.6 = (bf16[4,64,384]{2,1,0:T(8,128)(2,1)S(1)}, bf16[4,64,384]{2,1,0:T(8,128)(2,1)S(1)}, u32[]{:S(2)}, u32[]{:S(2)}) collective-permute-start(bf16[4,64,384]{2,1,0:T(8,128)(2,1)S(1)} %slice_bitcast_fusion.1), channel_id=1, source_target_pairs={{0,4},{4,8},{8,12},{12,16},{16,20},{20,24},{24,28},{28,0},{32,36},... | collective-permute-start | bytes 589832 | tf_op jit(solution)/shard_map/ppermute | solution.py:161
  51.6 0.0 collective-permute-done.4.refs_5_
  51.7 4.6 %collective-permute-start.7 = (bf16[4,64,384]{2,1,0:T(8,128)(2,1)S(1)}, bf16[4,64,384]{2,1,0:T(8,128)(2,1)S(1)}, u32[]{:S(2)}, u32[]{:S(2)}) collective-permute-start(bf16[4,64,384]{2,1,0:T(8,128)(2,1)S(1)} %slice_bitcast_fusion), channel_id=1, source_target_pairs={{0,28},{4,0},{8,4},{12,8},{16,12},{20,16},{24,20},{28,24},{32,60},... | collective-permute-start | bytes 589832 | tf_op jit(solution)/shard_map/ppermute | solution.py:162
  56.2 1.1 %collective-permute-done.6.refs_7_ = bf16[4,64,384]{2,1,0:T(8,128)(2,1)S(1)} collective-permute-done((bf16[4,64,384]{2,1,0:T(8,128)(2,1)S(1)}, bf16[4,64,384]{2,1,0:T(8,128)(2,1)S(1)}, u32[]{:S(2)}, u32[]{:S(2)}) %collective-permute-start.6) | collective-permute-done | bytes 196640 | tf_op jit(solution)/shard_map/ppermute | solution.py:161
  57.3 0.0 copy-done.1
  57.3 3.0 %shard_map.51 = (bf16[1,4,96,224]{3,2,1,0:T(8,128)(2,1)S(1)}, f32[224,384]{1,0:T(8,128)S(1)}, bf16[224,2048]{1,0:T(8,128)(2,1)}) custom-call(s32[2]{0:T(128)S(1)} %pad_add_fusion.here_ref, bf16[2,4,64,384]{3,2,1,0:T(8,128)(2,1)S(1)} %bitcast.22, bf16[2,4,64,384]{3,2,1,0:T(8,128)(2,1)S(1)} %collective-permute-done.refs_1_, ...), custom_call_target="tpu_custom_call" | custom-call | flops 704643072 | bytes 3145728 | tf_op jit(solution)/shard_map/pallas_call | solution.py:136
  60.3 0.0 collective-permute-done.7.far_ref
  60.3 1.0 shard_map.52
  61.3 35.6 %all_to_all.5 = bf16[8,96,224]{2,1,0:T(8,128)(2,1)S(1)} all-to-all(bf16[8,96,224]{2,1,0:T(8,128)(2,1)S(1)} %bitcast.24), channel_id=1, replica_groups={{0,1,2,3,896,897,898,899},{128,129,130,131,768,769,770,771},{256,257,25..., dimensions={0} | all-to-all | bytes 688128 | tf_op jit(solution)/shard_map/all_to_all | solution.py:193
  96.9 0.1 convert_reduce_fusion
  96.9 0.6 multiply_bitcast_fusion
  (2 shorter events, 0.0 us)
Async XLA Ops:
  17.2 9.7 %collective-permute-start.2 = (bf16[2,4,64,384]{3,2,1,0:T(8,128)(2,1)S(1)}, bf16[2,4,64,384]{3,2,1,0:T(8,128)(2,1)S(1)}, u32[]{:S(2)}, u32[]{:S(2)}) collective-permute-start(bf16[2,4,64,384]{3,2,1,0:T(8,128)(2,1)S(1)} %bitcast.19), channel_id=1, source_target_pairs={{0,4},{4,8},{8,12},{12,16},{16,20},{20,24},{24,28},{28,0},{32,36},... | collective-permute-start | bytes 1179656 | tf_op jit(solution)/shard_map/ppermute | solution.py:122
  19.9 8.9 %collective-permute-start = (bf16[2,4,64,384]{3,2,1,0:T(8,128)(2,1)S(1)}, bf16[2,4,64,384]{3,2,1,0:T(8,128)(2,1)S(1)}, u32[]{:S(2)}, u32[]{:S(2)}) collective-permute-start(bf16[2,4,64,384]{3,2,1,0:T(8,128)(2,1)S(1)} %bitcast.20), channel_id=1, source_target_pairs={{0,28},{4,0},{8,4},{12,8},{16,12},{20,16},{24,20},{28,24},{32,60},... | collective-permute-start | bytes 1179656 | tf_op jit(solution)/shard_map/ppermute | solution.py:123
  26.9 11.3 %collective-permute-start.3 = (bf16[2,4,64,384]{3,2,1,0:T(8,128)(2,1)S(1)}, bf16[2,4,64,384]{3,2,1,0:T(8,128)(2,1)S(1)}, u32[]{:S(2)}, u32[]{:S(2)}) collective-permute-start(bf16[2,4,64,384]{3,2,1,0:T(8,128)(2,1)S(1)} %collective-permute-done.2.refs_3_), channel_id=1, source_target_pairs={{0,4},{4,8},{8,12},{12,16},{16,20},{20,24},{24,28},{28,0},{32,36},... | collective-permute-start | bytes 1179656 | tf_op jit(solution)/shard_map/ppermute | solution.py:122
  28.8 11.3 %collective-permute-start.1 = (bf16[2,4,64,384]{3,2,1,0:T(8,128)(2,1)S(1)}, bf16[2,4,64,384]{3,2,1,0:T(8,128)(2,1)S(1)}, u32[]{:S(2)}, u32[]{:S(2)}) collective-permute-start(bf16[2,4,64,384]{3,2,1,0:T(8,128)(2,1)S(1)} %collective-permute-done.refs_1_), channel_id=1, source_target_pairs={{0,28},{4,0},{8,4},{12,8},{16,12},{20,16},{24,20},{28,24},{32,60},... | collective-permute-start | bytes 1179656 | tf_op jit(solution)/shard_map/ppermute | solution.py:123
  38.2 11.5 %collective-permute-start.5 = (bf16[2,4,64,384]{3,2,1,0:T(8,128)(2,1)S(1)}, bf16[2,4,64,384]{3,2,1,0:T(8,128)(2,1)S(1)}, u32[]{:S(2)}, u32[]{:S(2)}) collective-permute-start(bf16[2,4,64,384]{3,2,1,0:T(8,128)(2,1)S(1)} %collective-permute-done.3.refs_4_), channel_id=1, source_target_pairs={{0,4},{4,8},{8,12},{12,16},{16,20},{20,24},{24,28},{28,0},{32,36},... | collective-permute-start | bytes 1179656 | tf_op jit(solution)/shard_map/ppermute | solution.py:122
  40.1 11.5 %collective-permute-start.4 = (bf16[2,4,64,384]{3,2,1,0:T(8,128)(2,1)S(1)}, bf16[2,4,64,384]{3,2,1,0:T(8,128)(2,1)S(1)}, u32[]{:S(2)}, u32[]{:S(2)}) collective-permute-start(bf16[2,4,64,384]{3,2,1,0:T(8,128)(2,1)S(1)} %collective-permute-done.1.refs_2_), channel_id=1, source_target_pairs={{0,28},{4,0},{8,4},{12,8},{16,12},{20,16},{24,20},{28,24},{32,60},... | collective-permute-start | bytes 1179656 | tf_op jit(solution)/shard_map/ppermute | solution.py:123
  44.8 1.5 %copy-start = (bf16[1,1,2,2048,224]{3,4,2,1,0:T(8,128)(2,1)S(1)}, bf16[1,1,2,2048,224]{3,4,2,1,0:T(8,128)(2,1)}, u32[]{:S(2)}) copy-start(bf16[1,1,2,2048,224]{3,4,2,1,0:T(8,128)(2,1)} %param.3) | copy-start | bytes 5505028
  46.3 11.0 %copy-start.1 = (bf16[1,224,384]{2,1,0:T(8,128)(2,1)S(1)}, bf16[1,224,384]{2,1,0:T(8,128)(2,1)}, u32[]{:S(2)}) copy-start(bf16[1,224,384]{2,1,0:T(8,128)(2,1)} %param.5) | copy-start | bytes 516100
  49.7 7.6 %collective-permute-start.6 = (bf16[4,64,384]{2,1,0:T(8,128)(2,1)S(1)}, bf16[4,64,384]{2,1,0:T(8,128)(2,1)S(1)}, u32[]{:S(2)}, u32[]{:S(2)}) collective-permute-start(bf16[4,64,384]{2,1,0:T(8,128)(2,1)S(1)} %slice_bitcast_fusion.1), channel_id=1, source_target_pairs={{0,4},{4,8},{8,12},{12,16},{16,20},{20,24},{24,28},{28,0},{32,36},... | collective-permute-start | bytes 589832 | tf_op jit(solution)/shard_map/ppermute | solution.py:161
  51.7 8.6 %collective-permute-start.7 = (bf16[4,64,384]{2,1,0:T(8,128)(2,1)S(1)}, bf16[4,64,384]{2,1,0:T(8,128)(2,1)S(1)}, u32[]{:S(2)}, u32[]{:S(2)}) collective-permute-start(bf16[4,64,384]{2,1,0:T(8,128)(2,1)S(1)} %slice_bitcast_fusion), channel_id=1, source_target_pairs={{0,28},{4,0},{8,4},{12,8},{16,12},{20,16},{24,20},{28,24},{32,60},... | collective-permute-start | bytes 589832 | tf_op jit(solution)/shard_map/ppermute | solution.py:162

commit v7 on v6

--- a/solution.py
+++ b/solution.py
@@ -45,6 +45,19 @@
         )
 
 
+def third_kernel(here_ref, low_ref, high_ref, partial_ref, picked_ref, total_ref):
+    for direction in range(2):
+        total = partial_ref[direction]
+        for j, block in enumerate((low_ref, high_ref)):
+            for y in range(block.shape[1]):
+                total += jnp.dot(
+                    picked_ref[direction, j, y],
+                    block[direction, y],
+                    preferred_element_type=jnp.float32,
+                )
+        total_ref[direction] = total
+
+
 def put_shares(total, shares, slot):
     dp, share, _ = shares.shape[1:]
     turned = total.T.astype(shares.dtype)
@@ -53,17 +66,19 @@
 
 
 def middle_kernel(here_ref, *refs):
-    blocks, refs = refs[:-8], refs[-8:]
-    far_ref, weight_ref, partial_ref, picked_ref, fwd_ref, rev_ref, grad_ref, latent_ref = refs
+    blocks, refs = refs[:-7], refs[-7:]
+    far_ref, weight_ref, partial_ref, picked_ref, fwd_ref, grad_ref, latent_ref = refs
     ny, nx, _, channels = latent_ref.shape
-    late = blocks[-2:]
     for step, block in zip(near_steps(nx) + list(late_steps(nx)[:2]), blocks):
         place = lax.rem(here_ref[0] + step, nx)
         for y in range(ny):
             latent_ref[y, place] = block[0, y]
     place = lax.rem(here_ref[0] + late_steps(nx)[2], nx)
+    total = partial_ref[0]
     for y in range(ny):
         latent_ref[y, place] = far_ref[y]
+        total += jnp.dot(picked_ref[0, 2, y], far_ref[y], preferred_element_type=jnp.float32)
+    put_shares(total, fwd_ref, 0)
     grad = lax.dot_general(
         weight_ref[...],
         latent_ref[...].reshape(-1, channels),
@@ -71,27 +86,10 @@
         preferred_element_type=jnp.float32,
     )
     grad_ref[...] = grad.astype(grad_ref.dtype)
-    for direction in range(2):
-        total = partial_ref[direction]
-        for y in range(ny):
-            for j, block in enumerate(late):
-                total += jnp.dot(
-                    picked_ref[direction, j, y],
-                    block[direction, y],
-                    preferred_element_type=jnp.float32,
-                )
-            if direction == 0:
-                total += jnp.dot(
-                    picked_ref[0, 2, y], far_ref[y], preferred_element_type=jnp.float32
-                )
-        if direction == 0:
-            put_shares(total, fwd_ref, 0)
-        else:
-            rev_ref[...] = total
-
-
-def late_kernel(here_ref, far_ref, rev_ref, picked_ref, fwd_ref, shares_ref):
-    total = rev_ref[...]
+
+
+def late_kernel(here_ref, far_ref, partial_ref, picked_ref, fwd_ref, shares_ref):
+    total = partial_ref[1]
     for y in range(far_ref.shape[0]):
         total += jnp.dot(picked_ref[1, 2, y], far_ref[y], preferred_element_type=jnp.float32)
     put_shares(total, shares_ref, 1 - here_ref[1])
@@ -117,12 +115,7 @@
 
     both = lax.all_gather(grad_latent[0, 0][:, None], "seq", axis=1, tiled=True, axis_index_groups=columns)
     own = both
-    from_left, from_right = [own], [own]
-    for _ in range(nx // 2 - 1):
-        from_left.append(lax.ppermute(from_left[-1], "seq", right))
-        from_right.append(lax.ppermute(from_right[-1], "seq", left))
     far = nx // 2
-    near = from_right[: far - 1] + from_left[1 : far - 1]
     here = jnp.stack(
         [lax.rem(lax.axis_index("seq"), nx), lax.div(lax.axis_index("pipe"), pipe // 2)]
     )
@@ -132,7 +125,7 @@
     held = pltpu.VMEM((ny, nx, piece, channels), own.dtype)
     settings = pltpu.CompilerParams(vmem_limit_bytes=VMEM_BYTES)
 
-    def kernel_call(body, out_shape, scratch, flops, *operands):
+    def kernel_call(body, out_shape, scratch, flops, here, *operands):
         return pl.pallas_call(
             body,
             out_shape=out_shape,
@@ -146,36 +139,38 @@
         )(here, *operands)
 
     product = 2 * tokens * channels * width
+    sums_shape = (jax.ShapeDtypeStruct((2, width, channels), jnp.float32),)
+    from_left, from_right = [own], [own]
+    for step in range(1, far):
+        from_left.append(lax.ppermute(from_left[-1], "seq", right))
+        from_right.append(lax.ppermute(from_right[-1], "seq", left))
+    near = from_right[: far - 1] + from_left[1 : far - 1]
+    picked_shape = jax.ShapeDtypeStruct((2, 3, ny, width, piece), saved.dtype)
     partial, picked = kernel_call(
-        early_kernel,
-        (
-            jax.ShapeDtypeStruct((2, width, channels), jnp.float32),
-            jax.ShapeDtypeStruct((2, 3, ny, width, piece), saved.dtype),
-        ),
-        [held],
-        2 * product,
-        *near,
-        saved,
-    )
-    last_left, partial = lax.optimization_barrier((from_left[-1], partial))
-    far_fwd = lax.ppermute(last_left[0], "seq", right)
+        early_kernel, sums_shape + (picked_shape,), [held], 2 * product, here, *near, saved
+    )
+    from_left[-1], partial = lax.optimization_barrier((from_left[-1], partial))
+    far_fwd = lax.ppermute(from_left[-1][0], "seq", right)
     far_rev = lax.ppermute(from_right[-1][1], "seq", left)
+    third = (from_right[-1], from_left[-1])
+    (total,) = kernel_call(
+        third_kernel, sums_shape, [], product // 2, here, *third, partial, picked
+    )
     share_shape = (dp, channels // dp, width)
-    shares_fwd, total_rev, grad = kernel_call(
+    shares_fwd, grad = kernel_call(
         middle_kernel,
         (
             jax.ShapeDtypeStruct((1,) + share_shape, jnp.bfloat16),
-            jax.ShapeDtypeStruct((width, channels), jnp.float32),
             jax.ShapeDtypeStruct((width, tokens), own.dtype),
         ),
         [held],
-        2 * product,
+        product,
+        here,
         *near,
-        from_right[-1],
-        last_left,
+        *third,
         far_fwd,
         weights[0],
-        partial,
+        total,
         picked,
     )
     (shares,) = kernel_call(
@@ -183,8 +178,9 @@
         (jax.ShapeDtypeStruct((2,) + share_shape, jnp.bfloat16),),
         [],
         product // 8,
+        here,
         far_rev,
-        total_rev,
+        total,
         picked,
         shares_fwd,
     )

time: 98.9 us -> 99 us (level)
  waiting for transfers between devices: 9.09 us -> 8.02 us
    ppermute x1, waiting for transfers between devices: 1.08 us -> 0.01 us  [local(): far_fwd = lax.ppermute(from_left[-1][0], 'seq', right)]
    pallas_call x3 -> x4, Pallas kernels: 7.3 us -> 8.17 us  [kernel_call(): pl.pallas_call(body, out_shape=out_shape, in_specs=[smem] + [vmem] * len(...]
  transfers between devices with their start and end apart: 8 -> 8, of which waited for: 3 -> 2; matrix products, arithmetic and copies ran while one was open for 0% -> 0% of each run, Pallas kernels for 6% -> 7%
where the time goes in v7:
time: 99 us; the launch traced here: 97 us
  blocking collectives  51.6 us (52%)
  starting transfers between devices  26.1 us (26%)
  Pallas kernels  8.17 us (8%)
  waiting for transfers between devices  8.02 us (8%)
  local copies, waits for them, and re-layouts  1.55 us (2%)
    all_to_all x1, blocking collectives, local(): lax.all_to_all(shares.reshape(2 * dp, channels // dp, width), ('pipe', 'd...  35.1 us
    all_gather x1, blocking collectives, local(): lax.all_gather(grad_latent[0, 0][:, None], 'seq', axis=1, tiled=True, axi...  16.6 us
    ppermute x3, starting transfers between devices, local(): from_right.append(lax.ppermute(from_right[-1], 'seq', left))  12.9 us
    pallas_call x4, Pallas kernels, kernel_call(): pl.pallas_call(body, out_shape=out_shape, in_specs=[smem] + [vmem] * len(...  8.17 us
    ppermute x3, waiting for transfers between devices, local(): from_left.append(lax.ppermute(from_left[-1], 'seq', right))  8 us
    ppermute x3, starting transfers between devices, local(): from_left.append(lax.ppermute(from_left[-1], 'seq', right))  6.56 us
    ppermute x1, starting transfers between devices, local(): far_rev = lax.ppermute(from_right[-1][1], 'seq', left)  4.7 us
  transfers between devices with their start and end apart: 8, of which 2 were waited for; matrix products, arithmetic and copies ran while one was open for 0% of the time, Pallas kernels for 7%

profile of v7, /device:TPU:1, one launch (start us, length us, event | category | flops | bytes accessed | tf_op | source)
XLA Modules:
  0.0 97.0 jit_solution(12673594752492311182)
XLA Ops:
  0.6 16.6 %all-gather = bf16[1,1,2,256,384]{4,3,2,1,0:T(8,128)(2,1)S(1)} all-gather(bf16[1,1,2,64,384]{4,3,2,1,0:T(8,128)(2,1)} %param.4), channel_id=2, replica_groups={{0,32,64,96},{4,36,68,100},{8,40,72,104},{12,44,76,108},{16,48,80,112},..., dimensions={3}, use_global_device_ids=true | all-gather | bytes 491520 | tf_op jit(solution)/shard_map/all_gather | solution.py:116
  17.2 2.7 %collective-permute-start.2 = (bf16[2,4,64,384]{3,2,1,0:T(8,128)(2,1)S(1)}, bf16[2,4,64,384]{3,2,1,0:T(8,128)(2,1)S(1)}, u32[]{:S(2)}, u32[]{:S(2)}) collective-permute-start(bf16[2,4,64,384]{3,2,1,0:T(8,128)(2,1)S(1)} %bitcast.19), channel_id=1, source_target_pairs={{0,4},{4,8},{8,12},{12,16},{16,20},{20,24},{24,28},{28,0},{32,36},... | collective-permute-start | bytes 1179656 | tf_op jit(solution)/shard_map/ppermute | solution.py:145
  19.9 3.7 %collective-permute-start = (bf16[2,4,64,384]{3,2,1,0:T(8,128)(2,1)S(1)}, bf16[2,4,64,384]{3,2,1,0:T(8,128)(2,1)S(1)}, u32[]{:S(2)}, u32[]{:S(2)}) collective-permute-start(bf16[2,4,64,384]{3,2,1,0:T(8,128)(2,1)S(1)} %bitcast.20), channel_id=1, source_target_pairs={{0,28},{4,0},{8,4},{12,8},{16,12},{20,16},{24,20},{28,24},{32,60},... | collective-permute-start | bytes 1179656 | tf_op jit(solution)/shard_map/ppermute | solution.py:146
  23.7 3.2 %collective-permute-done.2.refs_3_ = bf16[2,4,64,384]{3,2,1,0:T(8,128)(2,1)S(1)} collective-permute-done((bf16[2,4,64,384]{3,2,1,0:T(8,128)(2,1)S(1)}, bf16[2,4,64,384]{3,2,1,0:T(8,128)(2,1)S(1)}, u32[]{:S(2)}, u32[]{:S(2)}) %collective-permute-start.2) | collective-permute-done | bytes 393248 | tf_op jit(solution)/shard_map/ppermute | solution.py:145
  26.9 1.9 %collective-permute-start.3 = (bf16[2,4,64,384]{3,2,1,0:T(8,128)(2,1)S(1)}, bf16[2,4,64,384]{3,2,1,0:T(8,128)(2,1)S(1)}, u32[]{:S(2)}, u32[]{:S(2)}) collective-permute-start(bf16[2,4,64,384]{3,2,1,0:T(8,128)(2,1)S(1)} %collective-permute-done.2.refs_3_), channel_id=1, source_target_pairs={{0,4},{4,8},{8,12},{12,16},{16,20},{20,24},{24,28},{28,0},{32,36},... | collective-permute-start | bytes 1179656 | tf_op jit(solution)/shard_map/ppermute | solution.py:145
  28.8 0.0 collective-permute-done.refs_1_
  28.8 4.6 %collective-permute-start.1 = (bf16[2,4,64,384]{3,2,1,0:T(8,128)(2,1)S(1)}, bf16[2,4,64,384]{3,2,1,0:T(8,128)(2,1)S(1)}, u32[]{:S(2)}, u32[]{:S(2)}) collective-permute-start(bf16[2,4,64,384]{3,2,1,0:T(8,128)(2,1)S(1)} %collective-permute-done.refs_1_), channel_id=1, source_target_pairs={{0,28},{4,0},{8,4},{12,8},{16,12},{20,16},{24,20},{28,24},{32,60},... | collective-permute-start | bytes 1179656 | tf_op jit(solution)/shard_map/ppermute | solution.py:146
  33.4 4.8 %collective-permute-done.3.refs_4_ = bf16[2,4,64,384]{3,2,1,0:T(8,128)(2,1)S(1)} collective-permute-done((bf16[2,4,64,384]{3,2,1,0:T(8,128)(2,1)S(1)}, bf16[2,4,64,384]{3,2,1,0:T(8,128)(2,1)S(1)}, u32[]{:S(2)}, u32[]{:S(2)}) %collective-permute-start.3) | collective-permute-done | bytes 393248 | tf_op jit(solution)/shard_map/ppermute | solution.py:145
  38.2 1.9 %collective-permute-start.5 = (bf16[2,4,64,384]{3,2,1,0:T(8,128)(2,1)S(1)}, bf16[2,4,64,384]{3,2,1,0:T(8,128)(2,1)S(1)}, u32[]{:S(2)}, u32[]{:S(2)}) collective-permute-start(bf16[2,4,64,384]{3,2,1,0:T(8,128)(2,1)S(1)} %collective-permute-done.3.refs_4_), channel_id=1, source_target_pairs={{0,4},{4,8},{8,12},{12,16},{16,20},{20,24},{24,28},{28,0},{32,36},... | collective-permute-start | bytes 1179656 | tf_op jit(solution)/shard_map/ppermute | solution.py:145
  40.1 0.0 collective-permute-done.1.refs_2_
  40.1 4.6 %collective-permute-start.4 = (bf16[2,4,64,384]{3,2,1,0:T(8,128)(2,1)S(1)}, bf16[2,4,64,384]{3,2,1,0:T(8,128)(2,1)S(1)}, u32[]{:S(2)}, u32[]{:S(2)}) collective-permute-start(bf16[2,4,64,384]{3,2,1,0:T(8,128)(2,1)S(1)} %collective-permute-done.1.refs_2_), channel_id=1, source_target_pairs={{0,28},{4,0},{8,4},{12,8},{16,12},{20,16},{24,20},{28,24},{32,60},... | collective-permute-start | bytes 1179656 | tf_op jit(solution)/shard_map/ppermute | solution.py:146
  44.7 0.1 pad_add_fusion.here_ref
  44.8 0.0 copy-start
  44.8 1.5 %copy-done = bf16[1,1,2,2048,224]{3,4,2,1,0:T(8,128)(2,1)S(1)} copy-done((bf16[1,1,2,2048,224]{3,4,2,1,0:T(8,128)(2,1)S(1)}, bf16[1,1,2,2048,224]{3,4,2,1,0:T(8,128)(2,1)}, u32[]{:S(2)}) %copy-start) | copy-done | bytes 1835032
  46.3 3.4 %shard_map.50 = (f32[2,224,384]{2,1,0:T(8,128)S(1)}, bf16[2,3,4,224,64]{4,3,2,1,0:T(8,128)(2,1)S(1)}) custom-call(s32[2]{0:T(128)S(1)} %pad_add_fusion.here_ref, bf16[2,4,64,384]{3,2,1,0:T(8,128)(2,1)S(1)} %bitcast.21, bf16[2,4,64,384]{3,2,1,0:T(8,128)(2,1)S(1)} %collective-permute-done.refs_1_, bf16[2,4,64,384]{3,2,1,0:T(8,128)(2,1)S(1)} %collective-permute-done.1.refs_2_, ...), custom_call_target="tpu_custom_call" | custom-call | flops 704643072 | bytes 3145728 | tf_op jit(solution)/shard_map/pallas_call | solution.py:129
  49.6 0.0 collective-permute-done.5.high_ref.refs_6_
  49.7 1.9 %collective-permute-start.6 = (bf16[4,64,384]{2,1,0:T(8,128)(2,1)S(1)}, bf16[4,64,384]{2,1,0:T(8,128)(2,1)S(1)}, u32[]{:S(2)}, u32[]{:S(2)}) collective-permute-start(bf16[4,64,384]{2,1,0:T(8,128)(2,1)S(1)} %slice_bitcast_fusion.1), channel_id=1, source_target_pairs={{0,4},{4,8},{8,12},{12,16},{16,20},{20,24},{24,28},{28,0},{32,36},... | collective-permute-start | bytes 589832 | tf_op jit(solution)/shard_map/ppermute | solution.py:153
  51.6 0.0 collective-permute-done.4.low_ref.refs_5_
  51.7 0.0 copy-start.1
  51.7 4.7 %collective-permute-start.7 = (bf16[4,64,384]{2,1,0:T(8,128)(2,1)S(1)}, bf16[4,64,384]{2,1,0:T(8,128)(2,1)S(1)}, u32[]{:S(2)}, u32[]{:S(2)}) collective-permute-start(bf16[4,64,384]{2,1,0:T(8,128)(2,1)S(1)} %slice_bitcast_fusion), channel_id=1, source_target_pairs={{0,28},{4,0},{8,4},{12,8},{16,12},{20,16},{24,20},{28,24},{32,60},... | collective-permute-start | bytes 589832 | tf_op jit(solution)/shard_map/ppermute | solution.py:154
  56.4 1.4 %shard_map.51.refs_9_.partial_ref = f32[2,224,384]{2,1,0:T(8,128)S(1)} custom-call(s32[2]{0:T(128)S(1)} %pad_add_fusion.here_ref, bf16[2,4,64,384]{3,2,1,0:T(8,128)(2,1)S(1)} %collective-permute-done.4.low_ref.refs_5_, bf16[2,4,64,384]{3,2,1,0:T(8,128)(2,1)S(1)} %collective-permute-done.5.high_ref.refs_6_, f32[2,224,384]{2,1,0:T(8,128)S(1)} %get-tuple-element.10.partial_ref, ...), custom_call_target="tpu_custom_call" | custom-call | flops 176160768 | bytes 3145728 | tf_op jit(solution)/shard_map/pallas_call | solution.py:129
  57.8 0.0 collective-permute-done.6.refs_7_
  57.8 0.0 copy-done.1
  57.8 2.5 %shard_map.52 = (bf16[1,4,96,224]{3,2,1,0:T(8,128)(2,1)S(1)}, bf16[224,2048]{1,0:T(8,128)(2,1)}) custom-call(s32[2]{0:T(128)S(1)} %pad_add_fusion.here_ref, bf16[2,4,64,384]{3,2,1,0:T(8,128)(2,1)S(1)} %bitcast.22, bf16[2,4,64,384]{3,2,1,0:T(8,128)(2,1)S(1)} %collective-permute-done.refs_1_, bf16[2,4,64,384]{3,2,1,0:T(8,128)(2,1)S(1)} %collective-permute-done.1.refs_2_, ...), custom_call_target="tpu_custom_call" | custom-call | flops 352321536 | bytes 3145728 | tf_op jit(solution)/shard_map/pallas_call | solution.py:129
  60.3 0.0 collective-permute-done.7.far_ref
  60.3 1.0 %shard_map.53 = bf16[2,4,96,224]{3,2,1,0:T(8,128)(2,1)S(1)} custom-call(s32[2]{0:T(128)S(1)} %pad_add_fusion.here_ref, bf16[4,64,384]{2,1,0:T(8,128)(2,1)S(1)} %collective-permute-done.7.far_ref, f32[2,224,384]{2,1,0:T(8,128)S(1)} %shard_map.51.refs_9_.partial_ref, bf16[2,3,4,224,64]{4,3,2,1,0:T(8,128)(2,1)S(1)} %get-tuple-element.11.picked_ref.refs_10_, ...), custom_call_target="tpu_custom_call" | custom-call | flops 44040192 | bytes 3145728 | tf_op jit(solution)/shard_map/pallas_call | solution.py:129
  61.2 35.1 %all_to_all.5 = bf16[8,96,224]{2,1,0:T(8,128)(2,1)S(1)} all-to-all(bf16[8,96,224]{2,1,0:T(8,128)(2,1)S(1)} %bitcast.24), channel_id=1, replica_groups={{0,1,2,3,896,897,898,899},{128,129,130,131,768,769,770,771},{256,257,25..., dimensions={0} | all-to-all | bytes 688128 | tf_op jit(solution)/shard_map/all_to_all | solution.py:189
  96.3 0.1 convert_reduce_fusion
  96.4 0.6 multiply_bitcast_fusion
  (2 shorter events, 0.0 us)
Async XLA Ops:
  17.2 9.7 %collective-permute-start.2 = (bf16[2,4,64,384]{3,2,1,0:T(8,128)(2,1)S(1)}, bf16[2,4,64,384]{3,2,1,0:T(8,128)(2,1)S(1)}, u32[]{:S(2)}, u32[]{:S(2)}) collective-permute-start(bf16[2,4,64,384]{3,2,1,0:T(8,128)(2,1)S(1)} %bitcast.19), channel_id=1, source_target_pairs={{0,4},{4,8},{8,12},{12,16},{16,20},{20,24},{24,28},{28,0},{32,36},... | collective-permute-start | bytes 1179656 | tf_op jit(solution)/shard_map/ppermute | solution.py:145
  19.9 8.9 %collective-permute-start = (bf16[2,4,64,384]{3,2,1,0:T(8,128)(2,1)S(1)}, bf16[2,4,64,384]{3,2,1,0:T(8,128)(2,1)S(1)}, u32[]{:S(2)}, u32[]{:S(2)}) collective-permute-start(bf16[2,4,64,384]{3,2,1,0:T(8,128)(2,1)S(1)} %bitcast.20), channel_id=1, source_target_pairs={{0,28},{4,0},{8,4},{12,8},{16,12},{20,16},{24,20},{28,24},{32,60},... | collective-permute-start | bytes 1179656 | tf_op jit(solution)/shard_map/ppermute | solution.py:146
  26.9 11.3 %collective-permute-start.3 = (bf16[2,4,64,384]{3,2,1,0:T(8,128)(2,1)S(1)}, bf16[2,4,64,384]{3,2,1,0:T(8,128)(2,1)S(1)}, u32[]{:S(2)}, u32[]{:S(2)}) collective-permute-start(bf16[2,4,64,384]{3,2,1,0:T(8,128)(2,1)S(1)} %collective-permute-done.2.refs_3_), channel_id=1, source_target_pairs={{0,4},{4,8},{8,12},{12,16},{16,20},{20,24},{24,28},{28,0},{32,36},... | collective-permute-start | bytes 1179656 | tf_op jit(solution)/shard_map/ppermute | solution.py:145
  28.8 11.3 %collective-permute-start.1 = (bf16[2,4,64,384]{3,2,1,0:T(8,128)(2,1)S(1)}, bf16[2,4,64,384]{3,2,1,0:T(8,128)(2,1)S(1)}, u32[]{:S(2)}, u32[]{:S(2)}) collective-permute-start(bf16[2,4,64,384]{3,2,1,0:T(8,128)(2,1)S(1)} %collective-permute-done.refs_1_), channel_id=1, source_target_pairs={{0,28},{4,0},{8,4},{12,8},{16,12},{20,16},{24,20},{28,24},{32,60},... | collective-permute-start | bytes 1179656 | tf_op jit(solution)/shard_map/ppermute | solution.py:146
  38.2 11.5 %collective-permute-start.5 = (bf16[2,4,64,384]{3,2,1,0:T(8,128)(2,1)S(1)}, bf16[2,4,64,384]{3,2,1,0:T(8,128)(2,1)S(1)}, u32[]{:S(2)}, u32[]{:S(2)}) collective-permute-start(bf16[2,4,64,384]{3,2,1,0:T(8,128)(2,1)S(1)} %collective-permute-done.3.refs_4_), channel_id=1, source_target_pairs={{0,4},{4,8},{8,12},{12,16},{16,20},{20,24},{24,28},{28,0},{32,36},... | collective-permute-start | bytes 1179656 | tf_op jit(solution)/shard_map/ppermute | solution.py:145
  40.1 11.5 %collective-permute-start.4 = (bf16[2,4,64,384]{3,2,1,0:T(8,128)(2,1)S(1)}, bf16[2,4,64,384]{3,2,1,0:T(8,128)(2,1)S(1)}, u32[]{:S(2)}, u32[]{:S(2)}) collective-permute-start(bf16[2,4,64,384]{3,2,1,0:T(8,128)(2,1)S(1)} %collective-permute-done.1.refs_2_), channel_id=1, source_target_pairs={{0,28},{4,0},{8,4},{12,8},{16,12},{20,16},{24,20},{28,24},{32,60},... | collective-permute-start | bytes 1179656 | tf_op jit(solution)/shard_map/ppermute | solution.py:146
  44.8 1.5 %copy-start = (bf16[1,1,2,2048,224]{3,4,2,1,0:T(8,128)(2,1)S(1)}, bf16[1,1,2,2048,224]{3,4,2,1,0:T(8,128)(2,1)}, u32[]{:S(2)}) copy-start(bf16[1,1,2,2048,224]{3,4,2,1,0:T(8,128)(2,1)} %param.3) | copy-start | bytes 5505028
  49.7 8.1 %collective-permute-start.6 = (bf16[4,64,384]{2,1,0:T(8,128)(2,1)S(1)}, bf16[4,64,384]{2,1,0:T(8,128)(2,1)S(1)}, u32[]{:S(2)}, u32[]{:S(2)}) collective-permute-start(bf16[4,64,384]{2,1,0:T(8,128)(2,1)S(1)} %slice_bitcast_fusion.1), channel_id=1, source_target_pairs={{0,4},{4,8},{8,12},{12,16},{16,20},{20,24},{24,28},{28,0},{32,36},... | collective-permute-start | bytes 589832 | tf_op jit(solution)/shard_map/ppermute | solution.py:153
  51.7 6.1 %copy-start.1 = (bf16[1,224,384]{2,1,0:T(8,128)(2,1)S(1)}, bf16[1,224,384]{2,1,0:T(8,128)(2,1)}, u32[]{:S(2)}) copy-start(bf16[1,224,384]{2,1,0:T(8,128)(2,1)} %param.5) | copy-start | bytes 516100
  51.7 8.6 %collective-permute-start.7 = (bf16[4,64,384]{2,1,0:T(8,128)(2,1)S(1)}, bf16[4,64,384]{2,1,0:T(8,128)(2,1)S(1)}, u32[]{:S(2)}, u32[]{:S(2)}) collective-permute-start(bf16[4,64,384]{2,1,0:T(8,128)(2,1)S(1)} %slice_bitcast_fusion), channel_id=1, source_target_pairs={{0,28},{4,0},{8,4},{12,8},{16,12},{20,16},{24,20},{28,24},{32,60},... | collective-permute-start | bytes 589832 | tf_op jit(solution)/shard_map/ppermute | solution.py:154
